TPU v7x, 32 devices: a whole 2x2x4 slice. The times are simulated.
32 devices in a mesh: seq: 8 (over z, y), head: 4 (over x, core).
Axes of the slice: x: 2, y: 2, z: 4, core: 2. Of those that a mesh axis runs over, the one named last changes fastest.
Arguments:
- queries: bfloat16 [4096, 3584], P(('seq', 'head')), may hold values from -256 to 256
- rotated_key_rows: bfloat16 [4096, 512], P(('seq', 'head')), may hold values from -5 to 5
- value_matrix: bfloat16 [4096, 512], P(('seq', 'head')), may hold values from -6 to 6
- cotangent: bfloat16 [4096, 3584], P(('seq', 'head')), may hold values from -6 to 6
- tree_mask: int32 [32, 4], P('seq'), may hold values from 0 to 1, as said below
Outputs:
- attention: bfloat16 [4096, 3584], P(('seq', 'head'))
- query_grad: bfloat16 [4096, 3584], P(('seq', 'head'))
- key_gradient: bfloat16 [4096, 512], P(('seq', 'head'))
- value_gradient: bfloat16 [4096, 512], P(('seq', 'head'))
Inputs may be any that keep to these rules, and one draw needn't show every extreme that they name: `tree_mask`: rows of the prompt's 4 blocks are 0. All blocks of one response share one row: 1 on its first r columns and 0 after, with r from 1 to 4; the first response reads all 4 prompt blocks.
All inputs are finite; a program needn't handle non-finite values.
Results may differ from a plain program's by a relative error of at most 0.034.
Values may be sent and summed in bfloat16 or wider, within the bound.
No kernel may reach another device: no remote copies, remote signals or barrier semaphores. Data moves between devices by JAX's collectives and lax.ppermute only.
A program may use at most 128 MiB of HBM per device.

v0:
```python
import jax
import jax.numpy as jnp
from jax import lax
from jax.sharding import PartitionSpec as P

QUERY_HEADS = 28
KEY_VALUE_HEADS = 4
HEAD_SIZE = 128
MASK_BLOCK_SIZE = 128


def broadcast(value, axis, source):
    kept = jnp.where(lax.axis_index(axis) == source, value, 0).astype(value.dtype)
    return lax.psum(kept, axis)


def attend(query_head_count, block_keys, block_values, head_cotangents, allowed):
    score_scale = HEAD_SIZE ** (-0.5)
    scores = (
        jnp.einsum(
            "rjgd,njd->jgrn", query_head_count, block_keys, preferred_element_type=jnp.float32
        )
        * score_scale
    )
    scores = jnp.where(allowed, scores, jnp.float32(-1e30))
    row_max = jnp.max(scores, axis=-1, keepdims=True)
    weights = jnp.where(allowed, jnp.exp(scores - row_max), jnp.float32(0.0))
    softmax_probs = weights / jnp.sum(weights, axis=-1, keepdims=True)
    rounded_probs = softmax_probs.astype(jnp.bfloat16)
    attention = jnp.einsum(
        "jgrn,njd->rjgd", rounded_probs, block_values, preferred_element_type=jnp.float32
    ).astype(jnp.bfloat16)
    out_delta = jnp.sum(
        head_cotangents.astype(jnp.float32) * attention.astype(jnp.float32), axis=-1
    )
    out_delta = jnp.transpose(out_delta, (1, 2, 0))[..., None]
    dprob = jnp.einsum(
        "rjgd,njd->jgrn", head_cotangents, block_values, preferred_element_type=jnp.float32
    )
    dscore = (softmax_probs * (dprob - out_delta)).astype(jnp.bfloat16)
    query_grad = (
        jnp.einsum("jgrn,njd->rjgd", dscore, block_keys, preferred_element_type=jnp.float32)
        * score_scale
    ).astype(jnp.bfloat16)
    key_terms = (
        jnp.einsum("jgrn,rjgd->njd", dscore, query_head_count, preferred_element_type=jnp.float32)
        * score_scale
    )
    value_terms = jnp.einsum(
        "jgrn,rjgd->njd", rounded_probs, head_cotangents, preferred_element_type=jnp.float32
    )
    return (attention, query_grad, key_terms, value_terms)


def on_device(queries, rotated_key_rows, value_matrix, cotangent, tree_mask):
    seq_index = lax.axis_index("seq")
    key_local, value_local = (
        lax.all_gather(rotated_key_rows, "head", axis=0, tiled=True),
        lax.all_gather(value_matrix, "head", axis=0, tiled=True),
    )
    start_row = lax.axis_index("head") * queries.shape[0]
    row_count = queries.shape[0]
    seg_tokens = key_local.shape[0]
    kv_local = key_local.shape[1] // HEAD_SIZE
    group_width = QUERY_HEADS // KEY_VALUE_HEADS
    prompt_keys, prompt_values = (broadcast(key_local, "seq", 0), broadcast(value_local, "seq", 0))
    block_keys = jnp.concatenate([prompt_keys, key_local], 0).reshape(
        2 * seg_tokens, kv_local, HEAD_SIZE
    )
    block_values = jnp.concatenate([prompt_values, value_local], 0).reshape(
        2 * seg_tokens, kv_local, HEAD_SIZE
    )
    token_mask = jnp.repeat(jnp.repeat(tree_mask, MASK_BLOCK_SIZE, axis=0), MASK_BLOCK_SIZE, axis=1)
    mask_rows = lax.dynamic_slice_in_dim(token_mask, start_row, row_count, 0)
    prompt_reads = (mask_rows > 0) & (seq_index > 0)
    positions = start_row + jnp.arange(row_count, dtype=jnp.int32)
    causal = jnp.arange(seg_tokens, dtype=jnp.int32)[None, :] <= positions[:, None]
    allowed = jnp.concatenate([prompt_reads, causal], 1)
    query_head_count = queries.reshape(row_count, kv_local, group_width, HEAD_SIZE)
    head_cotangents = cotangent.reshape(row_count, kv_local, group_width, HEAD_SIZE)
    attention, query_grad, key_terms, value_terms = attend(
        query_head_count, block_keys, block_values, head_cotangents, allowed
    )
    attention = attention.reshape(row_count, kv_local * group_width * HEAD_SIZE)
    query_grad = query_grad.reshape(row_count, kv_local * group_width * HEAD_SIZE)
    prompt_key_terms = key_terms[:seg_tokens].reshape(seg_tokens, kv_local * HEAD_SIZE)
    prompt_value_terms = value_terms[:seg_tokens].reshape(seg_tokens, kv_local * HEAD_SIZE)
    own_key = key_terms[seg_tokens:].reshape(seg_tokens, kv_local * HEAD_SIZE)
    own_value = value_terms[seg_tokens:].reshape(seg_tokens, kv_local * HEAD_SIZE)
    is_owner = seq_index == 0
    summed_key, summed_value, share_key, share_value = (
        lax.psum_scatter(own_key, "head", scatter_dimension=0, tiled=True),
        lax.psum_scatter(own_value, "head", scatter_dimension=0, tiled=True),
        lax.psum_scatter(prompt_key_terms, "head", scatter_dimension=0, tiled=True),
        lax.psum_scatter(prompt_value_terms, "head", scatter_dimension=0, tiled=True),
    )
    owner_key, owner_value = lax.psum((share_key, share_value), "seq")
    key_gradient = (summed_key + jnp.where(is_owner, owner_key, jnp.float32(0.0))).astype(
        jnp.bfloat16
    )
    value_gradient = (summed_value + jnp.where(is_owner, owner_value, jnp.float32(0.0))).astype(
        jnp.bfloat16
    )
    return (attention, query_grad, key_gradient, value_gradient)


def solution(mesh):
    in_specs = (
        P(("seq", "head"), None),
        P(("seq", "head"), None),
        P(("seq", "head"), None),
        P(("seq", "head"), None),
        P("seq", None),
    )
    out_specs = (
        P(("seq", "head"), None),
        P(("seq", "head"), None),
        P(("seq", "head"), None),
        P(("seq", "head"), None),
    )
    return jax.shard_map(
        on_device, mesh=mesh, in_specs=in_specs, out_specs=out_specs, check_vma=False
    )
```

profile of v0, /device:TPU:0, one launch (start us, length us, event | category | flops | bytes accessed | tf_op | source)
XLA Modules:
  0.0 331.5 jit_solution(10383871843600649964)
XLA Ops:
  7.2 0.0 copy-start.6
  7.2 0.0 all-reduce.7.cloned.1.call-start
  7.2 1.1 copy.29
  8.3 1.0 copy.27
  9.4 8.6 %all_gather.6 = bf16[512,512]{0,1:T(8,128)(2,1)S(1)} all-gather(bf16[128,512]{0,1:T(8,128)(2,1)S(1)} %copy.27), channel_id=1, replica_groups=mesh['seq'=8,'head'=4] {'head'}, dimensions={0}, use_global_device_ids=true | all-gather | bytes 655360 | tf_op jit(solution)/shard_map/all_gather | solution.py:59
  18.0 7.3 %all_gather.7 = bf16[512,512]{0,1:T(8,128)(2,1)S(1)} all-gather(bf16[128,512]{0,1:T(8,128)(2,1)S(1)} %copy.29), channel_id=1, replica_groups=mesh['seq'=8,'head'=4] {'head'}, dimensions={0}, use_global_device_ids=true | all-gather | bytes 655360 | tf_op jit(solution)/shard_map/all_gather | solution.py:58
  25.3 0.8 broadcast_select_fusion
  26.1 0.8 broadcast_select_fusion.1
  26.9 0.0 all-reduce.7.cloned.1.call-update
  27.0 0.0 reduce-scatter.11.cloned.1.call-start
  27.0 0.8 copy.28
  27.8 0.1 broadcast_bitcast_fusion
  27.9 2.2 copy.30
  30.1 0.0 copy-done.6
  30.1 0.6 copy.34
  30.7 0.1 broadcast_in_dim.35
  30.8 0.1 iota_compare_fusion
  31.0 75.5 %all-reduce.7.cloned.1.call-done = (bf16[512,512]{0,1:T(8,128)(2,1)}, bf16[512,512]{0,1:T(8,128)(2,1)}) async-done(((bf16[512,512]{0,1:T(8,128)(2,1)}, bf16[512,512]{0,1:T(8,128)(2,1)}), (bf16[512,512]{0,1:T(8,128)(2,1)}, bf16[512,512]{0,1:T(8,128)(2,1)})) %all-reduce.7.cloned.1.call-update) | async-done | bytes 1048592 | tf_op jit(solution)/shard_map/psum | solution.py:14
  106.5 2.5 pad_maximum_fusion
  109.0 10.1 %fusion.16 = (f32[4,7,128]{2,1,0:T(8,128)S(1)}, f32[4,7,128,1024]{2,3,1,0:T(8,128)}) fusion(pred[128,1024]{0,1:T(8,128)(4,1)S(1)} %pad_add_fusion, bf16[1024,4,128,1]{0,2,3,1:T(8,128)(2,1)S(1)} %bitcast.84, bf16[128,4,7,128]{0,3,2,1:T(8,128)(2,1)} %bitcast.93), kind=kOutput, calls=%fused_computation.36 | convolution fusion | flops 957875200 | bytes 16791552 | tf_op jit(solution)/shard_map/sub | solution.py:27
  119.1 9.9 %fusion.7 = bf16[4,7,128,1024]{2,3,1,0:T(8,128)(2,1)} fusion(f32[4,7,128,1024]{2,3,1,0:T(8,128)} %get-tuple-element.21, f32[4,7,128]{2,1,0:T(8,128)S(1)} %get-tuple-element.20), kind=kLoop, calls=%fused_computation.11 | loop fusion | flops 7340032 | bytes 22034432 | tf_op jit(solution)/shard_map/convert_element_type | solution.py:29
  128.9 0.0 copy-start
  128.9 0.0 copy-start.2
  128.9 5.7 %convolution_bitcast_fusion = f32[1024,4,128]{0,2,1:T(8,128)S(1)} fusion(bf16[4,7,128,1024]{2,3,1,0:T(8,128)(2,1)} %fusion.7, bf16[128,4,7,128]{0,3,2,1:T(8,128)(2,1)S(1)} %bitcast.81), kind=kOutput, calls=%fused_computation.16 | convolution fusion | flops 939524096 | bytes 10354688 | tf_op jit(solution)/shard_map/jgrn,rjgd->njd/dot_general | solution.py:49
  134.6 0.0 copy-done
  134.6 0.0 copy-done.2
  134.6 2.3 multiply_reduce_fusion
  136.9 1.5 fusion.14
  138.4 2.5 copy.43
  140.9 0.0 reduce-scatter.11.cloned.1.call-update
  141.0 0.2 reduce-scatter.7.cloned.1.call-start
  141.2 0.0 copy-start.5
  141.2 6.8 %fusion.2 = bf16[4,7,128,1024]{2,3,1,0:T(8,128)(2,1)S(1)} fusion(bf16[1024,4,128,1]{0,2,3,1:T(8,128)(2,1)S(1)} %bitcast.87, bf16[128,4,7,128]{0,3,2,1:T(8,128)(2,1)S(1)} %bitcast.83, f32[4,7,128]{2,1,0:T(8,128)S(1)} %bitcast.98, f32[4,7,128,1024]{2,3,1,0:T(8,128)} %get-tuple-element.21, f32[4,7,128]{2,1,0:T(8,128)S(1)} %get-tuple-element.20), kind=kOutput, calls=%fused_computation.3 | convolution fusion | flops 954204160 | bytes 24014848 | tf_op jit(solution)/shard_map/rjgd,njd->jgrn/dot_general | solution.py:37
  148.0 0.0 copy-start.1
  148.0 2.9 copy-done.1
  150.9 0.0 copy-done.5
  150.9 0.0 copy-start.3
  150.9 2.5 fusion.8
  153.4 1.2 fusion.15
  154.6 2.6 copy.40
  157.2 0.0 reduce-scatter.7.cloned.1.call-update
  157.2 0.0 reduce-scatter.9.cloned.1.call-start
  157.3 0.0 copy-done.3
  157.3 1.3 copy.42
  158.7 0.0 reduce-scatter.9.cloned.1.call-update
  158.7 0.0 all-reduce.5.cloned.1.call-start
  158.7 6.8 %reduce-scatter.11.cloned.1.call-done = f32[128,512]{1,0:T(8,128)} async-done(((f32[512,512]{1,0:T(8,128)}), f32[128,512]{1,0:T(8,128)}) %reduce-scatter.11.cloned.1.call-update) | async-done | bytes 262160 | tf_op jit(solution)/shard_map/reduce_scatter | solution.py:95
  165.5 27.5 %reduce-scatter.7.cloned.1.call-done = f32[128,512]{1,0:T(8,128)} async-done(((f32[512,512]{1,0:T(8,128)}), f32[128,512]{1,0:T(8,128)}) %reduce-scatter.7.cloned.1.call-update) | async-done | bytes 262160 | tf_op jit(solution)/shard_map/reduce_scatter | solution.py:94
  193.0 0.0 copy-start.4
  193.0 0.0 all-reduce.5.cloned.1.call-update
  193.0 0.0 reduce-scatter.5.cloned.1.call-start
  193.0 1.4 copy.39
  194.4 0.0 reduce-scatter.5.cloned.1.call-update
  194.5 4.4 %multiply_convert_fusion = bf16[4,128,7,128]{3,1,2,0:T(8,128)(2,1)S(1)} fusion(bf16[1024,4,128,1]{0,2,3,1:T(8,128)(2,1)S(1)} %bitcast.85, bf16[4,7,128,1024]{2,3,1,0:T(8,128)(2,1)} %copy-done.1), kind=kOutput, calls=%fused_computation.14 | convolution fusion | flops 940441600 | bytes 9306112 | tf_op jit(solution)/shard_map/jgrn,njd->rjgd/dot_general | solution.py:42
  198.8 1.3 copy.45
  200.1 0.0 copy-done.4
  200.1 1.3 copy.44
  201.4 19.0 %reduce-scatter.9.cloned.1.call-done = f32[128,512]{1,0:T(8,128)} async-done(((f32[512,512]{1,0:T(8,128)}), f32[128,512]{1,0:T(8,128)}) %reduce-scatter.9.cloned.1.call-update) | async-done | bytes 262160 | tf_op jit(solution)/shard_map/reduce_scatter | solution.py:93
  220.4 75.9 %all-reduce.5.cloned.1.call-done = (f32[128,512]{1,0:T(8,128)}, f32[128,512]{1,0:T(8,128)}) async-done(((f32[128,512]{1,0:T(8,128)}, f32[128,512]{1,0:T(8,128)}), (f32[128,512]{1,0:T(8,128)}, f32[128,512]{1,0:T(8,128)})) %all-reduce.5.cloned.1.call-update) | async-done | bytes 524304 | tf_op jit(solution)/shard_map/psum | solution.py:97
  296.3 1.7 add_convert_fusion
  298.0 24.9 %reduce-scatter.5.cloned.1.call-done = f32[128,512]{1,0:T(8,128)} async-done(((f32[512,512]{1,0:T(8,128)}), f32[128,512]{1,0:T(8,128)}) %reduce-scatter.5.cloned.1.call-update) | async-done | bytes 262160 | tf_op jit(solution)/shard_map/reduce_scatter | solution.py:92
  323.0 1.7 add_convert_fusion.1
  (3 shorter events, 0.0 us)
Async XLA Ops:
  7.2 22.9 %copy-start.6 = (bf16[128,3584]{1,0:T(8,128)(2,1)S(1)}, bf16[128,3584]{1,0:T(8,128)(2,1)}, u32[]{:S(2)}) copy-start(bf16[128,3584]{1,0:T(8,128)(2,1)} %param.8) | copy-start | bytes 2752516
  7.2 99.3 %all-reduce.7.cloned.1.call-start = ((), (), s32[]{:S(2)}) async-start(), calls=%async_computation.9 | async-start | bytes 2097152 | tf_op jit(solution)/shard_map/psum | solution.py:14
  27.0 138.5 %reduce-scatter.11.cloned.1.call-start = ((), (), s32[]{:S(2)}) async-start(), calls=%async_computation.7 | async-start | bytes 1310720 | tf_op jit(solution)/shard_map/reduce_scatter | solution.py:95
  128.9 5.7 %copy-start = (bf16[4,7,128,1024]{2,3,1,0:T(8,128)(2,1)S(1)}, bf16[4,7,128,1024]{2,3,1,0:T(8,128)(2,1)}, u32[]{:S(2)}) copy-start(bf16[4,7,128,1024]{2,3,1,0:T(8,128)(2,1)} %fusion.7) | copy-start | bytes 22020100
  128.9 5.7 %copy-start.2 = (bf16[1024,512]{0,1:T(8,128)(2,1)S(1)}, bf16[1024,512]{0,1:T(8,128)(2,1)}, u32[]{:S(2)}) copy-start(bf16[1024,512]{0,1:T(8,128)(2,1)} %get-tuple-element.24) | copy-start | bytes 3145732
  141.0 52.0 %reduce-scatter.7.cloned.1.call-start = ((), (), s32[]{:S(2)}) async-start(), calls=%async_computation.5 | async-start | bytes 1310720 | tf_op jit(solution)/shard_map/reduce_scatter | solution.py:94
  141.2 9.7 %copy-start.5 = (bf16[128,3584]{0,1:T(8,128)(2,1)S(1)}, bf16[128,3584]{0,1:T(8,128)(2,1)}, u32[]{:S(2)}) copy-start(bf16[128,3584]{0,1:T(8,128)(2,1)} %copy.30) | copy-start | bytes 2752516
  148.0 2.9 copy-start.1
  150.9 6.4 %copy-start.3 = (f32[512,4,128]{0,2,1:T(8,128)S(1)}, f32[512,4,128]{0,2,1:T(8,128)}, u32[]{:S(2)}) copy-start(f32[512,4,128]{0,2,1:T(8,128)} %get-tuple-element.16) | copy-start | bytes 3145732
  157.2 63.2 %reduce-scatter.9.cloned.1.call-start = ((), (), s32[]{:S(2)}) async-start(), calls=%async_computation.6 | async-start | bytes 1310720 | tf_op jit(solution)/shard_map/reduce_scatter | solution.py:93
  158.7 137.6 %all-reduce.5.cloned.1.call-start = ((), (), s32[]{:S(2)}) async-start(), calls=%async_computation.8 | async-start | bytes 1048576 | tf_op jit(solution)/shard_map/psum | solution.py:97
  193.0 7.1 %copy-start.4 = (bf16[4,128,7,128]{3,1,2,0:T(8,128)(2,1)S(1)}, bf16[4,128,7,128]{3,1,2,0:T(8,128)(2,1)}, u32[]{:S(2)}) copy-start(bf16[4,128,7,128]{3,1,2,0:T(8,128)(2,1)} %get-tuple-element.23) | copy-start | bytes 2752516
  193.0 130.0 %reduce-scatter.5.cloned.1.call-start = ((), (), s32[]{:S(2)}) async-start(), calls=%async_computation.4 | async-start | bytes 1310720 | tf_op jit(solution)/shard_map/reduce_scatter | solution.py:92
Sparse Core Ops, SparseCore 0:
  27.1 79.3 all-reduce.6
  141.1 24.3 reduce-scatter.10
  168.0 24.8 reduce-scatter.6
  195.5 24.8 reduce-scatter.8
  223.7 72.5 all-reduce.4
  298.9 24.0 reduce-scatter.4
where the time goes:
time: 332 us
  waiting for transfers between devices  230 us (69%)
  matrix products  31.6 us (10%)
  local copies, waits for them, and re-layouts  22 us (7%)
  other arithmetic  17.6 us (5%)
  blocking collectives  15.9 us (5%)
  between operations  14.3 us (4%)
    psum x1, waiting for transfers between devices, on_device(): owner_key, owner_value = lax.psum((share_key, share_value), 'seq')  75.9 us
    psum x1, waiting for transfers between devices, broadcast(): return lax.psum(kept, axis)  75.5 us
    reduce_scatter x1, waiting for transfers between devices, on_device(): lax.psum_scatter(prompt_key_terms, 'head', scatter_dimension=0, tiled=True)  27.5 us
    reduce_scatter x1, waiting for transfers between devices, on_device(): lax.psum_scatter(own_key, 'head', scatter_dimension=0, tiled=True)  24.9 us
    reduce_scatter x1, waiting for transfers between devices, on_device(): lax.psum_scatter(own_value, 'head', scatter_dimension=0, tiled=True)  19 us
    unnamed x23, local copies, waits for them, and re-layouts  11.3 us
    sub x1, matrix products, attend(): weights = jnp.where(allowed, jnp.exp(scores - row_max), jnp.float32(0.0))  10.1 us
    convert_element_type x1, other arithmetic, attend(): rounded_probs = softmax_probs.astype(jnp.bfloat16)  9.85 us
  transfers between devices with their start and end apart: 6, of which 6 were waited for; matrix products, arithmetic and copies ran while one was open for 9% of the time, Pallas kernels for 0%

commit v1 on v0

v1 whole, which is shorter than its diff:
```python
import functools
import math

import jax
import jax.numpy as jnp
from jax import lax
from jax.experimental import pallas as pl
from jax.experimental.pallas import tpu as pltpu
from jax.sharding import PartitionSpec as P

QUERY_HEADS = 28
KEY_VALUE_HEADS = 4
HEAD_SIZE = 128
GROUP = QUERY_HEADS // KEY_VALUE_HEADS
WIDTH = GROUP * HEAD_SIZE
SCALE = HEAD_SIZE ** (-0.5)
EXP2_SCALE = SCALE * math.log2(math.e)
MASKED = -1e30
VMEM_BYTES = 24 * 1024 * 1024


def dot_nt(a, b):
    return lax.dot_general(a, b, (((1,), (1,)), ((), ())), preferred_element_type=jnp.float32)


def dot_nn(a, b):
    return lax.dot_general(a, b, (((1,), (0,)), ((), ())), preferred_element_type=jnp.float32)


def head_rows(mine, sibling, g):
    columns = slice(g * HEAD_SIZE, (g + 1) * HEAD_SIZE)
    return jnp.concatenate([mine[:, columns], sibling[:, columns]], axis=0)


def causal_mask(scores, rows, h):
    lane = lax.broadcasted_iota(jnp.int32, (rows, rows), 1)
    sub = lax.broadcasted_iota(jnp.int32, (rows, rows), 0)
    ahead = lane - sub
    out = []
    for b in range(scores.shape[0] // rows):
        line = []
        for a in range(2):
            offset = ((h ^ b) - (h ^ a)) * rows
            tile = scores[b * rows : (b + 1) * rows, a * rows : (a + 1) * rows]
            line.append(jnp.where(ahead >= offset, tile, MASKED))
        out.append(jnp.concatenate(line, axis=1))
    return jnp.concatenate(out, axis=0)


def prompt_mask(scores, rows, h, s, tree_ref):
    lane = lax.broadcasted_iota(jnp.int32, (1, 2 * rows), 1)
    out = []
    for b in range(scores.shape[0] // rows):
        reads = [jnp.logical_and(tree_ref[h ^ a, h ^ b] > 0, s > 0) for a in range(2)]
        bias = [jnp.where(r, jnp.float32(0.0), jnp.float32(MASKED)) for r in reads]
        row = jnp.where(lane < rows, bias[0], bias[1])
        out.append(scores[b * rows : (b + 1) * rows] + row)
    return jnp.concatenate(out, axis=0)


def stats_kernel(ids, tree, qm, qs, cm, cs, near, far, stats):
    h = ids[0]
    rows = qm.shape[0]
    keys = jnp.concatenate([near[:, :HEAD_SIZE], far[:, :HEAD_SIZE]], axis=0)
    values = jnp.concatenate([near[:, HEAD_SIZE:], far[:, HEAD_SIZE:]], axis=0)
    for g in range(GROUP):
        q = head_rows(qm, qs, g)
        ct = head_rows(cm, cs, g)
        scores = causal_mask(dot_nt(keys, q), rows, h)
        top = jnp.max(scores, axis=0, keepdims=True)
        e = jnp.exp2((scores - top) * EXP2_SCALE)
        dprob = dot_nt(values, ct)
        stats[g, 0:1, :] = top
        stats[g, 1:2, :] = jnp.sum(e, axis=0, keepdims=True)
        stats[g, 2:3, :] = jnp.sum(e * dprob, axis=0, keepdims=True)


def prompt_kernel(ids, tree, qm, qs, cm, cs, near, far, own, stats, att, dq, terms, key_sum, value_sum):
    h = ids[0]
    s = ids[1]
    rows = qm.shape[0]
    keys = jnp.concatenate([near[:, :HEAD_SIZE], far[:, :HEAD_SIZE]], axis=0)
    values = jnp.concatenate([near[:, HEAD_SIZE:], far[:, HEAD_SIZE:]], axis=0)
    keys_t = keys.T
    values_t = values.T
    for g in range(GROUP):
        q = head_rows(qm, qs, g)
        ct = head_rows(cm, cs, g)
        scores = prompt_mask(dot_nt(keys, q), rows, h, s, tree)
        own_top = own[g, 0:1, :]
        top = jnp.maximum(own_top, jnp.max(scores, axis=0, keepdims=True))
        e = jnp.exp2((scores - top) * EXP2_SCALE)
        keep = jnp.exp2((own_top - top) * EXP2_SCALE)
        dprob = dot_nt(values, ct)
        inverse = 1.0 / (own[g, 1:2, :] * keep + jnp.sum(e, axis=0, keepdims=True))
        delta = (own[g, 2:3, :] * keep + jnp.sum(e * dprob, axis=0, keepdims=True)) * inverse
        probs = e * inverse
        rounded = probs.astype(jnp.bfloat16)
        dscore = (probs * (dprob - delta)).astype(jnp.bfloat16)
        stats[g, 0:1, :] = top
        stats[g, 1:2, :] = inverse
        stats[g, 2:3, :] = delta
        value_term = dot_nn(rounded, ct)
        key_term = dot_nn(dscore, q)
        if g == 0:
            value_sum[...] = value_term
            key_sum[...] = key_term
        else:
            value_sum[...] += value_term
            key_sum[...] += key_term
        att[g] = dot_nn(values_t, rounded)
        dq[g] = dot_nn(keys_t, dscore)
    terms[:, :HEAD_SIZE] = (key_sum[...] * SCALE).astype(terms.dtype)
    terms[:, HEAD_SIZE:] = value_sum[...].astype(terms.dtype)


def own_kernel(
    ids, tree, qm, qs, cm, cs, near, far, stats, att_p, dq_p,
    att_m, att_s, dq_m, dq_s, terms_near, terms_far, key_sum, value_sum,
):
    h = ids[0]
    rows = qm.shape[0]
    keys = jnp.concatenate([near[:, :HEAD_SIZE], far[:, :HEAD_SIZE]], axis=0)
    values = jnp.concatenate([near[:, HEAD_SIZE:], far[:, HEAD_SIZE:]], axis=0)
    keys_t = keys.T
    values_t = values.T
    for g in range(GROUP):
        columns = slice(g * HEAD_SIZE, (g + 1) * HEAD_SIZE)
        q = head_rows(qm, qs, g)
        ct = head_rows(cm, cs, g)
        scores = causal_mask(dot_nt(keys, q), rows, h)
        probs = jnp.exp2((scores - stats[g, 0:1, :]) * EXP2_SCALE) * stats[g, 1:2, :]
        dprob = dot_nt(values, ct)
        rounded = probs.astype(jnp.bfloat16)
        dscore = (probs * (dprob - stats[g, 2:3, :])).astype(jnp.bfloat16)
        value_term = dot_nn(rounded, ct)
        key_term = dot_nn(dscore, q)
        if g == 0:
            value_sum[...] = value_term
            key_sum[...] = key_term
        else:
            value_sum[...] += value_term
            key_sum[...] += key_term
        att = (att_p[g] + dot_nn(values_t, rounded)).T.astype(jnp.bfloat16)
        dq = ((dq_p[g] + dot_nn(keys_t, dscore)) * SCALE).T.astype(jnp.bfloat16)
        att_m[:, columns] = att[:rows]
        att_s[:, columns] = att[rows:]
        dq_m[:, columns] = dq[:rows]
        dq_s[:, columns] = dq[rows:]
    half = terms_near.shape[0]
    for out, part in ((terms_near, slice(0, half)), (terms_far, slice(half, 2 * half))):
        out[:, :HEAD_SIZE] = (key_sum[part, :] * SCALE).astype(out.dtype)
        out[:, HEAD_SIZE:] = value_sum[part, :].astype(out.dtype)


def full(shape):
    return pl.BlockSpec(shape, lambda i, *refs: (0,) * len(shape))


def call(kernel, j, scalars, inputs, outs, scratch, products):
    specs = []
    for x, where in inputs:
        if where == "mine":
            specs.append(
                pl.BlockSpec((x.shape[0], WIDTH), lambda i, ids, tree: (0, 2 * (ids[0] & 1) + j))
            )
        elif where == "half":
            specs.append(pl.BlockSpec((x.shape[0], WIDTH), lambda i, ids, tree: (0, j)))
        else:
            specs.append(full(x.shape))
    rows = inputs[0][0].shape[0]
    flops = 2 * products * (2 * rows * GROUP) * (4 * rows) * HEAD_SIZE
    return pl.pallas_call(
        kernel,
        grid_spec=pltpu.PrefetchScalarGridSpec(
            num_scalar_prefetch=2,
            grid=(1,),
            in_specs=specs,
            out_specs=[full(o.shape) for o in outs],
            scratch_shapes=scratch,
        ),
        out_shape=outs,
        compiler_params=pltpu.CompilerParams(vmem_limit_bytes=VMEM_BYTES),
        cost_estimate=pl.CostEstimate(
            flops=flops, bytes_accessed=4 * 2 * rows * WIDTH * 2, transcendentals=0
        ),
    )(*scalars, *[x for x, _ in inputs])


def on_device(seq_count, head_count, queries, rotated_key_rows, value_matrix, cotangent, tree_mask):
    s = lax.axis_index("seq")
    h = lax.axis_index("head")
    rows = queries.shape[0]
    half_heads = KEY_VALUE_HEADS // 2
    half = half_heads * HEAD_SIZE
    core = h & 1
    pair = [(i, i ^ 1) for i in range(head_count)]
    cross = [(i, i ^ 2) for i in range(head_count)]
    scalars = (jnp.stack([h, s]).astype(jnp.int32), tree_mask)

    def columns(x, place, width):
        return lax.dynamic_slice_in_dim(x, place * width, width, 1)

    def chunk(place, j):
        return jnp.concatenate(
            [
                columns(rotated_key_rows, half_heads * place + j, HEAD_SIZE),
                columns(value_matrix, half_heads * place + j, HEAD_SIZE),
            ],
            axis=1,
        )

    near, far, prompt_near, prompt_far = [], [], [], []
    for j in range(half_heads):
        got = lax.ppermute(chunk(1 - core, j), "head", pair)
        near.append(jnp.concatenate([chunk(core, j), got], axis=0))
    for j in range(half_heads):
        held = near[j]
        step = seq_count // 2
        while step:
            sends = [(i, i + step) for i in range(0, seq_count, 2 * step)]
            got = lax.ppermute(held, "seq", sends)
            held = jnp.where(s % (2 * step) == step, got, held)
            step //= 2
        prompt_near.append(held)
        prompt_far.append(lax.ppermute(held, "head", cross))
    for j in range(half_heads):
        far.append(lax.ppermute(near[j], "head", cross))

    query_width = half_heads * WIDTH
    q_sib = lax.ppermute(columns(queries, 1 - core, query_width), "head", pair)
    c_sib = lax.ppermute(columns(cotangent, 1 - core, query_width), "head", pair)

    f32, bf16 = jnp.float32, jnp.bfloat16
    shape = jax.ShapeDtypeStruct
    sums = [pltpu.VMEM((4 * rows, HEAD_SIZE), f32)] * 2
    stats_shape = shape((GROUP, 8, 2 * rows), f32)
    part_shape = shape((GROUP, HEAD_SIZE, 2 * rows), f32)
    rows_shape = shape((rows, WIDTH), bf16)
    att_m, att_s, dq_m, dq_s, totals = [], [], [], [], []
    heads = [
        [(queries, "mine"), (q_sib, "half"), (cotangent, "mine"), (c_sib, "half")]
        for _ in range(half_heads)
    ]
    own = [
        call(
            stats_kernel, j, scalars, heads[j] + [(near[j], ""), (far[j], "")], [stats_shape], [], 2
        )[0]
        for j in range(half_heads)
    ]
    mids = [
        call(
            prompt_kernel,
            j,
            scalars,
            heads[j] + [(prompt_near[j], ""), (prompt_far[j], ""), (own[j], "")],
            [stats_shape, part_shape, part_shape, shape((4 * rows, 2 * HEAD_SIZE), bf16)],
            sums,
            6,
        )
        for j in range(half_heads)
    ]
    prompt_sums = []
    for j in range(half_heads):
        terms = mids[j][3]
        got = lax.ppermute(terms[2 * rows :], "head", cross)
        total = terms[: 2 * rows].astype(f32) + got.astype(f32)
        step = 1
        while step < seq_count:
            sends = [(i + step, i) for i in range(0, seq_count, 2 * step)]
            got = lax.ppermute(total.astype(bf16), "seq", sends)
            total = total + got.astype(f32)
            step *= 2
        prompt_sums.append(total)
    for j in range(half_heads):
        a_m, a_s, d_m, d_s, t_near, t_far = call(
            own_kernel,
            j,
            scalars,
            heads[j] + [(near[j], ""), (far[j], "")] + [(x, "") for x in mids[j][:3]],
            [rows_shape] * 4 + [shape((2 * rows, 2 * HEAD_SIZE), f32), shape((2 * rows, 2 * HEAD_SIZE), bf16)],
            sums,
            6,
        )
        att_m.append(a_m)
        att_s.append(a_s)
        dq_m.append(d_m)
        dq_s.append(d_s)
        got = lax.ppermute(t_far, "head", cross)
        totals.append(t_near + got.astype(f32))

    def both_halves(mine, theirs):
        mine, theirs = jnp.concatenate(mine, axis=1), jnp.concatenate(theirs, axis=1)
        return jnp.where(
            core == 0,
            jnp.concatenate([mine, theirs], axis=1),
            jnp.concatenate([theirs, mine], axis=1),
        )

    def swap(x):
        return lax.ppermute(x, "head", pair)

    attention = both_halves(att_m, [swap(x) for x in att_s])
    query_grad = both_halves(dq_m, [swap(x) for x in dq_s])
    mine, theirs = [], []
    for j in range(half_heads):
        total = totals[j] + jnp.where(s == 0, prompt_sums[j], jnp.float32(0.0))
        total = total.astype(bf16)
        mine.append(total[:rows])
        theirs.append(swap(total[rows:]))
    key_gradient = both_halves(
        [x[:, :HEAD_SIZE] for x in mine], [x[:, :HEAD_SIZE] for x in theirs]
    )
    value_gradient = both_halves(
        [x[:, HEAD_SIZE:] for x in mine], [x[:, HEAD_SIZE:] for x in theirs]
    )
    return (attention, query_grad, key_gradient, value_gradient)


def solution(mesh):
    spec = P(("seq", "head"), None)
    return jax.shard_map(
        functools.partial(on_device, mesh.shape["seq"], mesh.shape["head"]),
        mesh=mesh,
        in_specs=(spec, spec, spec, spec, P("seq", None)),
        out_specs=(spec, spec, spec, spec),
        check_vma=False,
    )
```

time: 332 us -> 96.4 us (0.29)
  waiting for transfers between devices: 230 us -> 28 us
  starting transfers between devices: 0.42 us -> 38.2 us
  matrix products: 31.6 us -> 0 us
  Pallas kernels: 0 us -> 22 us
  local copies, waits for them, and re-layouts: 22 us -> 2.14 us
  blocking collectives: 15.9 us -> 0 us
  between operations: 14.3 us -> 1.06 us
  other arithmetic: 17.6 us -> 4.5 us
    psum x2 -> x0, waiting for transfers between devices: 151 us -> none  [the longest x1 75.9 us: on_device(): owner_key, owner_value = lax.psum((share_key, share_value), 'seq')]
    reduce_scatter x4 -> x0, waiting for transfers between devices: 78.2 us -> none  [the longest x1 27.5 us: on_device(): lax.psum_scatter(prompt_key_terms, 'head', scatter_dimension=0, tiled=True)]
    ppermute x0 -> x30, starting transfers between devices: none -> 38.2 us  [the longest x6 18.5 us: on_device(): got = lax.ppermute(held, 'seq', sends)]
    ppermute x0 -> x30, waiting for transfers between devices: none -> 28 us  [the longest x6 14.8 us: on_device(): got = lax.ppermute(total.astype(bf16), 'seq', sends)]
    pallas_call x0 -> x6, Pallas kernels: none -> 22 us  [call(): pl.pallas_call(kernel, grid_spec=pltpu.PrefetchScalarGridSpec(num_scalar_...]
    dot_general x5 -> x0, matrix products: 21.5 us -> none  [the longest x1 6.77 us: attend(): jnp.einsum('rjgd,njd->jgrn', head_cotangents, block_values, preferred_ele...]
    all_gather x2 -> x0, blocking collectives: 15.9 us -> none  [the longest x1 8.62 us: on_device(): lax.all_gather(value_matrix, 'head', axis=0, tiled=True)]
    convert_element_type x3 -> x8, other arithmetic: 13.3 us -> 0.58 us  [the longest x6 0.31 us: on_device(): got = lax.ppermute(total.astype(bf16), 'seq', sends)]
  transfers between devices with their start and end apart: 6 -> 30, of which waited for: 6 -> 14; matrix products, arithmetic and copies ran while one was open for 9% -> 4% of each run, Pallas kernels for 0% -> 23%
where the time goes in v1:
time: 96.4 us; the launch traced here: 96 us
  starting transfers between devices  38.2 us (40%)
  waiting for transfers between devices  28 us (29%)
  Pallas kernels  22 us (23%)
  other arithmetic  4.5 us (5%)
  local copies, waits for them, and re-layouts  2.14 us (2%)
  between operations  1.06 us (1%)
    pallas_call x6, Pallas kernels, call(): pl.pallas_call(kernel, grid_spec=pltpu.PrefetchScalarGridSpec(num_scalar_...  22 us
    ppermute x6, starting transfers between devices, on_device(): got = lax.ppermute(held, 'seq', sends)  18.5 us
    ppermute x6, waiting for transfers between devices, on_device(): got = lax.ppermute(total.astype(bf16), 'seq', sends)  14.8 us
    ppermute x6, waiting for transfers between devices, on_device(): got = lax.ppermute(held, 'seq', sends)  11.1 us
    ppermute x6, starting transfers between devices, on_device(): got = lax.ppermute(total.astype(bf16), 'seq', sends)  7.73 us
    select_n x4, other arithmetic, both_halves(): jnp.where(core == 0, jnp.concatenate([mine, theirs], axis=1), jnp.concate...  3.65 us
    ppermute x2, starting transfers between devices, on_device(): got = lax.ppermute(terms[2 * rows:], 'head', cross)  3.13 us
    ppermute x2, starting transfers between devices, on_device(): far.append(lax.ppermute(near[j], 'head', cross))  3.05 us
  transfers between devices with their start and end apart: 30, of which 14 were waited for; matrix products, arithmetic and copies ran while one was open for 4% of the time, Pallas kernels for 23%

profile of v1, /device:TPU:0, one launch (start us, length us, event | category | flops | bytes accessed | tf_op | source)
XLA Modules:
  0.0 96.0 jit_solution(10099027884881208810)
XLA Ops:
  0.7 1.0 %constant_dynamic-slice_fusion.6 = (bf16[128,128]{1,0:T(8,128)(2,1)S(1)}, bf16[128,128]{1,0:T(8,128)(2,1)S(1)}, bf16[128,128]{1,0:T(8,128)(2,1)S(1)}, bf16[128,1...) fusion(bf16[128,512]{1,0:T(8,128)(2,1)} %param.7, ...), kind=kLoop, calls=%fused_computation.34 | loop fusion | bytes 524304 | tf_op jit(solution)/shard_map/dynamic_slice | solution.py:202
  1.7 0.5 collective-permute-start.8
  2.2 0.1 collective-permute-start.2
  2.3 1.0 %constant_dynamic-slice_fusion.8 = bf16[128,1792]{1,0:T(8,128)(2,1)S(1)} fusion(bf16[128,3584]{1,0:T(8,128)(2,1)} %cm.11, s32[]{:T(128)S(6)} %select_n.110), kind=kLoop, calls=%fused_computation.36 | loop fusion | bytes 917508 | tf_op jit(solution)/shard_map/dynamic_slice | solution.py:202
  3.4 0.5 collective-permute-start.1
  3.9 0.1 collective-permute-start
  4.1 5.9 %collective-permute-start.4 = (bf16[256,256]{1,0:T(8,128)(2,1)S(1)}, bf16[256,256]{1,0:T(8,128)(2,1)S(1)}, u32[]{:S(2)}, u32[]{:S(2)}) collective-permute-start(bf16[256,256]{1,0:T(8,128)(2,1)S(1)} %pad_maximum_fusion.near), channel_id=1, source_target_pairs={{0,16},{1,17},{2,18},{3,19}} | collective-permute-start | bytes 393224 | tf_op jit(solution)/shard_map/ppermute | solution.py:222
  10.0 0.1 pad_add_fusion.ids
  10.1 1.3 %collective-permute-start.10 = (bf16[256,256]{1,0:T(8,128)(2,1)S(1)}, bf16[256,256]{1,0:T(8,128)(2,1)S(1)}, u32[]{:S(2)}, u32[]{:S(2)}) collective-permute-start(bf16[256,256]{1,0:T(8,128)(2,1)S(1)} %pad_maximum_fusion.1.near), channel_id=1, source_target_pairs={{0,16},{1,17},{2,18},{3,19}} | collective-permute-start | bytes 393224 | tf_op jit(solution)/shard_map/ppermute | solution.py:222
  11.4 1.6 %collective-permute-start.9 = (bf16[256,256]{1,0:T(8,128)(2,1)S(1)}, bf16[256,256]{1,0:T(8,128)(2,1)S(1)}, u32[]{:S(2)}, u32[]{:S(2)}) collective-permute-start(bf16[256,256]{1,0:T(8,128)(2,1)S(1)} %pad_maximum_fusion.1.near), channel_id=1, source_target_pairs={{0,2},{1,3},{2,0},{3,1},{4,6},{5,7},{6,4},{7,5},{8,10},{9,11},{10,... | collective-permute-start | bytes 393224 | tf_op jit(solution)/shard_map/ppermute | solution.py:228
  13.0 0.9 collective-permute-done.4
  13.9 1.5 %collective-permute-start.3 = (bf16[256,256]{1,0:T(8,128)(2,1)S(1)}, bf16[256,256]{1,0:T(8,128)(2,1)S(1)}, u32[]{:S(2)}, u32[]{:S(2)}) collective-permute-start(bf16[256,256]{1,0:T(8,128)(2,1)S(1)} %pad_maximum_fusion.near), channel_id=1, source_target_pairs={{0,2},{1,3},{2,0},{3,1},{4,6},{5,7},{6,4},{7,5},{8,10},{9,11},{10,... | collective-permute-start | bytes 393224 | tf_op jit(solution)/shard_map/ppermute | solution.py:228
  15.4 0.0 copy-start.1
  15.4 0.0 copy-start.2
  15.4 0.3 collective-permute-done.10
  15.8 1.3 %collective-permute-start.5 = (bf16[256,256]{1,0:T(8,128)(2,1)S(1)}, bf16[256,256]{1,0:T(8,128)(2,1)S(1)}, u32[]{:S(2)}, u32[]{:S(2)}) collective-permute-start(bf16[256,256]{1,0:T(8,128)(2,1)S(1)} %broadcast_select_fusion.1), channel_id=1, source_target_pairs={{0,8},{16,24},{1,9},{17,25},{2,10},{18,26},{3,11},{19,27}} | collective-permute-start | bytes 393224 | tf_op jit(solution)/shard_map/ppermute | solution.py:222
  17.1 2.5 %collective-permute-done.5 = bf16[256,256]{1,0:T(8,128)(2,1)S(1)} collective-permute-done((bf16[256,256]{1,0:T(8,128)(2,1)S(1)}, bf16[256,256]{1,0:T(8,128)(2,1)S(1)}, u32[]{:S(2)}, u32[]{:S(2)}) %collective-permute-start.5) | collective-permute-done | bytes 131104 | tf_op jit(solution)/shard_map/ppermute | solution.py:222
  19.5 4.3 %collective-permute-start.11 = (bf16[256,256]{1,0:T(8,128)(2,1)S(1)}, bf16[256,256]{1,0:T(8,128)(2,1)S(1)}, u32[]{:S(2)}, u32[]{:S(2)}) collective-permute-start(bf16[256,256]{1,0:T(8,128)(2,1)S(1)} %broadcast_select_fusion), channel_id=1, source_target_pairs={{0,8},{16,24},{1,9},{17,25},{2,10},{18,26},{3,11},{19,27}} | collective-permute-start | bytes 393224 | tf_op jit(solution)/shard_map/ppermute | solution.py:222
  23.9 2.5 %collective-permute-done.11 = bf16[256,256]{1,0:T(8,128)(2,1)S(1)} collective-permute-done((bf16[256,256]{1,0:T(8,128)(2,1)S(1)}, bf16[256,256]{1,0:T(8,128)(2,1)S(1)}, u32[]{:S(2)}, u32[]{:S(2)}) %collective-permute-start.11) | collective-permute-done | bytes 131104 | tf_op jit(solution)/shard_map/ppermute | solution.py:222
  26.4 1.3 %collective-permute-start.6 = (bf16[256,256]{1,0:T(8,128)(2,1)S(1)}, bf16[256,256]{1,0:T(8,128)(2,1)S(1)}, u32[]{:S(2)}, u32[]{:S(2)}) collective-permute-start(bf16[256,256]{1,0:T(8,128)(2,1)S(1)} %broadcast_select_fusion.3), channel_id=1, source_target_pairs={{0,4},{8,12},{16,20},{24,28},{1,5},{9,13},{17,21},{25,29},{2,6},{1... | collective-permute-start | bytes 393224 | tf_op jit(solution)/shard_map/ppermute | solution.py:222
  27.7 2.5 %collective-permute-done.6 = bf16[256,256]{1,0:T(8,128)(2,1)S(1)} collective-permute-done((bf16[256,256]{1,0:T(8,128)(2,1)S(1)}, bf16[256,256]{1,0:T(8,128)(2,1)S(1)}, u32[]{:S(2)}, u32[]{:S(2)}) %collective-permute-start.6) | collective-permute-done | bytes 131104 | tf_op jit(solution)/shard_map/ppermute | solution.py:222
  30.2 4.3 %collective-permute-start.12 = (bf16[256,256]{1,0:T(8,128)(2,1)S(1)}, bf16[256,256]{1,0:T(8,128)(2,1)S(1)}, u32[]{:S(2)}, u32[]{:S(2)}) collective-permute-start(bf16[256,256]{1,0:T(8,128)(2,1)S(1)} %broadcast_select_fusion.2), channel_id=1, source_target_pairs={{0,4},{8,12},{16,20},{24,28},{1,5},{9,13},{17,21},{25,29},{2,6},{1... | collective-permute-start | bytes 393224 | tf_op jit(solution)/shard_map/ppermute | solution.py:222
  34.6 2.5 %collective-permute-done.12 = bf16[256,256]{1,0:T(8,128)(2,1)S(1)} collective-permute-done((bf16[256,256]{1,0:T(8,128)(2,1)S(1)}, bf16[256,256]{1,0:T(8,128)(2,1)S(1)}, u32[]{:S(2)}, u32[]{:S(2)}) %collective-permute-start.12) | collective-permute-done | bytes 131104 | tf_op jit(solution)/shard_map/ppermute | solution.py:222
  37.0 1.5 %collective-permute-start.7 = (bf16[256,256]{1,0:T(8,128)(2,1)S(1)}, bf16[256,256]{1,0:T(8,128)(2,1)S(1)}, u32[]{:S(2)}, u32[]{:S(2)}) collective-permute-start(bf16[256,256]{1,0:T(8,128)(2,1)S(1)} %broadcast_select_fusion.5.near), channel_id=1, source_target_pairs={{0,2},{1,3},{2,0},{3,1},{4,6},{5,7},{6,4},{7,5},{8,10},{9,11},{10,... | collective-permute-start | bytes 393224 | tf_op jit(solution)/shard_map/ppermute | solution.py:226
  38.6 0.6 collective-permute-start.13
  39.2 2.3 %shard_map.87.own = f32[7,8,256]{2,1,0:T(8,128)S(1)} custom-call(s32[2]{0:T(128)S(1)} %pad_add_fusion.ids, s32[4,4]{1,0:T(4,128)S(1)} %copy-done.2, bf16[128,3584]{1,0:T(8,128)(2,1)S(1)} %copy-done, bf16[128,1792]{1,0:T(8,128)(2,1)S(1)} %collective-permute-done.qs, bf16[128,3584]{1,0:T(8,128)(2,1)S(1)} %copy-done.1, ...), custom_call_target="tpu_custom_call" | custom-call | flops 469762048 | bytes 1835008 | tf_op jit(solution)/shard_map/pallas_call | solution.py:173
  41.5 2.3 %shard_map.84.own = f32[7,8,256]{2,1,0:T(8,128)S(1)} custom-call(s32[2]{0:T(128)S(1)} %pad_add_fusion.ids, s32[4,4]{1,0:T(4,128)S(1)} %copy-done.2, bf16[128,3584]{1,0:T(8,128)(2,1)S(1)} %copy-done, bf16[128,1792]{1,0:T(8,128)(2,1)S(1)} %collective-permute-done.qs, bf16[128,3584]{1,0:T(8,128)(2,1)S(1)} %copy-done.1, ...), custom_call_target="tpu_custom_call" | custom-call | flops 469762048 | bytes 1835008 | tf_op jit(solution)/shard_map/pallas_call | solution.py:173
  43.8 5.3 %shard_map.85 = (f32[7,8,256]{2,1,0:T(8,128)S(1)}, f32[7,128,256]{2,1,0:T(8,128)S(1)}, f32[7,128,256]{2,1,0:T(8,128)S(1)}, bf16[512,256]{1,0:T(8,128)(2,1)S(1)}) custom-call(s32[2]{0:T(128)S(1)} %pad_add_fusion.ids, s32[4,4]{1,0:T(4,128)S(1)} %copy-done.2, bf16[128,3584]{1,0:T(8,128)(2,1)S(1)} %copy-done, bf16[128,1792]{1,0:T(8,128)(2,1)S(1)} %collective-permute-done.qs, ...), custom_call_target="tpu_custom_call" | custom-call | flops 1409286144 | bytes 1835008 | tf_op jit(solution)/shard_map/pallas_call | solution.py:173
  49.1 1.6 %collective-permute-start.19 = (bf16[256,256]{1,0:T(8,128)(2,1)S(1)}, bf16[256,256]{1,0:T(8,128)(2,1)S(1)}, u32[]{:S(2)}, u32[]{:S(2)}) collective-permute-start(bf16[256,256]{1,0:T(8,128)(2,1)S(1)} %slice.49), channel_id=1, source_target_pairs={{0,2},{1,3},{2,0},{3,1},{4,6},{5,7},{6,4},{7,5},{8,10},{9,11},{10,... | collective-permute-start | bytes 393224 | tf_op jit(solution)/shard_map/ppermute | solution.py:266
  50.7 3.4 %shard_map.86 = (bf16[128,896]{1,0:T(8,128)(2,1)S(1)}, bf16[128,896]{1,0:T(8,128)(2,1)S(1)}, bf16[128,896]{1,0:T(8,128)(2,1)S(1)}, bf16[128,896]{1,0:T(8,128)(2,...) custom-call(s32[2]{0:T(128)S(1)} %pad_add_fusion.ids, s32[4,4]{1,0:T(4,128)S(1)} %copy-done.2, ...), custom_call_target="tpu_custom_call" | custom-call | flops 1409286144 | bytes 1835008 | tf_op jit(solution)/shard_map/pallas_call | solution.py:173
  54.0 0.6 collective-permute-start.18
  54.6 0.5 collective-permute-start.16
  55.1 5.4 %shard_map.88 = (f32[7,8,256]{2,1,0:T(8,128)S(1)}, f32[7,128,256]{2,1,0:T(8,128)S(1)}, f32[7,128,256]{2,1,0:T(8,128)S(1)}, bf16[512,256]{1,0:T(8,128)(2,1)S(1)}) custom-call(s32[2]{0:T(128)S(1)} %pad_add_fusion.ids, s32[4,4]{1,0:T(4,128)S(1)} %copy-done.2, bf16[128,3584]{1,0:T(8,128)(2,1)S(1)} %copy-done, bf16[128,1792]{1,0:T(8,128)(2,1)S(1)} %collective-permute-done.qs, ...), custom_call_target="tpu_custom_call" | custom-call | flops 1409286144 | bytes 1835008 | tf_op jit(solution)/shard_map/pallas_call | solution.py:173
  60.6 1.6 %collective-permute-start.24 = (bf16[256,256]{1,0:T(8,128)(2,1)S(1)}, bf16[256,256]{1,0:T(8,128)(2,1)S(1)}, u32[]{:S(2)}, u32[]{:S(2)}) collective-permute-start(bf16[256,256]{1,0:T(8,128)(2,1)S(1)} %slice.52), channel_id=1, source_target_pairs={{0,2},{1,3},{2,0},{3,1},{4,6},{5,7},{6,4},{7,5},{8,10},{9,11},{10,... | collective-permute-start | bytes 393224 | tf_op jit(solution)/shard_map/ppermute | solution.py:266
  62.2 3.4 %shard_map.89 = (bf16[128,896]{1,0:T(8,128)(2,1)S(1)}, bf16[128,896]{1,0:T(8,128)(2,1)S(1)}, bf16[128,896]{1,0:T(8,128)(2,1)S(1)}, bf16[128,896]{1,0:T(8,128)(2,...) custom-call(s32[2]{0:T(128)S(1)} %pad_add_fusion.ids, s32[4,4]{1,0:T(4,128)S(1)} %copy-done.2, ...), custom_call_target="tpu_custom_call" | custom-call | flops 1409286144 | bytes 1835008 | tf_op jit(solution)/shard_map/pallas_call | solution.py:173
  65.5 0.6 collective-permute-start.23
  66.2 0.1 collective-permute-start.15
  66.3 0.6 collective-permute-start.17
  66.9 0.9 collective-permute-done.15
  67.7 1.3 %collective-permute-start.20 = (bf16[256,256]{1,0:T(8,128)(2,1)S(1)}, bf16[256,256]{1,0:T(8,128)(2,1)S(1)}, u32[]{:S(2)}, u32[]{:S(2)}) collective-permute-start(bf16[256,256]{1,0:T(8,128)(2,1)S(1)} %fusion), channel_id=1, source_target_pairs={{4,0},{12,8},{20,16},{28,24},{5,1},{13,9},{21,17},{29,25},{6,2},{1... | collective-permute-start | bytes 393224 | tf_op jit(solution)/shard_map/ppermute | solution.py:271
  69.0 1.1 %maximum_select_fusion = bf16[128,3584]{1,0:T(8,128)(2,1)} fusion(bf16[128,896]{1,0:T(8,128)(2,1)S(1)} %collective-permute-done.15, bf16[128,896]{1,0:T(8,128)(2,1)S(1)} %collective-permute-done.14, bf16[128,896]{1,0:T(8,128)(2,1)S(1)} %get-tuple-element.31, bf16[128,896]{1,0:T(8,128)(2,1)S(1)} %get-tuple-element.27, pred[]{:T(512)S(6)} %eq.29), kind=kLoop, calls=%fused_computation | loop fusion | flops 7798784 | bytes 1835009 | tf_op jit(solution)/shard_map/jit(_where)/select_n | solution.py:294
  70.2 1.3 %collective-permute-start.25 = (bf16[256,256]{1,0:T(8,128)(2,1)S(1)}, bf16[256,256]{1,0:T(8,128)(2,1)S(1)}, u32[]{:S(2)}, u32[]{:S(2)}) collective-permute-start(bf16[256,256]{1,0:T(8,128)(2,1)S(1)} %fusion.1), channel_id=1, source_target_pairs={{4,0},{12,8},{20,16},{28,24},{5,1},{13,9},{21,17},{29,25},{6,2},{1... | collective-permute-start | bytes 393224 | tf_op jit(solution)/shard_map/ppermute | solution.py:271
  71.5 1.1 %maximum_select_fusion.1 = bf16[128,3584]{1,0:T(8,128)(2,1)} fusion(bf16[128,896]{1,0:T(8,128)(2,1)S(1)} %collective-permute-done.17, bf16[128,896]{1,0:T(8,128)(2,1)S(1)} %collective-permute-done.16, bf16[128,896]{1,0:T(8,128)(2,1)S(1)} %get-tuple-element.35, bf16[128,896]{1,0:T(8,128)(2,1)S(1)} %get-tuple-element.34, pred[]{:T(512)S(6)} %eq.29), kind=kLoop, calls=%fused_computation.1 | loop fusion | flops 7798784 | bytes 1835009 | tf_op jit(solution)/shard_map/jit(_where)/select_n | solution.py:294
  72.6 2.9 %collective-permute-done.20 = bf16[256,256]{1,0:T(8,128)(2,1)S(1)} collective-permute-done((bf16[256,256]{1,0:T(8,128)(2,1)S(1)}, bf16[256,256]{1,0:T(8,128)(2,1)S(1)}, u32[]{:S(2)}, u32[]{:S(2)}) %collective-permute-start.20) | collective-permute-done | bytes 131104 | tf_op jit(solution)/shard_map/ppermute | solution.py:271
  75.6 0.1 fusion.4
  75.6 1.3 %collective-permute-start.21 = (bf16[256,256]{1,0:T(8,128)(2,1)S(1)}, bf16[256,256]{1,0:T(8,128)(2,1)S(1)}, u32[]{:S(2)}, u32[]{:S(2)}) collective-permute-start(bf16[256,256]{1,0:T(8,128)(2,1)S(1)} %fusion.4), channel_id=1, source_target_pairs={{8,0},{24,16},{9,1},{25,17},{10,2},{26,18},{11,3},{27,19}} | collective-permute-start | bytes 393224 | tf_op jit(solution)/shard_map/ppermute | solution.py:271
  76.9 1.1 %collective-permute-done.25 = bf16[256,256]{1,0:T(8,128)(2,1)S(1)} collective-permute-done((bf16[256,256]{1,0:T(8,128)(2,1)S(1)}, bf16[256,256]{1,0:T(8,128)(2,1)S(1)}, u32[]{:S(2)}, u32[]{:S(2)}) %collective-permute-start.25) | collective-permute-done | bytes 131104 | tf_op jit(solution)/shard_map/ppermute | solution.py:271
  78.1 0.1 fusion.5
  78.1 1.3 %collective-permute-start.26 = (bf16[256,256]{1,0:T(8,128)(2,1)S(1)}, bf16[256,256]{1,0:T(8,128)(2,1)S(1)}, u32[]{:S(2)}, u32[]{:S(2)}) collective-permute-start(bf16[256,256]{1,0:T(8,128)(2,1)S(1)} %fusion.5), channel_id=1, source_target_pairs={{8,0},{24,16},{9,1},{25,17},{10,2},{26,18},{11,3},{27,19}} | collective-permute-start | bytes 393224 | tf_op jit(solution)/shard_map/ppermute | solution.py:271
  79.4 3.1 %collective-permute-done.21 = bf16[256,256]{1,0:T(8,128)(2,1)S(1)} collective-permute-done((bf16[256,256]{1,0:T(8,128)(2,1)S(1)}, bf16[256,256]{1,0:T(8,128)(2,1)S(1)}, u32[]{:S(2)}, u32[]{:S(2)}) %collective-permute-start.21) | collective-permute-done | bytes 131104 | tf_op jit(solution)/shard_map/ppermute | solution.py:271
  82.5 0.1 fusion.2
  82.5 1.3 %collective-permute-start.22 = (bf16[256,256]{1,0:T(8,128)(2,1)S(1)}, bf16[256,256]{1,0:T(8,128)(2,1)S(1)}, u32[]{:S(2)}, u32[]{:S(2)}) collective-permute-start(bf16[256,256]{1,0:T(8,128)(2,1)S(1)} %fusion.2), channel_id=1, source_target_pairs={{16,0},{17,1},{18,2},{19,3}} | collective-permute-start | bytes 393224 | tf_op jit(solution)/shard_map/ppermute | solution.py:271
  83.8 1.4 %collective-permute-done.26 = bf16[256,256]{1,0:T(8,128)(2,1)S(1)} collective-permute-done((bf16[256,256]{1,0:T(8,128)(2,1)S(1)}, bf16[256,256]{1,0:T(8,128)(2,1)S(1)}, u32[]{:S(2)}, u32[]{:S(2)}) %collective-permute-start.26) | collective-permute-done | bytes 131104 | tf_op jit(solution)/shard_map/ppermute | solution.py:271
  85.3 0.1 fusion.3
  85.3 1.3 %collective-permute-start.27 = (bf16[256,256]{1,0:T(8,128)(2,1)S(1)}, bf16[256,256]{1,0:T(8,128)(2,1)S(1)}, u32[]{:S(2)}, u32[]{:S(2)}) collective-permute-start(bf16[256,256]{1,0:T(8,128)(2,1)S(1)} %fusion.3), channel_id=1, source_target_pairs={{16,0},{17,1},{18,2},{19,3}} | collective-permute-start | bytes 393224 | tf_op jit(solution)/shard_map/ppermute | solution.py:271
  86.7 4.1 %collective-permute-done.22 = bf16[256,256]{1,0:T(8,128)(2,1)S(1)} collective-permute-done((bf16[256,256]{1,0:T(8,128)(2,1)S(1)}, bf16[256,256]{1,0:T(8,128)(2,1)S(1)}, u32[]{:S(2)}, u32[]{:S(2)}) %collective-permute-start.22) | collective-permute-done | bytes 131104 | tf_op jit(solution)/shard_map/ppermute | solution.py:271
  90.7 0.1 add_convert_fusion.1
  90.9 0.1 collective-permute-start.28
  91.0 2.1 %collective-permute-done.27 = bf16[256,256]{1,0:T(8,128)(2,1)S(1)} collective-permute-done((bf16[256,256]{1,0:T(8,128)(2,1)S(1)}, bf16[256,256]{1,0:T(8,128)(2,1)S(1)}, u32[]{:S(2)}, u32[]{:S(2)}) %collective-permute-start.27) | collective-permute-done | bytes 131104 | tf_op jit(solution)/shard_map/ppermute | solution.py:271
  93.1 0.1 add_convert_fusion
  93.3 0.1 collective-permute-start.29
  93.4 1.2 %collective-permute-done.29 = bf16[128,256]{1,0:T(8,128)(2,1)S(1)} collective-permute-done((bf16[128,256]{1,0:T(8,128)(2,1)S(1)}, bf16[128,256]{1,0:T(8,128)(2,1)S(1)}, u32[]{:S(2)}, u32[]{:S(2)}) %collective-permute-start.29) | collective-permute-done | bytes 65568 | tf_op jit(solution)/shard_map/ppermute | solution.py:301
  94.6 0.7 maximum_select_fusion.3
  95.3 0.7 maximum_select_fusion.2
  (42 shorter events, 0.4 us)
Async XLA Ops:
  0.6 3.2 %copy-start = (bf16[128,3584]{1,0:T(8,128)(2,1)S(1)}, bf16[128,3584]{1,0:T(8,128)(2,1)}, u32[]{:S(2)}) copy-start(bf16[128,3584]{1,0:T(8,128)(2,1)} %qm.11) | copy-start | bytes 2752516
  1.7 8.4 %collective-permute-start.8 = (bf16[128,256]{1,0:T(8,128)(2,1)S(1)}, bf16[128,256]{1,0:T(8,128)(2,1)S(1)}, u32[]{:S(2)}, u32[]{:S(2)}) collective-permute-start(bf16[128,256]{1,0:T(8,128)(2,1)S(1)} %pad_maximum_fusion.3), channel_id=1, source_target_pairs={{0,1},{1,0},{2,3},{3,2},{4,5},{5,4},{6,7},{7,6},{8,9},{9,8},{10,11... | collective-permute-start | bytes 196616 | tf_op jit(solution)/shard_map/ppermute | solution.py:215
  2.2 1.9 %collective-permute-start.2 = (bf16[128,256]{1,0:T(8,128)(2,1)S(1)}, bf16[128,256]{1,0:T(8,128)(2,1)S(1)}, u32[]{:S(2)}, u32[]{:S(2)}) collective-permute-start(bf16[128,256]{1,0:T(8,128)(2,1)S(1)} %pad_maximum_fusion.2), channel_id=1, source_target_pairs={{0,1},{1,0},{2,3},{3,2},{4,5},{5,4},{6,7},{7,6},{8,9},{9,8},{10,11... | collective-permute-start | bytes 196616 | tf_op jit(solution)/shard_map/ppermute | solution.py:215
  3.4 35.8 %collective-permute-start.1 = (bf16[128,1792]{1,0:T(8,128)(2,1)S(1)}, bf16[128,1792]{1,0:T(8,128)(2,1)S(1)}, u32[]{:S(2)}, u32[]{:S(2)}) collective-permute-start(bf16[128,1792]{1,0:T(8,128)(2,1)S(1)} %constant_dynamic-slice_fusion.8), channel_id=1, source_target_pairs={{0,1},{1,0},{2,3},{3,2},{4,5},{5,4},{6,7},{7,6},{8,9},{9,8},{10,11... | collective-permute-start | bytes 1376264 | tf_op jit(solution)/shard_map/ppermute | solution.py:232
  3.9 35.2 %collective-permute-start = (bf16[128,1792]{1,0:T(8,128)(2,1)S(1)}, bf16[128,1792]{1,0:T(8,128)(2,1)S(1)}, u32[]{:S(2)}, u32[]{:S(2)}) collective-permute-start(bf16[128,1792]{1,0:T(8,128)(2,1)S(1)} %constant_dynamic-slice_fusion.9), channel_id=1, source_target_pairs={{0,1},{1,0},{2,3},{3,2},{4,5},{5,4},{6,7},{7,6},{8,9},{9,8},{10,11... | collective-permute-start | bytes 1376264 | tf_op jit(solution)/shard_map/ppermute | solution.py:231
  4.1 9.8 %collective-permute-start.4 = (bf16[256,256]{1,0:T(8,128)(2,1)S(1)}, bf16[256,256]{1,0:T(8,128)(2,1)S(1)}, u32[]{:S(2)}, u32[]{:S(2)}) collective-permute-start(bf16[256,256]{1,0:T(8,128)(2,1)S(1)} %pad_maximum_fusion.near), channel_id=1, source_target_pairs={{0,16},{1,17},{2,18},{3,19}} | collective-permute-start | bytes 393224 | tf_op jit(solution)/shard_map/ppermute | solution.py:222
  10.1 5.6 %collective-permute-start.10 = (bf16[256,256]{1,0:T(8,128)(2,1)S(1)}, bf16[256,256]{1,0:T(8,128)(2,1)S(1)}, u32[]{:S(2)}, u32[]{:S(2)}) collective-permute-start(bf16[256,256]{1,0:T(8,128)(2,1)S(1)} %pad_maximum_fusion.1.near), channel_id=1, source_target_pairs={{0,16},{1,17},{2,18},{3,19}} | collective-permute-start | bytes 393224 | tf_op jit(solution)/shard_map/ppermute | solution.py:222
  11.4 27.1 %collective-permute-start.9 = (bf16[256,256]{1,0:T(8,128)(2,1)S(1)}, bf16[256,256]{1,0:T(8,128)(2,1)S(1)}, u32[]{:S(2)}, u32[]{:S(2)}) collective-permute-start(bf16[256,256]{1,0:T(8,128)(2,1)S(1)} %pad_maximum_fusion.1.near), channel_id=1, source_target_pairs={{0,2},{1,3},{2,0},{3,1},{4,6},{5,7},{6,4},{7,5},{8,10},{9,11},{10,... | collective-permute-start | bytes 393224 | tf_op jit(solution)/shard_map/ppermute | solution.py:228
  13.9 27.6 %collective-permute-start.3 = (bf16[256,256]{1,0:T(8,128)(2,1)S(1)}, bf16[256,256]{1,0:T(8,128)(2,1)S(1)}, u32[]{:S(2)}, u32[]{:S(2)}) collective-permute-start(bf16[256,256]{1,0:T(8,128)(2,1)S(1)} %pad_maximum_fusion.near), channel_id=1, source_target_pairs={{0,2},{1,3},{2,0},{3,1},{4,6},{5,7},{6,4},{7,5},{8,10},{9,11},{10,... | collective-permute-start | bytes 393224 | tf_op jit(solution)/shard_map/ppermute | solution.py:228
  15.4 23.8 %copy-start.1 = (bf16[128,3584]{1,0:T(8,128)(2,1)S(1)}, bf16[128,3584]{1,0:T(8,128)(2,1)}, u32[]{:S(2)}) copy-start(bf16[128,3584]{1,0:T(8,128)(2,1)} %cm.11) | copy-start | bytes 2752516
  15.4 23.8 %copy-start.2 = (s32[4,4]{1,0:T(4,128)S(1)}, s32[4,4]{1,0:T(4,128)}, u32[]{:S(2)}) copy-start(s32[4,4]{1,0:T(4,128)} %tree.11) | copy-start | bytes 196
  15.8 3.8 %collective-permute-start.5 = (bf16[256,256]{1,0:T(8,128)(2,1)S(1)}, bf16[256,256]{1,0:T(8,128)(2,1)S(1)}, u32[]{:S(2)}, u32[]{:S(2)}) collective-permute-start(bf16[256,256]{1,0:T(8,128)(2,1)S(1)} %broadcast_select_fusion.1), channel_id=1, source_target_pairs={{0,8},{16,24},{1,9},{17,25},{2,10},{18,26},{3,11},{19,27}} | collective-permute-start | bytes 393224 | tf_op jit(solution)/shard_map/ppermute | solution.py:222
  19.5 6.8 %collective-permute-start.11 = (bf16[256,256]{1,0:T(8,128)(2,1)S(1)}, bf16[256,256]{1,0:T(8,128)(2,1)S(1)}, u32[]{:S(2)}, u32[]{:S(2)}) collective-permute-start(bf16[256,256]{1,0:T(8,128)(2,1)S(1)} %broadcast_select_fusion), channel_id=1, source_target_pairs={{0,8},{16,24},{1,9},{17,25},{2,10},{18,26},{3,11},{19,27}} | collective-permute-start | bytes 393224 | tf_op jit(solution)/shard_map/ppermute | solution.py:222
  26.4 3.8 %collective-permute-start.6 = (bf16[256,256]{1,0:T(8,128)(2,1)S(1)}, bf16[256,256]{1,0:T(8,128)(2,1)S(1)}, u32[]{:S(2)}, u32[]{:S(2)}) collective-permute-start(bf16[256,256]{1,0:T(8,128)(2,1)S(1)} %broadcast_select_fusion.3), channel_id=1, source_target_pairs={{0,4},{8,12},{16,20},{24,28},{1,5},{9,13},{17,21},{25,29},{2,6},{1... | collective-permute-start | bytes 393224 | tf_op jit(solution)/shard_map/ppermute | solution.py:222
  30.2 6.8 %collective-permute-start.12 = (bf16[256,256]{1,0:T(8,128)(2,1)S(1)}, bf16[256,256]{1,0:T(8,128)(2,1)S(1)}, u32[]{:S(2)}, u32[]{:S(2)}) collective-permute-start(bf16[256,256]{1,0:T(8,128)(2,1)S(1)} %broadcast_select_fusion.2), channel_id=1, source_target_pairs={{0,4},{8,12},{16,20},{24,28},{1,5},{9,13},{17,21},{25,29},{2,6},{1... | collective-permute-start | bytes 393224 | tf_op jit(solution)/shard_map/ppermute | solution.py:222
  37.0 6.8 %collective-permute-start.7 = (bf16[256,256]{1,0:T(8,128)(2,1)S(1)}, bf16[256,256]{1,0:T(8,128)(2,1)S(1)}, u32[]{:S(2)}, u32[]{:S(2)}) collective-permute-start(bf16[256,256]{1,0:T(8,128)(2,1)S(1)} %broadcast_select_fusion.5.near), channel_id=1, source_target_pairs={{0,2},{1,3},{2,0},{3,1},{4,6},{5,7},{6,4},{7,5},{8,10},{9,11},{10,... | collective-permute-start | bytes 393224 | tf_op jit(solution)/shard_map/ppermute | solution.py:226
  38.6 16.6 %collective-permute-start.13 = (bf16[256,256]{1,0:T(8,128)(2,1)S(1)}, bf16[256,256]{1,0:T(8,128)(2,1)S(1)}, u32[]{:S(2)}, u32[]{:S(2)}) collective-permute-start(bf16[256,256]{1,0:T(8,128)(2,1)S(1)} %broadcast_select_fusion.4.near), channel_id=1, source_target_pairs={{0,2},{1,3},{2,0},{3,1},{4,6},{5,7},{6,4},{7,5},{8,10},{9,11},{10,... | collective-permute-start | bytes 393224 | tf_op jit(solution)/shard_map/ppermute | solution.py:226
  49.1 16.4 %collective-permute-start.19 = (bf16[256,256]{1,0:T(8,128)(2,1)S(1)}, bf16[256,256]{1,0:T(8,128)(2,1)S(1)}, u32[]{:S(2)}, u32[]{:S(2)}) collective-permute-start(bf16[256,256]{1,0:T(8,128)(2,1)S(1)} %slice.49), channel_id=1, source_target_pairs={{0,2},{1,3},{2,0},{3,1},{4,6},{5,7},{6,4},{7,5},{8,10},{9,11},{10,... | collective-permute-start | bytes 393224 | tf_op jit(solution)/shard_map/ppermute | solution.py:266
  54.0 32.6 %collective-permute-start.18 = (bf16[256,256]{1,0:T(8,128)(2,1)S(1)}, bf16[256,256]{1,0:T(8,128)(2,1)S(1)}, u32[]{:S(2)}, u32[]{:S(2)}) collective-permute-start(bf16[256,256]{1,0:T(8,128)(2,1)S(1)} %get-tuple-element.39), channel_id=1, source_target_pairs={{0,2},{1,3},{2,0},{3,1},{4,6},{5,7},{6,4},{7,5},{8,10},{9,11},{10,... | collective-permute-start | bytes 393224 | tf_op jit(solution)/shard_map/ppermute | solution.py:289
  54.6 11.7 %collective-permute-start.14 = (bf16[128,896]{1,0:T(8,128)(2,1)S(1)}, bf16[128,896]{1,0:T(8,128)(2,1)S(1)}, u32[]{:S(2)}, u32[]{:S(2)}) collective-permute-start(bf16[128,896]{1,0:T(8,128)(2,1)S(1)} %get-tuple-element.32), channel_id=1, source_target_pairs={{0,1},{1,0},{2,3},{3,2},{4,5},{5,4},{6,7},{7,6},{8,9},{9,8},{10,11... | collective-permute-start | bytes 688136 | tf_op jit(solution)/shard_map/ppermute | solution.py:301
  54.6 15.5 %collective-permute-start.16 = (bf16[128,896]{1,0:T(8,128)(2,1)S(1)}, bf16[128,896]{1,0:T(8,128)(2,1)S(1)}, u32[]{:S(2)}, u32[]{:S(2)}) collective-permute-start(bf16[128,896]{1,0:T(8,128)(2,1)S(1)} %get-tuple-element.36), channel_id=1, source_target_pairs={{0,1},{1,0},{2,3},{3,2},{4,5},{5,4},{6,7},{7,6},{8,9},{9,8},{10,11... | collective-permute-start | bytes 688136 | tf_op jit(solution)/shard_map/ppermute | solution.py:301
  60.6 5.6 %collective-permute-start.24 = (bf16[256,256]{1,0:T(8,128)(2,1)S(1)}, bf16[256,256]{1,0:T(8,128)(2,1)S(1)}, u32[]{:S(2)}, u32[]{:S(2)}) collective-permute-start(bf16[256,256]{1,0:T(8,128)(2,1)S(1)} %slice.52), channel_id=1, source_target_pairs={{0,2},{1,3},{2,0},{3,1},{4,6},{5,7},{6,4},{7,5},{8,10},{9,11},{10,... | collective-permute-start | bytes 393224 | tf_op jit(solution)/shard_map/ppermute | solution.py:266
  65.5 25.4 %collective-permute-start.23 = (bf16[256,256]{1,0:T(8,128)(2,1)S(1)}, bf16[256,256]{1,0:T(8,128)(2,1)S(1)}, u32[]{:S(2)}, u32[]{:S(2)}) collective-permute-start(bf16[256,256]{1,0:T(8,128)(2,1)S(1)} %get-tuple-element.42), channel_id=1, source_target_pairs={{0,2},{1,3},{2,0},{3,1},{4,6},{5,7},{6,4},{7,5},{8,10},{9,11},{10,... | collective-permute-start | bytes 393224 | tf_op jit(solution)/shard_map/ppermute | solution.py:289
  66.2 1.6 %collective-permute-start.15 = (bf16[128,896]{1,0:T(8,128)(2,1)S(1)}, bf16[128,896]{1,0:T(8,128)(2,1)S(1)}, u32[]{:S(2)}, u32[]{:S(2)}) collective-permute-start(bf16[128,896]{1,0:T(8,128)(2,1)S(1)} %get-tuple-element.33), channel_id=1, source_target_pairs={{0,1},{1,0},{2,3},{3,2},{4,5},{5,4},{6,7},{7,6},{8,9},{9,8},{10,11... | collective-permute-start | bytes 688136 | tf_op jit(solution)/shard_map/ppermute | solution.py:301
  66.3 5.1 %collective-permute-start.17 = (bf16[128,896]{1,0:T(8,128)(2,1)S(1)}, bf16[128,896]{1,0:T(8,128)(2,1)S(1)}, u32[]{:S(2)}, u32[]{:S(2)}) collective-permute-start(bf16[128,896]{1,0:T(8,128)(2,1)S(1)} %get-tuple-element.37), channel_id=1, source_target_pairs={{0,1},{1,0},{2,3},{3,2},{4,5},{5,4},{6,7},{7,6},{8,9},{9,8},{10,11... | collective-permute-start | bytes 688136 | tf_op jit(solution)/shard_map/ppermute | solution.py:301
  67.7 7.8 %collective-permute-start.20 = (bf16[256,256]{1,0:T(8,128)(2,1)S(1)}, bf16[256,256]{1,0:T(8,128)(2,1)S(1)}, u32[]{:S(2)}, u32[]{:S(2)}) collective-permute-start(bf16[256,256]{1,0:T(8,128)(2,1)S(1)} %fusion), channel_id=1, source_target_pairs={{4,0},{12,8},{20,16},{28,24},{5,1},{13,9},{21,17},{29,25},{6,2},{1... | collective-permute-start | bytes 393224 | tf_op jit(solution)/shard_map/ppermute | solution.py:271
  70.2 7.9 %collective-permute-start.25 = (bf16[256,256]{1,0:T(8,128)(2,1)S(1)}, bf16[256,256]{1,0:T(8,128)(2,1)S(1)}, u32[]{:S(2)}, u32[]{:S(2)}) collective-permute-start(bf16[256,256]{1,0:T(8,128)(2,1)S(1)} %fusion.1), channel_id=1, source_target_pairs={{4,0},{12,8},{20,16},{28,24},{5,1},{13,9},{21,17},{29,25},{6,2},{1... | collective-permute-start | bytes 393224 | tf_op jit(solution)/shard_map/ppermute | solution.py:271
  75.6 6.9 %collective-permute-start.21 = (bf16[256,256]{1,0:T(8,128)(2,1)S(1)}, bf16[256,256]{1,0:T(8,128)(2,1)S(1)}, u32[]{:S(2)}, u32[]{:S(2)}) collective-permute-start(bf16[256,256]{1,0:T(8,128)(2,1)S(1)} %fusion.4), channel_id=1, source_target_pairs={{8,0},{24,16},{9,1},{25,17},{10,2},{26,18},{11,3},{27,19}} | collective-permute-start | bytes 393224 | tf_op jit(solution)/shard_map/ppermute | solution.py:271
  78.1 7.2 %collective-permute-start.26 = (bf16[256,256]{1,0:T(8,128)(2,1)S(1)}, bf16[256,256]{1,0:T(8,128)(2,1)S(1)}, u32[]{:S(2)}, u32[]{:S(2)}) collective-permute-start(bf16[256,256]{1,0:T(8,128)(2,1)S(1)} %fusion.5), channel_id=1, source_target_pairs={{8,0},{24,16},{9,1},{25,17},{10,2},{26,18},{11,3},{27,19}} | collective-permute-start | bytes 393224 | tf_op jit(solution)/shard_map/ppermute | solution.py:271
  82.5 8.2 %collective-permute-start.22 = (bf16[256,256]{1,0:T(8,128)(2,1)S(1)}, bf16[256,256]{1,0:T(8,128)(2,1)S(1)}, u32[]{:S(2)}, u32[]{:S(2)}) collective-permute-start(bf16[256,256]{1,0:T(8,128)(2,1)S(1)} %fusion.2), channel_id=1, source_target_pairs={{16,0},{17,1},{18,2},{19,3}} | collective-permute-start | bytes 393224 | tf_op jit(solution)/shard_map/ppermute | solution.py:271
  85.3 7.8 %collective-permute-start.27 = (bf16[256,256]{1,0:T(8,128)(2,1)S(1)}, bf16[256,256]{1,0:T(8,128)(2,1)S(1)}, u32[]{:S(2)}, u32[]{:S(2)}) collective-permute-start(bf16[256,256]{1,0:T(8,128)(2,1)S(1)} %fusion.3), channel_id=1, source_target_pairs={{16,0},{17,1},{18,2},{19,3}} | collective-permute-start | bytes 393224 | tf_op jit(solution)/shard_map/ppermute | solution.py:271
  90.9 2.5 %collective-permute-start.28 = (bf16[128,256]{1,0:T(8,128)(2,1)S(1)}, bf16[128,256]{1,0:T(8,128)(2,1)S(1)}, u32[]{:S(2)}, u32[]{:S(2)}) collective-permute-start(bf16[128,256]{1,0:T(8,128)(2,1)S(1)} %slice.64), channel_id=1, source_target_pairs={{0,1},{1,0},{2,3},{3,2},{4,5},{5,4},{6,7},{7,6},{8,9},{9,8},{10,11... | collective-permute-start | bytes 196616 | tf_op jit(solution)/shard_map/ppermute | solution.py:301
  93.3 1.3 %collective-permute-start.29 = (bf16[128,256]{1,0:T(8,128)(2,1)S(1)}, bf16[128,256]{1,0:T(8,128)(2,1)S(1)}, u32[]{:S(2)}, u32[]{:S(2)}) collective-permute-start(bf16[128,256]{1,0:T(8,128)(2,1)S(1)} %slice.66), channel_id=1, source_target_pairs={{0,1},{1,0},{2,3},{3,2},{4,5},{5,4},{6,7},{7,6},{8,9},{9,8},{10,11... | collective-permute-start | bytes 196616 | tf_op jit(solution)/shard_map/ppermute | solution.py:301

commit v2 on v1

v2 whole, which is shorter than its diff:
```python
import functools
import math

import jax
import jax.numpy as jnp
from jax import lax
from jax.experimental import pallas as pl
from jax.experimental.pallas import tpu as pltpu
from jax.sharding import PartitionSpec as P

QUERY_HEADS = 28
KEY_VALUE_HEADS = 4
HEAD_SIZE = 128
GROUP = QUERY_HEADS // KEY_VALUE_HEADS
WIDTH = GROUP * HEAD_SIZE
SCALE = HEAD_SIZE ** (-0.5)
EXP2_SCALE = SCALE * math.log2(math.e)
MASKED = -1e30
VMEM_BYTES = 24 * 1024 * 1024


def dot_nt(a, b):
    return lax.dot_general(a, b, (((1,), (1,)), ((), ())), preferred_element_type=jnp.float32)


def dot_nn(a, b):
    return lax.dot_general(a, b, (((1,), (0,)), ((), ())), preferred_element_type=jnp.float32)


def head_rows(mine, sibling, g):
    columns = slice(g * HEAD_SIZE, (g + 1) * HEAD_SIZE)
    return jnp.concatenate([mine[:, columns], sibling[:, columns]], axis=0)


def causal_mask(scores, rows, h):
    lane = lax.broadcasted_iota(jnp.int32, (rows, rows), 1)
    sub = lax.broadcasted_iota(jnp.int32, (rows, rows), 0)
    ahead = lane - sub
    out = []
    for b in range(scores.shape[0] // rows):
        line = []
        for a in range(2):
            offset = ((h ^ b) - (h ^ a)) * rows
            tile = scores[b * rows : (b + 1) * rows, a * rows : (a + 1) * rows]
            line.append(jnp.where(ahead >= offset, tile, MASKED))
        out.append(jnp.concatenate(line, axis=1))
    return jnp.concatenate(out, axis=0)


def prompt_mask(scores, rows, h, s, tree_ref):
    lane = lax.broadcasted_iota(jnp.int32, (1, 2 * rows), 1)
    out = []
    for b in range(scores.shape[0] // rows):
        reads = [jnp.logical_and(tree_ref[h ^ a, h ^ b] > 0, s > 0) for a in range(2)]
        bias = [jnp.where(r, jnp.float32(0.0), jnp.float32(MASKED)) for r in reads]
        row = jnp.where(lane < rows, bias[0], bias[1])
        out.append(scores[b * rows : (b + 1) * rows] + row)
    return jnp.concatenate(out, axis=0)


def stats_kernel(ids, tree, qm, qs, cm, cs, near, far, stats):
    h = ids[0]
    rows = qm.shape[0]
    keys = jnp.concatenate([near[0, :, :HEAD_SIZE], far[0, :, :HEAD_SIZE]], axis=0)
    values = jnp.concatenate([near[0, :, HEAD_SIZE:], far[0, :, HEAD_SIZE:]], axis=0)
    for g in range(GROUP):
        q = head_rows(qm, qs, g)
        ct = head_rows(cm, cs, g)
        scores = causal_mask(dot_nt(keys, q), rows, h)
        top = jnp.max(scores, axis=0, keepdims=True)
        e = jnp.exp2((scores - top) * EXP2_SCALE)
        dprob = dot_nt(values, ct)
        stats[0, g, 0:1, :] = top
        stats[0, g, 1:2, :] = jnp.sum(e, axis=0, keepdims=True)
        stats[0, g, 2:3, :] = jnp.sum(e * dprob, axis=0, keepdims=True)


def prompt_kernel(ids, tree, qm, qs, cm, cs, near, far, own, stats, att, dq, terms, key_sum, value_sum):
    h = ids[0]
    s = ids[1]
    rows = qm.shape[0]
    keys = jnp.concatenate([near[0, :, :HEAD_SIZE], far[0, :, :HEAD_SIZE]], axis=0)
    values = jnp.concatenate([near[0, :, HEAD_SIZE:], far[0, :, HEAD_SIZE:]], axis=0)
    keys_t = keys.T
    values_t = values.T
    for g in range(GROUP):
        q = head_rows(qm, qs, g)
        ct = head_rows(cm, cs, g)
        scores = prompt_mask(dot_nt(keys, q), rows, h, s, tree)
        own_top = own[0, g, 0:1, :]
        top = jnp.maximum(own_top, jnp.max(scores, axis=0, keepdims=True))
        e = jnp.exp2((scores - top) * EXP2_SCALE)
        keep = jnp.exp2((own_top - top) * EXP2_SCALE)
        dprob = dot_nt(values, ct)
        inverse = 1.0 / (own[0, g, 1:2, :] * keep + jnp.sum(e, axis=0, keepdims=True))
        delta = (own[0, g, 2:3, :] * keep + jnp.sum(e * dprob, axis=0, keepdims=True)) * inverse
        probs = e * inverse
        rounded = probs.astype(jnp.bfloat16)
        dscore = (probs * (dprob - delta)).astype(jnp.bfloat16)
        stats[0, g, 0:1, :] = top
        stats[0, g, 1:2, :] = inverse
        stats[0, g, 2:3, :] = delta
        value_term = dot_nn(rounded, ct)
        key_term = dot_nn(dscore, q)
        if g == 0:
            value_sum[...] = value_term
            key_sum[...] = key_term
        else:
            value_sum[...] += value_term
            key_sum[...] += key_term
        att[0, g] = dot_nn(values_t, rounded)
        dq[0, g] = dot_nn(keys_t, dscore)
    terms[0, :, :HEAD_SIZE] = (key_sum[...] * SCALE).astype(terms.dtype)
    terms[0, :, HEAD_SIZE:] = value_sum[...].astype(terms.dtype)


def own_kernel(
    ids, tree, qm, qs, cm, cs, near, far, stats, att_p, dq_p,
    att_m, att_s, dq_m, dq_s, terms_near, terms_far, key_sum, value_sum,
):
    h = ids[0]
    rows = qm.shape[0]
    keys = jnp.concatenate([near[0, :, :HEAD_SIZE], far[0, :, :HEAD_SIZE]], axis=0)
    values = jnp.concatenate([near[0, :, HEAD_SIZE:], far[0, :, HEAD_SIZE:]], axis=0)
    keys_t = keys.T
    values_t = values.T
    for g in range(GROUP):
        columns = slice(g * HEAD_SIZE, (g + 1) * HEAD_SIZE)
        q = head_rows(qm, qs, g)
        ct = head_rows(cm, cs, g)
        scores = causal_mask(dot_nt(keys, q), rows, h)
        probs = jnp.exp2((scores - stats[0, g, 0:1, :]) * EXP2_SCALE) * stats[0, g, 1:2, :]
        dprob = dot_nt(values, ct)
        rounded = probs.astype(jnp.bfloat16)
        dscore = (probs * (dprob - stats[0, g, 2:3, :])).astype(jnp.bfloat16)
        value_term = dot_nn(rounded, ct)
        key_term = dot_nn(dscore, q)
        if g == 0:
            value_sum[...] = value_term
            key_sum[...] = key_term
        else:
            value_sum[...] += value_term
            key_sum[...] += key_term
        att = (att_p[0, g] + dot_nn(values_t, rounded)).T.astype(jnp.bfloat16)
        dq = ((dq_p[0, g] + dot_nn(keys_t, dscore)) * SCALE).T.astype(jnp.bfloat16)
        att_m[:, columns] = att[:rows]
        att_s[:, columns] = att[rows:]
        dq_m[:, columns] = dq[:rows]
        dq_s[:, columns] = dq[rows:]
    half = terms_near.shape[1]
    for out, part in ((terms_near, slice(0, half)), (terms_far, slice(half, 2 * half))):
        out[0, :, :HEAD_SIZE] = (key_sum[part, :] * SCALE).astype(out.dtype)
        out[0, :, HEAD_SIZE:] = value_sum[part, :].astype(out.dtype)


def per_head(shape):
    return pl.BlockSpec((1, *shape[1:]), lambda j, *refs: (j,) + (0,) * (len(shape) - 1))


def at_head(j, shape):
    return pl.BlockSpec((1, *shape[1:]), lambda i, *refs: (j,) + (0,) * (len(shape) - 1))


def full(shape):
    return pl.BlockSpec(shape, lambda i, *refs: (0,) * len(shape))


def call(kernel, j, scalars, heads, inputs, outs, scratch, products):
    queries, q_sib, cotangent, c_sib = heads
    rows = queries.shape[0]
    steps = q_sib.shape[1] // WIDTH
    mine = pl.BlockSpec(
        (rows, WIDTH), lambda i, ids, tree: (0, steps * (ids[0] & 1) + (i if j is None else j))
    )
    sib = pl.BlockSpec((rows, WIDTH), lambda i, *refs: (0, i if j is None else j))
    specs = [mine, sib, mine, sib]
    for x, per in inputs:
        if not per:
            specs.append(full(x.shape))
        elif j is None:
            specs.append(per_head(x.shape))
        else:
            specs.append(at_head(j, x.shape))
    out_specs = []
    for o in outs:
        if len(o.shape) == 2:
            out_specs.append(pl.BlockSpec((rows, WIDTH), lambda i, *refs: (0, i)))
        elif j is None:
            out_specs.append(per_head(o.shape))
        else:
            out_specs.append(full(o.shape))
    count = steps if j is None else 1
    flops = count * 2 * products * (2 * rows * GROUP) * (4 * rows) * HEAD_SIZE
    return pl.pallas_call(
        kernel,
        grid_spec=pltpu.PrefetchScalarGridSpec(
            num_scalar_prefetch=2,
            grid=(count,),
            in_specs=specs,
            out_specs=out_specs,
            scratch_shapes=scratch,
        ),
        out_shape=outs,
        compiler_params=pltpu.CompilerParams(vmem_limit_bytes=VMEM_BYTES),
        cost_estimate=pl.CostEstimate(
            flops=flops, bytes_accessed=count * 4 * 2 * rows * WIDTH * 2, transcendentals=0
        ),
    )(*scalars, *heads, *[x for x, _ in inputs])


def on_device(seq_count, head_count, queries, rotated_key_rows, value_matrix, cotangent, tree_mask):
    s = lax.axis_index("seq")
    h = lax.axis_index("head")
    rows = queries.shape[0]
    heads = KEY_VALUE_HEADS // 2
    core = h & 1
    pair = [(i, i ^ 1) for i in range(head_count)]
    cross = [(i, i ^ 2) for i in range(head_count)]
    scalars = (jnp.stack([h, s]).astype(jnp.int32), tree_mask)
    f32, bf16 = jnp.float32, jnp.bfloat16

    def columns(x, place, width):
        return lax.dynamic_slice_in_dim(x, place * width, width, 1)

    def half(place):
        k = columns(rotated_key_rows, place, heads * HEAD_SIZE).reshape(rows, heads, 1, HEAD_SIZE)
        v = columns(value_matrix, place, heads * HEAD_SIZE).reshape(rows, heads, 1, HEAD_SIZE)
        kv = jnp.concatenate([k, v], axis=2).reshape(rows, heads, 2 * HEAD_SIZE)
        return jnp.transpose(kv, (1, 0, 2))

    near = jnp.concatenate([half(core), lax.ppermute(half(1 - core), "head", pair)], axis=1)
    held, hops = near, []
    step = seq_count // 2
    while step:
        sends = [(i, i + step) for i in range(0, seq_count, 2 * step)]
        got = lax.ppermute(held, "seq", sends)
        held = jnp.where(s % (2 * step) == step, got, held)
        hops.append(held)
        step //= 2
    prompt_near = held
    prompt_far = [lax.ppermute(held[j : j + 1], "head", cross) for j in range(heads)]

    _, near_later = lax.optimization_barrier((hops[0], near))
    far = lax.ppermute(near_later, "head", cross)
    _, q_in, c_in = lax.optimization_barrier((hops[0], queries, cotangent))
    q_sib = lax.ppermute(columns(q_in, 1 - core, heads * WIDTH), "head", pair)
    c_sib = lax.ppermute(columns(c_in, 1 - core, heads * WIDTH), "head", pair)
    work = (queries, q_sib, cotangent, c_sib)

    shape = jax.ShapeDtypeStruct
    sums = [pltpu.VMEM((4 * rows, HEAD_SIZE), f32)] * 2

    def stats_shape(n):
        return shape((n, GROUP, 8, 2 * rows), f32)

    def part_shape(n):
        return shape((n, GROUP, HEAD_SIZE, 2 * rows), f32)

    own = call(
        stats_kernel, None, scalars, work, [(near, 1), (far, 1)], [stats_shape(heads)], [], 2
    )[0]
    mids, prompt_sums = [], []
    for j in range(heads):
        mid = call(
            prompt_kernel,
            j,
            scalars,
            work,
            [(prompt_near, 1), (prompt_far[j], 0), (own, 1)],
            [
                stats_shape(1),
                part_shape(1),
                part_shape(1),
                shape((1, 4 * rows, 2 * HEAD_SIZE), bf16),
            ],
            sums,
            6,
        )
        got = lax.ppermute(mid[3][0, 2 * rows :], "head", cross)
        mids.append(mid[:3])
        prompt_sums.append(mid[3][0, : 2 * rows].astype(f32) + got.astype(f32))
    total = jnp.stack(prompt_sums)
    step = 1
    while step < seq_count:
        sends = [(i + step, i) for i in range(0, seq_count, 2 * step)]
        total = total + lax.ppermute(total.astype(bf16), "seq", sends).astype(f32)
        step *= 2

    stats, att_p, dq_p = [jnp.concatenate(x, axis=0) for x in zip(*mids)]
    rows_shape = shape((rows, heads * WIDTH), bf16)
    att_m, att_s, dq_m, dq_s, t_near, t_far = call(
        own_kernel,
        None,
        scalars,
        work,
        [(x, 1) for x in (near, far, stats, att_p, dq_p)],
        [rows_shape] * 4
        + [
            shape((heads, 2 * rows, 2 * HEAD_SIZE), f32),
            shape((heads, 2 * rows, 2 * HEAD_SIZE), bf16),
        ],
        sums,
        6,
    )
    own_sums = t_near + lax.ppermute(t_far, "head", cross).astype(f32)

    def both_halves(mine, theirs):
        return jnp.where(
            core == 0,
            jnp.concatenate([mine, theirs], axis=1),
            jnp.concatenate([theirs, mine], axis=1),
        )

    attention = both_halves(att_m, lax.ppermute(att_s, "head", pair))
    query_grad = both_halves(dq_m, lax.ppermute(dq_s, "head", pair))
    total = (own_sums + jnp.where(s == 0, total, jnp.float32(0.0))).astype(bf16)
    mine, theirs = total[:, :rows], lax.ppermute(total[:, rows:], "head", pair)

    def gradient(part):
        return both_halves(
            jnp.concatenate([mine[j, :, part] for j in range(heads)], axis=1),
            jnp.concatenate([theirs[j, :, part] for j in range(heads)], axis=1),
        )

    return (
        attention,
        query_grad,
        gradient(slice(0, HEAD_SIZE)),
        gradient(slice(HEAD_SIZE, 2 * HEAD_SIZE)),
    )


def solution(mesh):
    spec = P(("seq", "head"), None)
    return jax.shard_map(
        functools.partial(on_device, mesh.shape["seq"], mesh.shape["head"]),
        mesh=mesh,
        in_specs=(spec, spec, spec, spec, P("seq", None)),
        out_specs=(spec, spec, spec, spec),
        check_vma=False,
    )
```

time: 96.4 us -> 94.6 us (0.981)
  starting transfers between devices: 38.2 us -> 22.5 us
  waiting for transfers between devices: 28 us -> 37 us
  other arithmetic: 4.5 us -> 8.46 us
  local copies, waits for them, and re-layouts: 2.14 us -> 3.53 us
    ppermute x6 -> x3, starting transfers between devices: 18.5 us -> 8.48 us  [on_device(): got = lax.ppermute(held, 'seq', sends)]
    ppermute x24 -> x15, waiting for transfers between devices: 16.9 us -> 23.5 us  [the longest x3 15.2 us: on_device(): total = total + lax.ppermute(total.astype(bf16), 'seq', sends).astype(f32)]
    ppermute x24 -> x15, starting transfers between devices: 19.7 us -> 14 us  [the longest x3 4.05 us: on_device(): total = total + lax.ppermute(total.astype(bf16), 'seq', sends).astype(f32)]
    convert_element_type x8 -> x4, other arithmetic: 0.58 us -> 4.11 us  [the longest x3 2.97 us: on_device(): total = total + lax.ppermute(total.astype(bf16), 'seq', sends).astype(f32)]
    ppermute x6 -> x3, waiting for transfers between devices: 11.1 us -> 13.5 us  [on_device(): got = lax.ppermute(held, 'seq', sends)]
    unnamed x6 -> x22, local copies, waits for them, and re-layouts: 0.02 us -> 1.96 us
    dynamic_slice x3, local copies, waits for them, and re-layouts: 2.06 us -> 1.04 us  [columns(): return lax.dynamic_slice_in_dim(x, place * width, width, 1)]
    pallas_call x6 -> x4, Pallas kernels: 22 us -> 21.7 us  [call(): pl.pallas_call(kernel, grid_spec=pltpu.PrefetchScalarGridSpec(num_scalar_...]
  transfers between devices with their start and end apart: 30 -> 18, of which waited for: 14 -> 9; matrix products, arithmetic and copies ran while one was open for 4% -> 6% of each run, Pallas kernels for 23% -> 23%
where the time goes in v2:
time: 94.6 us; the launch traced here: 94.2 us
  waiting for transfers between devices  37 us (39%)
  starting transfers between devices  22.5 us (24%)
  Pallas kernels  21.7 us (23%)
  other arithmetic  8.46 us (9%)
  local copies, waits for them, and re-layouts  3.53 us (4%)
  between operations  1.04 us (1%)
    pallas_call x4, Pallas kernels, call(): pl.pallas_call(kernel, grid_spec=pltpu.PrefetchScalarGridSpec(num_scalar_...  21.7 us
    ppermute x3, waiting for transfers between devices, on_device(): total = total + lax.ppermute(total.astype(bf16), 'seq', sends).astype(f32)  15.2 us
    ppermute x3, waiting for transfers between devices, on_device(): got = lax.ppermute(held, 'seq', sends)  13.5 us
    ppermute x3, starting transfers between devices, on_device(): got = lax.ppermute(held, 'seq', sends)  8.48 us
    ppermute x3, starting transfers between devices, on_device(): total = total + lax.ppermute(total.astype(bf16), 'seq', sends).astype(f32)  4.05 us
    select_n x4, other arithmetic, both_halves(): jnp.where(core == 0, jnp.concatenate([mine, theirs], axis=1), jnp.concate...  3.64 us
    ppermute x1, waiting for transfers between devices, on_device(): far = lax.ppermute(near_later, 'head', cross)  3.53 us
    ppermute x2, starting transfers between devices, on_device(): lax.ppermute(held[j:j + 1], 'head', cross)  3.11 us
  transfers between devices with their start and end apart: 18, of which 9 were waited for; matrix products, arithmetic and copies ran while one was open for 6% of the time, Pallas kernels for 23%

profile of v2, /device:TPU:0, one launch (start us, length us, event | category | flops | bytes accessed | tf_op | source)
XLA Modules:
  0.0 94.2 jit_solution(16983883611131761155)
XLA Ops:
  0.6 1.0 %constant_dynamic-slice_fusion.4 = (bf16[128,256]{1,0:T(8,128)(2,1)S(1)}, bf16[128,256]{1,0:T(8,128)(2,1)S(1)}, bf16[128,256]{1,0:T(8,128)(2,1)S(1)}, bf16[128,256]{1,0:T(8,128)(2,1)S(1)}) fusion(bf16[128,512]{1,0:T(8,128)(2,1)} %param.7, s32[]{:T(128)S(6)} %select_n.82, s32[]{:T(128)S(6)} %select_n.83, bf16[128,512]{1,0:T(8,128)(2,1)} %param.6), kind=kLoop, calls=%fused_computation.38 | loop fusion | bytes 524296 | tf_op jit(solution)/shard_map/dynamic_slice | solution.py:223
  1.6 0.1 copy.18
  1.7 0.1 copy.17
  1.9 0.0 copy-start
  1.9 0.1 copy.14
  2.0 0.1 reshape.35
  2.1 0.5 collective-permute-start
  2.6 0.1 copy.16
  2.7 0.1 copy.15
  2.9 0.0 copy-start.1
  2.9 0.1 copy.11
  3.0 0.1 reshape.32
  3.1 0.5 collective-permute-done
  3.6 5.9 %collective-permute-start.1 = (bf16[2,256,256]{2,1,0:T(8,128)(2,1)S(1)}, bf16[2,256,256]{2,1,0:T(8,128)(2,1)S(1)}, u32[]{:S(2)}, u32[]{:S(2)}) collective-permute-start(bf16[2,256,256]{2,1,0:T(8,128)(2,1)S(1)} %pad_maximum_fusion.3.near), channel_id=1, source_target_pairs={{0,16},{1,17},{2,18},{3,19}} | collective-permute-start | bytes 786440 | tf_op jit(solution)/shard_map/ppermute | solution.py:236
  9.5 5.8 %collective-permute-done.1 = bf16[2,256,256]{2,1,0:T(8,128)(2,1)S(1)} collective-permute-done((bf16[2,256,256]{2,1,0:T(8,128)(2,1)S(1)}, bf16[2,256,256]{2,1,0:T(8,128)(2,1)S(1)}, u32[]{:S(2)}, u32[]{:S(2)}) %collective-permute-start.1) | collective-permute-done | bytes 262176 | tf_op jit(solution)/shard_map/ppermute | solution.py:236
  15.4 0.1 broadcast_select_fusion.2
  15.4 1.3 %collective-permute-start.5 = (bf16[2,256,256]{2,1,0:T(8,128)(2,1)S(1)}, bf16[2,256,256]{2,1,0:T(8,128)(2,1)S(1)}, u32[]{:S(2)}, u32[]{:S(2)}) collective-permute-start(bf16[2,256,256]{2,1,0:T(8,128)(2,1)S(1)} %broadcast_select_fusion.2), channel_id=1, source_target_pairs={{0,8},{16,24},{1,9},{17,25},{2,10},{18,26},{3,11},{19,27}} | collective-permute-start | bytes 786440 | tf_op jit(solution)/shard_map/ppermute | solution.py:236
  16.8 0.0 copy-start.4
  16.8 5.3 %collective-permute-done.5 = bf16[2,256,256]{2,1,0:T(8,128)(2,1)S(1)} collective-permute-done((bf16[2,256,256]{2,1,0:T(8,128)(2,1)S(1)}, bf16[2,256,256]{2,1,0:T(8,128)(2,1)S(1)}, u32[]{:S(2)}, u32[]{:S(2)}) %collective-permute-start.5) | collective-permute-done | bytes 262176 | tf_op jit(solution)/shard_map/ppermute | solution.py:236
  22.1 1.3 %collective-permute-start.6 = (bf16[2,256,256]{2,1,0:T(8,128)(2,1)S(1)}, bf16[2,256,256]{2,1,0:T(8,128)(2,1)S(1)}, u32[]{:S(2)}, u32[]{:S(2)}) collective-permute-start(bf16[2,256,256]{2,1,0:T(8,128)(2,1)S(1)} %broadcast_select_fusion), channel_id=1, source_target_pairs={{0,4},{8,12},{16,20},{24,28},{1,5},{9,13},{17,21},{25,29},{2,6},{1... | collective-permute-start | bytes 786440 | tf_op jit(solution)/shard_map/ppermute | solution.py:236
  23.4 0.1 collective-permute-start.2
  23.6 0.5 collective-permute-start.3
  24.1 1.5 %collective-permute-start.4 = (bf16[2,256,256]{2,1,0:T(8,128)(2,1)S(1)}, bf16[2,256,256]{2,1,0:T(8,128)(2,1)S(1)}, u32[]{:S(2)}, u32[]{:S(2)}) collective-permute-start(bf16[2,256,256]{2,1,0:T(8,128)(2,1)S(1)} %pad_maximum_fusion.3.near), channel_id=1, source_target_pairs={{0,2},{1,3},{2,0},{3,1},{4,6},{5,7},{6,4},{7,5},{8,10},{9,11},{10,... | collective-permute-start | bytes 786440 | tf_op jit(solution)/shard_map/ppermute | solution.py:244
  25.6 2.4 %collective-permute-done.6 = bf16[2,256,256]{2,1,0:T(8,128)(2,1)S(1)} collective-permute-done((bf16[2,256,256]{2,1,0:T(8,128)(2,1)S(1)}, bf16[2,256,256]{2,1,0:T(8,128)(2,1)S(1)}, u32[]{:S(2)}, u32[]{:S(2)}) %collective-permute-start.6) | collective-permute-done | bytes 262176 | tf_op jit(solution)/shard_map/ppermute | solution.py:236
  28.1 1.6 %collective-permute-start.8 = (bf16[1,256,256]{2,1,0:T(8,128)(2,1)S(1)}, bf16[1,256,256]{2,1,0:T(8,128)(2,1)S(1)}, u32[]{:S(2)}, u32[]{:S(2)}) collective-permute-start(bf16[1,256,256]{2,1,0:T(8,128)(2,1)S(1)} %get-tuple-element.43), channel_id=1, source_target_pairs={{0,2},{1,3},{2,0},{3,1},{4,6},{5,7},{6,4},{7,5},{8,10},{9,11},{10,... | collective-permute-start | bytes 393224 | tf_op jit(solution)/shard_map/ppermute | solution.py:241
  29.7 0.1 pad_add_fusion.ids
  29.7 3.5 %collective-permute-done.4.far = bf16[2,256,256]{2,1,0:T(8,128)(2,1)S(1)} collective-permute-done((bf16[2,256,256]{2,1,0:T(8,128)(2,1)S(1)}, bf16[2,256,256]{2,1,0:T(8,128)(2,1)S(1)}, u32[]{:S(2)}, u32[]{:S(2)}) %collective-permute-start.4) | collective-permute-done | bytes 262176 | tf_op jit(solution)/shard_map/ppermute | solution.py:244
  33.3 0.0 collective-permute-done.2.qs
  33.3 0.0 collective-permute-done.3.cs
  33.3 4.1 %shard_map.84.own = f32[2,7,8,256]{3,2,1,0:T(8,128)S(1)} custom-call(s32[2]{0:T(128)S(1)} %pad_add_fusion.ids, s32[4,4]{1,0:T(4,128)S(1)} %copy-done.4, bf16[128,3584]{1,0:T(8,128)(2,1)S(1)} %copy-done, bf16[128,1792]{1,0:T(8,128)(2,1)S(1)} %collective-permute-done.2.qs, bf16[128,3584]{1,0:T(8,128)(2,1)S(1)} %copy-done.1, ...), custom_call_target="tpu_custom_call" | custom-call | flops 939524096 | bytes 3670016 | tf_op jit(solution)/shard_map/pallas_call | solution.py:194
  37.4 1.6 %collective-permute-start.7 = (bf16[1,256,256]{2,1,0:T(8,128)(2,1)S(1)}, bf16[1,256,256]{2,1,0:T(8,128)(2,1)S(1)}, u32[]{:S(2)}, u32[]{:S(2)}) collective-permute-start(bf16[1,256,256]{2,1,0:T(8,128)(2,1)S(1)} %get-tuple-element.42), channel_id=1, source_target_pairs={{0,2},{1,3},{2,0},{3,1},{4,6},{5,7},{6,4},{7,5},{8,10},{9,11},{10,... | collective-permute-start | bytes 393224 | tf_op jit(solution)/shard_map/ppermute | solution.py:241
  38.9 5.2 %shard_map.86 = (f32[1,7,8,256]{3,2,1,0:T(8,128)S(1)}, f32[1,7,128,256]{3,2,1,0:T(8,128)S(1)}, f32[1,7,128,256]{3,2,1,0:T(8,128)S(1)}, bf16[1,512,256]{2,1,0:T(8,128)(2,1)S(1)}) custom-call(s32[2]{0:T(128)S(1)} %pad_add_fusion.ids, s32[4,4]{1,0:T(4,128)S(1)} %copy-done.4, bf16[128,3584]{1,0:T(8,128)(2,1)S(1)} %copy-done, ...), custom_call_target="tpu_custom_call" | custom-call | flops 1409286144 | bytes 1835008 | tf_op jit(solution)/shard_map/pallas_call | solution.py:194
  44.2 0.6 collective-permute-start.13
  44.8 0.0 collective-permute-done.7.far
  44.8 5.3 %shard_map.85 = (f32[1,7,8,256]{3,2,1,0:T(8,128)S(1)}, f32[1,7,128,256]{3,2,1,0:T(8,128)S(1)}, f32[1,7,128,256]{3,2,1,0:T(8,128)S(1)}, bf16[1,512,256]{2,1,0:T(8,128)(2,1)S(1)}) custom-call(s32[2]{0:T(128)S(1)} %pad_add_fusion.ids, s32[4,4]{1,0:T(4,128)S(1)} %copy-done.4, bf16[128,3584]{1,0:T(8,128)(2,1)S(1)} %copy-done, ...), custom_call_target="tpu_custom_call" | custom-call | flops 1409286144 | bytes 1835008 | tf_op jit(solution)/shard_map/pallas_call | solution.py:194
  50.1 1.6 %collective-permute-start.12 = (bf16[256,256]{1,0:T(8,128)(2,1)S(1)}, bf16[256,256]{1,0:T(8,128)(2,1)S(1)}, u32[]{:S(2)}, u32[]{:S(2)}) collective-permute-start(bf16[256,256]{1,0:T(8,128)(2,1)S(1)} %slice_bitcast_fusion.1), channel_id=1, source_target_pairs={{0,2},{1,3},{2,0},{3,1},{4,6},{5,7},{6,4},{7,5},{8,10},{9,11},{10,... | collective-permute-start | bytes 393224 | tf_op jit(solution)/shard_map/ppermute | solution.py:279
  51.6 0.2 pad_maximum_fusion.att_p
  51.8 0.2 pad_maximum_fusion.1.dq_p
  52.1 3.0 %collective-permute-done.12 = bf16[256,256]{1,0:T(8,128)(2,1)S(1)} collective-permute-done((bf16[256,256]{1,0:T(8,128)(2,1)S(1)}, bf16[256,256]{1,0:T(8,128)(2,1)S(1)}, u32[]{:S(2)}, u32[]{:S(2)}) %collective-permute-start.12) | collective-permute-done | bytes 131104 | tf_op jit(solution)/shard_map/ppermute | solution.py:279
  55.2 0.8 fusion
  55.9 1.5 %collective-permute-start.14 = (bf16[2,256,256]{2,1,0:T(8,128)(2,1)}, bf16[2,256,256]{2,1,0:T(8,128)(2,1)}, u32[]{:S(2)}, u32[]{:S(2)}) collective-permute-start(bf16[2,256,256]{2,1,0:T(8,128)(2,1)} %fusion), channel_id=1, source_target_pairs={{4,0},{12,8},{20,16},{28,24},{5,1},{13,9},{21,17},{29,25},{6,2},{1... | collective-permute-start | bytes 786440 | tf_op jit(solution)/shard_map/ppermute | solution.py:286
  57.4 7.1 %shard_map.87 = (bf16[128,1792]{1,0:T(8,128)(2,1)S(1)}, bf16[128,1792]{1,0:T(8,128)(2,1)}, bf16[128,1792]{1,0:T(8,128)(2,1)S(1)}, bf16[128,1792]{1,0:T(8,128)(2,...) custom-call(s32[2]{0:T(128)S(1)} %pad_add_fusion.ids, s32[4,4]{1,0:T(4,128)S(1)} %copy-done.4, ...), custom_call_target="tpu_custom_call" | custom-call | flops 2818572288 | bytes 3670016 | tf_op jit(solution)/shard_map/pallas_call | solution.py:194
  64.5 0.8 copy-done.2
  65.3 0.7 copy-done.3
  66.0 0.0 collective-permute-start.9
  66.0 0.5 collective-permute-start.10
  66.5 1.5 %collective-permute-start.11 = (bf16[2,256,256]{2,1,0:T(8,128)(2,1)}, bf16[2,256,256]{2,1,0:T(8,128)(2,1)S(1)}, u32[]{:S(2)}, u32[]{:S(2)}) collective-permute-start(bf16[2,256,256]{2,1,0:T(8,128)(2,1)} %copy-done.3), channel_id=1, source_target_pairs={{0,2},{1,3},{2,0},{3,1},{4,6},{5,7},{6,4},{7,5},{8,10},{9,11},{10,... | collective-permute-start | bytes 786440 | tf_op jit(solution)/shard_map/ppermute | solution.py:305
  68.0 0.0 collective-permute-done.14
  68.0 1.2 %fusion.4 = bf16[2,256,256]{2,1,0:T(8,128)(2,1)S(1)} fusion(bf16[2,256,256]{2,1,0:T(8,128)(2,1)} %collective-permute-done.14, f32[1,256,256]{2,1,0:T(8,128)} %copy-done.5, f32[1,256,256]{2,1,0:T(8,128)} %copy-done.7), kind=kLoop, calls=%fused_computation.33 | loop fusion | flops 524288 | bytes 1048576 | tf_op jit(solution)/shard_map/convert_element_type | solution.py:286
  69.2 1.3 %collective-permute-start.15 = (bf16[2,256,256]{2,1,0:T(8,128)(2,1)S(1)}, bf16[2,256,256]{2,1,0:T(8,128)(2,1)S(1)}, u32[]{:S(2)}, u32[]{:S(2)}) collective-permute-start(bf16[2,256,256]{2,1,0:T(8,128)(2,1)S(1)} %fusion.4), channel_id=1, source_target_pairs={{8,0},{24,16},{9,1},{25,17},{10,2},{26,18},{11,3},{27,19}} | collective-permute-start | bytes 786440 | tf_op jit(solution)/shard_map/ppermute | solution.py:286
  70.5 0.0 collective-permute-done.9
  70.5 1.1 %maximum_select_fusion = bf16[128,3584]{1,0:T(8,128)(2,1)} fusion(bf16[128,1792]{1,0:T(8,128)(2,1)S(1)} %collective-permute-done.9, bf16[128,1792]{1,0:T(8,128)(2,1)S(1)} %get-tuple-element.30, pred[]{:T(512)S(6)} %eq.22), kind=kLoop, calls=%fused_computation.2 | loop fusion | flops 4128768 | bytes 1835009 | tf_op jit(solution)/shard_map/jit(_where)/select_n | solution.py:308
  71.6 7.5 %collective-permute-done.15 = bf16[2,256,256]{2,1,0:T(8,128)(2,1)S(1)} collective-permute-done((bf16[2,256,256]{2,1,0:T(8,128)(2,1)S(1)}, bf16[2,256,256]{2,1,0:T(8,128)(2,1)S(1)}, u32[]{:S(2)}, u32[]{:S(2)}) %collective-permute-start.15) | collective-permute-done | bytes 262176 | tf_op jit(solution)/shard_map/ppermute | solution.py:286
  79.1 1.0 %fusion.1 = bf16[2,256,256]{2,1,0:T(8,128)(2,1)S(1)} fusion(bf16[2,256,256]{2,1,0:T(8,128)(2,1)S(1)} %collective-permute-done.15, bf16[2,256,256]{2,1,0:T(8,128)(2,1)} %collective-permute-done.14, f32[1,256,256]{2,1,0:T(8,128)S(1)} %copy-done.6, f32[1,256,256]{2,1,0:T(8,128)S(1)} %copy-done.8), kind=kLoop, calls=%fused_computation.9 | loop fusion | flops 786432 | bytes 1310720 | tf_op jit(solution)/shard_map/convert_element_type | solution.py:286
  80.2 1.3 %collective-permute-start.16 = (bf16[2,256,256]{2,1,0:T(8,128)(2,1)S(1)}, bf16[2,256,256]{2,1,0:T(8,128)(2,1)S(1)}, u32[]{:S(2)}, u32[]{:S(2)}) collective-permute-start(bf16[2,256,256]{2,1,0:T(8,128)(2,1)S(1)} %fusion.1), channel_id=1, source_target_pairs={{16,0},{17,1},{18,2},{19,3}} | collective-permute-start | bytes 786440 | tf_op jit(solution)/shard_map/ppermute | solution.py:286
  81.5 0.0 collective-permute-done.10
  81.5 1.1 %maximum_select_fusion.1 = bf16[128,3584]{1,0:T(8,128)(2,1)} fusion(bf16[128,1792]{1,0:T(8,128)(2,1)S(1)} %collective-permute-done.10, bf16[128,1792]{1,0:T(8,128)(2,1)S(1)} %get-tuple-element.32, pred[]{:T(512)S(6)} %eq.22), kind=kLoop, calls=%fused_computation.3 | loop fusion | flops 4128768 | bytes 1835009 | tf_op jit(solution)/shard_map/jit(_where)/select_n | solution.py:308
  82.6 0.0 collective-permute-done.11
  82.6 7.6 %collective-permute-done.16 = bf16[2,256,256]{2,1,0:T(8,128)(2,1)S(1)} collective-permute-done((bf16[2,256,256]{2,1,0:T(8,128)(2,1)S(1)}, bf16[2,256,256]{2,1,0:T(8,128)(2,1)S(1)}, u32[]{:S(2)}, u32[]{:S(2)}) %collective-permute-start.16) | collective-permute-done | bytes 262176 | tf_op jit(solution)/shard_map/ppermute | solution.py:286
  90.3 1.1 %add_convert_fusion = bf16[2,256,256]{2,1,0:T(8,128)(2,1)S(1)} fusion(bf16[2,256,256]{2,1,0:T(8,128)(2,1)S(1)} %collective-permute-done.16, f32[2,256,256]{2,1,0:T(8,128)S(1)} %get-tuple-element.34, bf16[2,256,256]{2,1,0:T(8,128)(2,1)S(1)} %collective-permute-done.11, bf16[2,256,256]{2,1,0:T(8,128)(2,1)S(1)} %collective-permute-done.15, pred[]{:T(512)S(6)} %eq.26, ...), kind=kLoop, calls=%fused_computation.5 | loop fusion | flops 1572864 | bytes 2359297 | tf_op jit(solution)/shard_map/convert_element_type | solution.py:316
  91.4 0.1 collective-permute-start.17
  91.5 1.3 %collective-permute-done.17 = bf16[2,128,256]{2,1,0:T(8,128)(2,1)S(1)} collective-permute-done((bf16[2,128,256]{2,1,0:T(8,128)(2,1)S(1)}, bf16[2,128,256]{2,1,0:T(8,128)(2,1)S(1)}, u32[]{:S(2)}, u32[]{:S(2)}) %collective-permute-start.17) | collective-permute-done | bytes 131104 | tf_op jit(solution)/shard_map/ppermute | solution.py:317
  92.9 0.7 maximum_select_fusion.2
  93.5 0.7 maximum_select_fusion.3
  (31 shorter events, 0.4 us)
Async XLA Ops:
  1.9 21.5 %copy-start = (bf16[128,3584]{1,0:T(8,128)(2,1)S(1)}, bf16[128,3584]{1,0:T(8,128)(2,1)}, u32[]{:S(2)}) copy-start(bf16[128,3584]{1,0:T(8,128)(2,1)} %qm.7) | copy-start | bytes 2752516
  2.1 1.5 %collective-permute-start = (bf16[2,128,256]{2,1,0:T(8,128)(2,1)S(1)}, bf16[2,128,256]{2,1,0:T(8,128)(2,1)S(1)}, u32[]{:S(2)}, u32[]{:S(2)}) collective-permute-start(bf16[2,128,256]{2,1,0:T(8,128)(2,1)S(1)} %bitcast.48), channel_id=1, source_target_pairs={{0,1},{1,0},{2,3},{3,2},{4,5},{5,4},{6,7},{7,6},{8,9},{9,8},{10,11... | collective-permute-start | bytes 393224 | tf_op jit(solution)/shard_map/ppermute | solution.py:231
  2.9 20.6 %copy-start.1 = (bf16[128,3584]{1,0:T(8,128)(2,1)S(1)}, bf16[128,3584]{1,0:T(8,128)(2,1)}, u32[]{:S(2)}) copy-start(bf16[128,3584]{1,0:T(8,128)(2,1)} %cm.7) | copy-start | bytes 2752516
  3.6 11.7 %collective-permute-start.1 = (bf16[2,256,256]{2,1,0:T(8,128)(2,1)S(1)}, bf16[2,256,256]{2,1,0:T(8,128)(2,1)S(1)}, u32[]{:S(2)}, u32[]{:S(2)}) collective-permute-start(bf16[2,256,256]{2,1,0:T(8,128)(2,1)S(1)} %pad_maximum_fusion.3.near), channel_id=1, source_target_pairs={{0,16},{1,17},{2,18},{3,19}} | collective-permute-start | bytes 786440 | tf_op jit(solution)/shard_map/ppermute | solution.py:236
  15.4 6.6 %collective-permute-start.5 = (bf16[2,256,256]{2,1,0:T(8,128)(2,1)S(1)}, bf16[2,256,256]{2,1,0:T(8,128)(2,1)S(1)}, u32[]{:S(2)}, u32[]{:S(2)}) collective-permute-start(bf16[2,256,256]{2,1,0:T(8,128)(2,1)S(1)} %broadcast_select_fusion.2), channel_id=1, source_target_pairs={{0,8},{16,24},{1,9},{17,25},{2,10},{18,26},{3,11},{19,27}} | collective-permute-start | bytes 786440 | tf_op jit(solution)/shard_map/ppermute | solution.py:236
  16.8 16.5 %copy-start.4 = (s32[4,4]{1,0:T(4,128)S(1)}, s32[4,4]{1,0:T(4,128)}, u32[]{:S(2)}) copy-start(s32[4,4]{1,0:T(4,128)} %tree.7) | copy-start | bytes 196
  22.1 6.0 %collective-permute-start.6 = (bf16[2,256,256]{2,1,0:T(8,128)(2,1)S(1)}, bf16[2,256,256]{2,1,0:T(8,128)(2,1)S(1)}, u32[]{:S(2)}, u32[]{:S(2)}) collective-permute-start(bf16[2,256,256]{2,1,0:T(8,128)(2,1)S(1)} %broadcast_select_fusion), channel_id=1, source_target_pairs={{0,4},{8,12},{16,20},{24,28},{1,5},{9,13},{17,21},{25,29},{2,6},{1... | collective-permute-start | bytes 786440 | tf_op jit(solution)/shard_map/ppermute | solution.py:236
  23.4 9.8 %collective-permute-start.2 = (bf16[128,1792]{1,0:T(8,128)(2,1)S(1)}, bf16[128,1792]{1,0:T(8,128)(2,1)S(1)}, u32[]{:S(2)}, u32[]{:S(2)}) collective-permute-start(bf16[128,1792]{1,0:T(8,128)(2,1)S(1)} %constant_dynamic-slice_fusion.1), channel_id=1, source_target_pairs={{0,1},{1,0},{2,3},{3,2},{4,5},{5,4},{6,7},{7,6},{8,9},{9,8},{10,11... | collective-permute-start | bytes 1376264 | tf_op jit(solution)/shard_map/ppermute | solution.py:246
  23.6 9.7 %collective-permute-start.3 = (bf16[128,1792]{1,0:T(8,128)(2,1)S(1)}, bf16[128,1792]{1,0:T(8,128)(2,1)S(1)}, u32[]{:S(2)}, u32[]{:S(2)}) collective-permute-start(bf16[128,1792]{1,0:T(8,128)(2,1)S(1)} %constant_dynamic-slice_fusion), channel_id=1, source_target_pairs={{0,1},{1,0},{2,3},{3,2},{4,5},{5,4},{6,7},{7,6},{8,9},{9,8},{10,11... | collective-permute-start | bytes 1376264 | tf_op jit(solution)/shard_map/ppermute | solution.py:247
  24.1 9.2 %collective-permute-start.4 = (bf16[2,256,256]{2,1,0:T(8,128)(2,1)S(1)}, bf16[2,256,256]{2,1,0:T(8,128)(2,1)S(1)}, u32[]{:S(2)}, u32[]{:S(2)}) collective-permute-start(bf16[2,256,256]{2,1,0:T(8,128)(2,1)S(1)} %pad_maximum_fusion.3.near), channel_id=1, source_target_pairs={{0,2},{1,3},{2,0},{3,1},{4,6},{5,7},{6,4},{7,5},{8,10},{9,11},{10,... | collective-permute-start | bytes 786440 | tf_op jit(solution)/shard_map/ppermute | solution.py:244
  28.1 10.8 %collective-permute-start.8 = (bf16[1,256,256]{2,1,0:T(8,128)(2,1)S(1)}, bf16[1,256,256]{2,1,0:T(8,128)(2,1)S(1)}, u32[]{:S(2)}, u32[]{:S(2)}) collective-permute-start(bf16[1,256,256]{2,1,0:T(8,128)(2,1)S(1)} %get-tuple-element.43), channel_id=1, source_target_pairs={{0,2},{1,3},{2,0},{3,1},{4,6},{5,7},{6,4},{7,5},{8,10},{9,11},{10,... | collective-permute-start | bytes 393224 | tf_op jit(solution)/shard_map/ppermute | solution.py:241
  37.4 7.4 %collective-permute-start.7 = (bf16[1,256,256]{2,1,0:T(8,128)(2,1)S(1)}, bf16[1,256,256]{2,1,0:T(8,128)(2,1)S(1)}, u32[]{:S(2)}, u32[]{:S(2)}) collective-permute-start(bf16[1,256,256]{2,1,0:T(8,128)(2,1)S(1)} %get-tuple-element.42), channel_id=1, source_target_pairs={{0,2},{1,3},{2,0},{3,1},{4,6},{5,7},{6,4},{7,5},{8,10},{9,11},{10,... | collective-permute-start | bytes 393224 | tf_op jit(solution)/shard_map/ppermute | solution.py:241
  44.2 7.9 %collective-permute-start.13 = (bf16[256,256]{1,0:T(8,128)(2,1)S(1)}, bf16[256,256]{1,0:T(8,128)(2,1)S(1)}, u32[]{:S(2)}, u32[]{:S(2)}) collective-permute-start(bf16[256,256]{1,0:T(8,128)(2,1)S(1)} %slice_bitcast_fusion), channel_id=1, source_target_pairs={{0,2},{1,3},{2,0},{3,1},{4,6},{5,7},{6,4},{7,5},{8,10},{9,11},{10,... | collective-permute-start | bytes 393224 | tf_op jit(solution)/shard_map/ppermute | solution.py:279
  50.1 5.0 %collective-permute-start.12 = (bf16[256,256]{1,0:T(8,128)(2,1)S(1)}, bf16[256,256]{1,0:T(8,128)(2,1)S(1)}, u32[]{:S(2)}, u32[]{:S(2)}) collective-permute-start(bf16[256,256]{1,0:T(8,128)(2,1)S(1)} %slice_bitcast_fusion.1), channel_id=1, source_target_pairs={{0,2},{1,3},{2,0},{3,1},{4,6},{5,7},{6,4},{7,5},{8,10},{9,11},{10,... | collective-permute-start | bytes 393224 | tf_op jit(solution)/shard_map/ppermute | solution.py:279
  52.1 3.8 %copy-start.5 = (f32[1,256,256]{2,1,0:T(8,128)}, f32[1,256,256]{2,1,0:T(8,128)S(1)}, u32[]{:S(2)}) copy-start(f32[1,256,256]{2,1,0:T(8,128)S(1)} %fusion.2) | copy-start | bytes 786436
  55.1 0.8 copy-start.7
  55.9 12.1 %collective-permute-start.14 = (bf16[2,256,256]{2,1,0:T(8,128)(2,1)}, bf16[2,256,256]{2,1,0:T(8,128)(2,1)}, u32[]{:S(2)}, u32[]{:S(2)}) collective-permute-start(bf16[2,256,256]{2,1,0:T(8,128)(2,1)} %fusion), channel_id=1, source_target_pairs={{4,0},{12,8},{20,16},{28,24},{5,1},{13,9},{21,17},{29,25},{6,2},{1... | collective-permute-start | bytes 786440 | tf_op jit(solution)/shard_map/ppermute | solution.py:286
  64.5 0.8 copy-start.2
  65.3 0.7 copy-start.3
  66.0 13.1 %copy-start.6 = (f32[1,256,256]{2,1,0:T(8,128)S(1)}, f32[1,256,256]{2,1,0:T(8,128)}, u32[]{:S(2)}) copy-start(f32[1,256,256]{2,1,0:T(8,128)} %copy-done.5) | copy-start | bytes 786436
  66.0 13.1 %copy-start.8 = (f32[1,256,256]{2,1,0:T(8,128)S(1)}, f32[1,256,256]{2,1,0:T(8,128)}, u32[]{:S(2)}) copy-start(f32[1,256,256]{2,1,0:T(8,128)} %copy-done.7) | copy-start | bytes 786436
  66.0 4.5 %collective-permute-start.9 = (bf16[128,1792]{1,0:T(8,128)(2,1)}, bf16[128,1792]{1,0:T(8,128)(2,1)S(1)}, u32[]{:S(2)}, u32[]{:S(2)}) collective-permute-start(bf16[128,1792]{1,0:T(8,128)(2,1)} %get-tuple-element.31), channel_id=1, source_target_pairs={{0,1},{1,0},{2,3},{3,2},{4,5},{5,4},{6,7},{7,6},{8,9},{9,8},{10,11... | collective-permute-start | bytes 1376264 | tf_op jit(solution)/shard_map/ppermute | solution.py:314
  66.0 15.5 %collective-permute-start.10 = (bf16[128,1792]{1,0:T(8,128)(2,1)}, bf16[128,1792]{1,0:T(8,128)(2,1)S(1)}, u32[]{:S(2)}, u32[]{:S(2)}) collective-permute-start(bf16[128,1792]{1,0:T(8,128)(2,1)} %copy-done.2), channel_id=1, source_target_pairs={{0,1},{1,0},{2,3},{3,2},{4,5},{5,4},{6,7},{7,6},{8,9},{9,8},{10,11... | collective-permute-start | bytes 1376264 | tf_op jit(solution)/shard_map/ppermute | solution.py:315
  66.5 16.1 %collective-permute-start.11 = (bf16[2,256,256]{2,1,0:T(8,128)(2,1)}, bf16[2,256,256]{2,1,0:T(8,128)(2,1)S(1)}, u32[]{:S(2)}, u32[]{:S(2)}) collective-permute-start(bf16[2,256,256]{2,1,0:T(8,128)(2,1)} %copy-done.3), channel_id=1, source_target_pairs={{0,2},{1,3},{2,0},{3,1},{4,6},{5,7},{6,4},{7,5},{8,10},{9,11},{10,... | collective-permute-start | bytes 786440 | tf_op jit(solution)/shard_map/ppermute | solution.py:305
  69.2 10.0 %collective-permute-start.15 = (bf16[2,256,256]{2,1,0:T(8,128)(2,1)S(1)}, bf16[2,256,256]{2,1,0:T(8,128)(2,1)S(1)}, u32[]{:S(2)}, u32[]{:S(2)}) collective-permute-start(bf16[2,256,256]{2,1,0:T(8,128)(2,1)S(1)} %fusion.4), channel_id=1, source_target_pairs={{8,0},{24,16},{9,1},{25,17},{10,2},{26,18},{11,3},{27,19}} | collective-permute-start | bytes 786440 | tf_op jit(solution)/shard_map/ppermute | solution.py:286
  80.2 10.1 %collective-permute-start.16 = (bf16[2,256,256]{2,1,0:T(8,128)(2,1)S(1)}, bf16[2,256,256]{2,1,0:T(8,128)(2,1)S(1)}, u32[]{:S(2)}, u32[]{:S(2)}) collective-permute-start(bf16[2,256,256]{2,1,0:T(8,128)(2,1)S(1)} %fusion.1), channel_id=1, source_target_pairs={{16,0},{17,1},{18,2},{19,3}} | collective-permute-start | bytes 786440 | tf_op jit(solution)/shard_map/ppermute | solution.py:286
  91.4 1.4 %collective-permute-start.17 = (bf16[2,128,256]{2,1,0:T(8,128)(2,1)S(1)}, bf16[2,128,256]{2,1,0:T(8,128)(2,1)S(1)}, u32[]{:S(2)}, u32[]{:S(2)}) collective-permute-start(bf16[2,128,256]{2,1,0:T(8,128)(2,1)S(1)} %slice.69), channel_id=1, source_target_pairs={{0,1},{1,0},{2,3},{3,2},{4,5},{5,4},{6,7},{7,6},{8,9},{9,8},{10,11... | collective-permute-start | bytes 393224 | tf_op jit(solution)/shard_map/ppermute | solution.py:317

commit v3 on v2

v3 whole, which is shorter than its diff:
```python
import functools
import math

import jax
import jax.numpy as jnp
from jax import lax
from jax.experimental import pallas as pl
from jax.experimental.pallas import tpu as pltpu
from jax.sharding import PartitionSpec as P

QUERY_HEADS = 28
KEY_VALUE_HEADS = 4
HEAD_SIZE = 128
GROUP = QUERY_HEADS // KEY_VALUE_HEADS
WIDTH = GROUP * HEAD_SIZE
HEADS = KEY_VALUE_HEADS // 2
SCALE = HEAD_SIZE ** (-0.5)
EXP2_SCALE = SCALE * math.log2(math.e)
MASKED = -1e30
VMEM_BYTES = 16 * 1024 * 1024


def dot_nt(a, b):
    return lax.dot_general(a, b, (((1,), (1,)), ((), ())), preferred_element_type=jnp.float32)


def dot_nn(a, b):
    return lax.dot_general(a, b, (((1,), (0,)), ((), ())), preferred_element_type=jnp.float32)


def head_rows(mine, sibling, g):
    columns = slice(g * HEAD_SIZE, (g + 1) * HEAD_SIZE)
    return jnp.concatenate([mine[:, columns], sibling[:, columns]], axis=0)


def causal_mask(scores, places, rows, ids, tree):
    h = ids[0]
    lane = lax.broadcasted_iota(jnp.int32, (rows, rows), 1)
    sub = lax.broadcasted_iota(jnp.int32, (rows, rows), 0)
    ahead = lane - sub
    out = []
    for i, b in enumerate(places):
        line = []
        for a in range(2):
            offset = ((h ^ b) - (h ^ a)) * rows
            tile = scores[i * rows : (i + 1) * rows, a * rows : (a + 1) * rows]
            line.append(jnp.where(ahead >= offset, tile, MASKED))
        out.append(jnp.concatenate(line, axis=1))
    return jnp.concatenate(out, axis=0)


def prompt_mask(scores, places, rows, ids, tree):
    h, s = ids[0], ids[1]
    lane = lax.broadcasted_iota(jnp.int32, (1, 2 * rows), 1)
    out = []
    for i, b in enumerate(places):
        reads = [jnp.logical_and(tree[h ^ a, h ^ b] > 0, s > 0) for a in range(2)]
        bias = [jnp.where(r, jnp.float32(0.0), jnp.float32(MASKED)) for r in reads]
        row = jnp.where(lane < rows, bias[0], bias[1])
        out.append(scores[i * rows : (i + 1) * rows] + row)
    return jnp.concatenate(out, axis=0)


def keys_values(blocks):
    keys = jnp.concatenate([b[:, :HEAD_SIZE] for b in blocks], axis=0)
    values = jnp.concatenate([b[:, HEAD_SIZE:] for b in blocks], axis=0)
    return keys, values


def scores_of(segments, q, rows, ids, tree):
    parts = [mask(dot_nt(keys, q), places, rows, ids, tree) for mask, places, keys, _ in segments]
    return parts[0] if len(parts) == 1 else jnp.concatenate(parts, axis=0)


def dprob_of(segments, ct):
    parts = [dot_nt(values, ct) for _, _, _, values in segments]
    return parts[0] if len(parts) == 1 else jnp.concatenate(parts, axis=0)


def load(layout, refs):
    segments = []
    for mask, places in layout:
        segments.append((mask, places, *keys_values(refs[: len(places)])))
        refs = refs[len(places) :]
    return segments, refs


def stats_kernel(layout, ids, tree, qm, qs, cm, cs, *refs):
    segments, refs = load(layout, refs)
    stats = refs[-1]
    rows = qm.shape[0]
    for g in range(GROUP):
        q = head_rows(qm, qs, g)
        ct = head_rows(cm, cs, g)
        scores = scores_of(segments, q, rows, ids, tree)
        top = jnp.max(scores, axis=0, keepdims=True)
        e = jnp.exp2((scores - top) * EXP2_SCALE)
        stats[0, g, 0:1, :] = top
        stats[0, g, 1:2, :] = jnp.sum(e, axis=0, keepdims=True)
        stats[0, g, 2:3, :] = jnp.sum(e * dprob_of(segments, ct), axis=0, keepdims=True)


def add_terms(g, key_sum, value_sum, rounded, dscore, ct, q):
    value_term = dot_nn(rounded, ct)
    key_term = dot_nn(dscore, q)
    if g == 0:
        value_sum[...] = value_term
        key_sum[...] = key_term
    else:
        value_sum[...] += value_term
        key_sum[...] += key_term


def put_terms(out, part, key_sum, value_sum):
    out[:, :HEAD_SIZE] = (key_sum[part, :] * SCALE).astype(out.dtype)
    out[:, HEAD_SIZE:] = value_sum[part, :].astype(out.dtype)


def last_keys_kernel(layout, ids, tree, qm, qs, cm, cs, *refs):
    segments, refs = load(layout, refs)
    old, stats, terms, key_sum, value_sum = refs
    rows = qm.shape[0]
    for g in range(GROUP):
        q = head_rows(qm, qs, g)
        ct = head_rows(cm, cs, g)
        scores = scores_of(segments, q, rows, ids, tree)
        old_top = old[0, g, 0:1, :]
        top = jnp.maximum(jnp.max(scores, axis=0, keepdims=True), old_top)
        keep = jnp.exp2((old_top - top) * EXP2_SCALE)
        e = jnp.exp2((scores - top) * EXP2_SCALE)
        dprob = dprob_of(segments, ct)
        inverse = 1.0 / (jnp.sum(e, axis=0, keepdims=True) + old[0, g, 1:2, :] * keep)
        delta = jnp.sum(e * dprob, axis=0, keepdims=True) + old[0, g, 2:3, :] * keep
        delta = delta * inverse
        probs = e * inverse
        dscore = (probs * (dprob - delta)).astype(jnp.bfloat16)
        add_terms(g, key_sum, value_sum, probs.astype(jnp.bfloat16), dscore, ct, q)
        stats[0, g, 0:1, :] = top
        stats[0, g, 1:2, :] = inverse
        stats[0, g, 2:3, :] = delta
    put_terms(terms, slice(None), key_sum, value_sum)


def probs_dscore(segments, stats, g, q, ct, rows, ids, tree):
    scores = scores_of(segments, q, rows, ids, tree)
    probs = jnp.exp2((scores - stats[0, g, 0:1, :]) * EXP2_SCALE) * stats[0, g, 1:2, :]
    dscore = probs * (dprob_of(segments, ct) - stats[0, g, 2:3, :])
    return probs.astype(jnp.bfloat16), dscore.astype(jnp.bfloat16)


def terms_kernel(layout, ids, tree, qm, qs, cm, cs, *refs):
    segments, refs = load(layout, refs)
    stats, terms, key_sum, value_sum = refs
    for g in range(GROUP):
        q = head_rows(qm, qs, g)
        ct = head_rows(cm, cs, g)
        rounded, dscore = probs_dscore(segments, stats, g, q, ct, qm.shape[0], ids, tree)
        add_terms(g, key_sum, value_sum, rounded, dscore, ct, q)
    put_terms(terms, slice(None), key_sum, value_sum)


def rows_kernel(layout, ids, tree, qm, qs, cm, cs, *refs):
    segments, refs = load(layout, refs)
    stats, _, att_m, att_s, dq_m, dq_s, near, far, token, key_sum, value_sum = refs
    token[...] = jnp.zeros_like(token)
    rows = qm.shape[0]
    own = segments[0][2].shape[0]
    keys_t = jnp.concatenate([keys for _, _, keys, _ in segments], axis=0).T
    values_t = jnp.concatenate([values for _, _, _, values in segments], axis=0).T
    for g in range(GROUP):
        columns = slice(g * HEAD_SIZE, (g + 1) * HEAD_SIZE)
        q = head_rows(qm, qs, g)
        ct = head_rows(cm, cs, g)
        rounded, dscore = probs_dscore(segments, stats, g, q, ct, rows, ids, tree)
        add_terms(g, key_sum, value_sum, rounded[:own], dscore[:own], ct, q)
        att = dot_nn(values_t, rounded).T.astype(jnp.bfloat16)
        dq = (dot_nn(keys_t, dscore) * SCALE).T.astype(jnp.bfloat16)
        att_m[:, columns] = att[:rows]
        att_s[:, columns] = att[rows:]
        dq_m[:, columns] = dq[:rows]
        dq_s[:, columns] = dq[rows:]
    half = near.shape[0]
    put_terms(near, slice(0, half), key_sum, value_sum)
    put_terms(far, slice(half, 2 * half), key_sum, value_sum)


def call(kernel, layout, heads, scalars, work, blocks, inputs, outs, scratch, products, tie=None):
    rows = work[0].shape[0]
    first, count = heads
    mine = pl.BlockSpec((rows, WIDTH), lambda i, ids, tree: (0, HEADS * (ids[0] & 1) + i + first))

    def spec(shape, base):
        if len(shape) == 2:
            return pl.BlockSpec((shape[0], shape[1] // (HEADS if base is not None else count)), lambda i, *refs: (0, i + (base or 0)))
        return pl.BlockSpec((1, *shape[1:]), lambda i, *refs: (i + (base or 0),) + (0,) * (len(shape) - 1))

    sib = spec((rows, HEADS * WIDTH), first)
    specs = [mine, sib, mine, sib] + [spec(x.shape, first) for x in (*blocks, *inputs)]
    operands = [*scalars, *work, *blocks, *inputs]
    out_specs = [spec(o.shape, None) for o in outs]
    if tie is not None:
        operands.append(tie)
        specs.append(pl.BlockSpec((16, HEAD_SIZE), lambda i, *refs: (0, 0)))
        outs = [*outs, jax.ShapeDtypeStruct(tie.shape, tie.dtype)]
        out_specs.append(pl.BlockSpec(tie.shape, lambda i, *refs: (0, 0)))
    flops = count * 2 * products * (2 * rows * GROUP) * (len(blocks) * rows) * HEAD_SIZE
    return pl.pallas_call(
        functools.partial(kernel, layout),
        grid_spec=pltpu.PrefetchScalarGridSpec(
            num_scalar_prefetch=2,
            grid=(count,),
            in_specs=specs,
            out_specs=out_specs,
            scratch_shapes=scratch,
        ),
        out_shape=outs,
        compiler_params=pltpu.CompilerParams(vmem_limit_bytes=VMEM_BYTES),
        cost_estimate=pl.CostEstimate(
            flops=flops, bytes_accessed=count * 4 * 2 * rows * WIDTH * 2, transcendentals=0
        ),
    )(*operands)


def after(x, *tokens):
    return lax.optimization_barrier((x, *tokens))[0]


def on_device(seq_count, head_count, queries, rotated_key_rows, value_matrix, cotangent, tree_mask):
    s = lax.axis_index("seq")
    h = lax.axis_index("head")
    rows = queries.shape[0]
    core = h & 1
    scalars = (jnp.stack([h, s]).astype(jnp.int32), tree_mask)
    f32, bf16 = jnp.float32, jnp.bfloat16
    shape = jax.ShapeDtypeStruct

    def send(x, mask):
        return lax.ppermute(x, "head", [(i, i ^ mask) for i in range(head_count)])

    def columns(x, place, width):
        return lax.dynamic_slice_in_dim(x, place * width, width, 1)

    def half(kv, place):
        k, v = [columns(x, place, HEADS * HEAD_SIZE) for x in kv]
        parts = []
        for j in range(HEADS):
            part = slice(j * HEAD_SIZE, (j + 1) * HEAD_SIZE)
            parts += [k[:, part], v[:, part]]
        return jnp.concatenate(parts, axis=1)

    def gathered(kv, place):
        mine, other = half(kv, place), half(kv, 1 - place)
        return [mine, send(other, 1), send(mine, 2), send(other, 3)]

    hops = [1]
    step = seq_count // 2
    while step > 1:
        hops.append(step)
        step //= 2
    held = (rotated_key_rows, value_matrix)
    for hop, step in enumerate(hops):
        reached = seq_count if hop == 0 else 2 * step
        sends = [(i, i + step) for i in range(0, seq_count, reached)]
        if hop:
            sends += [(i + 1, i + 1 + step) for i, _ in sends]
            place = s - s % 2
            got = lax.ppermute(held, "seq", sends)
        else:
            place = s
            got = jnp.concatenate([lax.ppermute(x, "seq", sends) for x in held], axis=1)
            held = jnp.concatenate(held, axis=1)
        held = jnp.where(place % reached == step, got, held)
        if hop == 0:
            side = after(core, held[:16, :HEAD_SIZE])
            own_blocks = gathered((rotated_key_rows, value_matrix), side)
            q_sib = send(columns(queries, 1 - side, HEADS * WIDTH), 1)
            c_sib = send(columns(cotangent, 1 - side, HEADS * WIDTH), 1)
            work = (queries, q_sib, cotangent, c_sib)
    width = KEY_VALUE_HEADS * HEAD_SIZE
    prompt = (held[:, :width], held[:, width:])
    prompt_blocks = gathered(prompt, core)

    near, far = (0, 1), (2, 3)
    own_all = (causal_mask, near + far)
    every, one = (0, HEADS), 1

    def stats_shape():
        return shape((HEADS, GROUP, 8, 2 * rows), f32)

    def terms_shape(count, dtype):
        return shape((2 * rows, 2 * count * HEAD_SIZE), dtype)

    def sums(n):
        return [pltpu.VMEM((n * rows, HEAD_SIZE), f32)] * 2

    layout = (own_all, (prompt_mask, near))
    blocks = [*own_blocks, *prompt_blocks[:2]]
    stats = call(stats_kernel, layout, every, scalars, work, blocks, [], [stats_shape()], [], 2)[0]
    layout = ((prompt_mask, far),)
    outs = [stats_shape(), terms_shape(HEADS, bf16)]
    stats, terms_far = call(
        last_keys_kernel, layout, every, scalars, work, prompt_blocks[2:], [stats], outs, sums(2), 4
    )
    layout = ((prompt_mask, near),)
    outs = [terms_shape(HEADS, f32)]
    terms = call(
        terms_kernel, layout, every, scalars, work, prompt_blocks[:2], [stats], outs, sums(2), 4
    )[0]

    def plus(a, b):
        return a.astype(f32) + b.astype(f32)

    total = plus(terms, send(terms_far, 2)).astype(bf16)
    layout = (own_all, (prompt_mask, near + far))
    blocks = [*own_blocks, *prompt_blocks]
    att, dq, own_sums = [], [], []
    step, hop = 1, 0
    while step < seq_count:
        sends = [(i + step, i) for i in range(0, seq_count, 2 * step)]
        got = lax.ppermute(total, "seq", sends)
        if hop < HEADS:
            outs = [shape((rows, WIDTH), bf16)] * 4 + [terms_shape(1, f32), terms_shape(1, bf16)]
            a_m, a_s, d_m, d_s, own_near, own_far, token = call(
                rows_kernel, layout, (hop, one), scalars, work, blocks, [stats], outs, sums(4), 8, total
            )
            att.append((a_m, send(a_s, 1)))
            dq.append((d_m, send(d_s, 1)))
            own_sums.append((own_near, own_far))
            got = plus(got, token)
        total = plus(total, got).astype(bf16)
        step *= 2
        hop += 1

    def both_halves(parts):
        mine = jnp.concatenate([x for x, _ in parts], axis=1)
        theirs = jnp.concatenate([x for _, x in parts], axis=1)
        return jnp.where(
            core == 0,
            jnp.concatenate([mine, theirs], axis=1),
            jnp.concatenate([theirs, mine], axis=1),
        )

    attention, query_grad = both_halves(att), both_halves(dq)
    total = jnp.where(s == 0, total.astype(f32), jnp.float32(0.0))
    own_near, own_far = [jnp.concatenate(x, axis=1) for x in zip(*own_sums)]
    total = (plus(own_near, send(own_far, 2)) + total).astype(bf16)
    total = both_halves([(total[:rows], send(total[rows:], 1))])

    def gradient(first):
        parts = []
        for j in range(KEY_VALUE_HEADS):
            start = (2 * j + first) * HEAD_SIZE
            parts.append(total[:, start : start + HEAD_SIZE])
        return jnp.concatenate(parts, axis=1)

    return (attention, query_grad, gradient(0), gradient(1))


def solution(mesh):
    spec = P(("seq", "head"), None)
    return jax.shard_map(
        functools.partial(on_device, mesh.shape["seq"], mesh.shape["head"]),
        mesh=mesh,
        in_specs=(spec, spec, spec, spec, P("seq", None)),
        out_specs=(spec, spec, spec, spec),
        check_vma=False,
    )
```

time: 94.6 us -> 83.5 us (0.88)
  waiting for transfers between devices: 37 us -> 23.3 us
  Pallas kernels: 21.7 us -> 25.7 us
  other arithmetic: 8.46 us -> 7 us
    ppermute x3 -> x2, waiting for transfers between devices: 13.5 us -> 4.74 us  [on_device(): got = lax.ppermute(held, 'seq', sends)]
    ppermute x15 -> x20, starting transfers between devices: 14 us -> 19.1 us  [the longest x15 8.71 us: send(): return lax.ppermute(x, 'head', [(i, i ^ mask) for i in range(head_count)])]
    ppermute x3 -> x2, starting transfers between devices: 8.48 us -> 3.44 us  [on_device(): got = lax.ppermute(held, 'seq', sends)]
    ppermute x15 -> x20, waiting for transfers between devices: 23.5 us -> 18.6 us  [the longest x3 9.36 us: on_device(): got = lax.ppermute(total, 'seq', sends)]
    pallas_call x4 -> x5, Pallas kernels: 21.7 us -> 25.7 us  [call(): pl.pallas_call(functools.partial(kernel, layout), grid_spec=pltpu.Prefetc...]
    convert_element_type x4, other arithmetic: 4.11 us -> 1.37 us  [the longest x1 1.02 us: on_device(): total = plus(terms, send(terms_far, 2)).astype(bf16)]
    concatenate x6 -> x7, other arithmetic: 0.45 us -> 2.09 us  [the longest x2 1.34 us: gradient(): return jnp.concatenate(parts, axis=1)]
    select_n x4 -> x3, other arithmetic: 3.64 us -> 2.37 us  [both_halves(): jnp.where(core == 0, jnp.concatenate([mine, theirs], axis=1), jnp.concate...]
  transfers between devices with their start and end apart: 18 -> 22, of which waited for: 9 -> 11; matrix products, arithmetic and copies ran while one was open for 6% -> 6% of each run, Pallas kernels for 23% -> 23%
where the time goes in v3:
time: 83.5 us; the launch traced here: 83.1 us
  Pallas kernels  25.7 us (31%)
  waiting for transfers between devices  23.3 us (28%)
  starting transfers between devices  22.5 us (27%)
  other arithmetic  7 us (8%)
  local copies, waits for them, and re-layouts  3.47 us (4%)
  between operations  1.11 us (1%)
    pallas_call x5, Pallas kernels, call(): pl.pallas_call(functools.partial(kernel, layout), grid_spec=pltpu.Prefetc...  25.7 us
    ppermute x3, waiting for transfers between devices, on_device(): got = lax.ppermute(total, 'seq', sends)  9.36 us
    ppermute x15, starting transfers between devices, send(): return lax.ppermute(x, 'head', [(i, i ^ mask) for i in range(head_count)])  8.71 us
    ppermute x2, starting transfers between devices, on_device(): got = jnp.concatenate([lax.ppermute(x, 'seq', sends) for x in held], axis=1)  6.31 us
    ppermute x15, waiting for transfers between devices, send(): return lax.ppermute(x, 'head', [(i, i ^ mask) for i in range(head_count)])  5.5 us
    ppermute x2, waiting for transfers between devices, on_device(): got = lax.ppermute(held, 'seq', sends)  4.74 us
    ppermute x3, starting transfers between devices, on_device(): got = lax.ppermute(total, 'seq', sends)  4.06 us
    ppermute x2, waiting for transfers between devices, on_device(): got = jnp.concatenate([lax.ppermute(x, 'seq', sends) for x in held], axis=1)  3.69 us
  transfers between devices with their start and end apart: 22, of which 11 were waited for; matrix products, arithmetic and copies ran while one was open for 6% of the time, Pallas kernels for 23%

profile of v3, /device:TPU:0, one launch (start us, length us, event | category | flops | bytes accessed | tf_op | source)
XLA Modules:
  0.0 83.1 jit_solution(3898498978440764086)
XLA Ops:
  0.6 0.0 copy-start.14
  0.6 5.0 %collective-permute-start.5 = (bf16[128,512]{1,0:T(8,128)(2,1)}, bf16[128,512]{1,0:T(8,128)(2,1)S(1)}, u32[]{:S(2)}, u32[]{:S(2)}) collective-permute-start(bf16[128,512]{1,0:T(8,128)(2,1)} %param.6), channel_id=1, source_target_pairs={{0,4},{1,5},{2,6},{3,7}} | collective-permute-start | bytes 393224 | tf_op jit(solution)/shard_map/ppermute | solution.py:270
  5.7 1.3 %collective-permute-start.6 = (bf16[128,512]{1,0:T(8,128)(2,1)}, bf16[128,512]{1,0:T(8,128)(2,1)S(1)}, u32[]{:S(2)}, u32[]{:S(2)}) collective-permute-start(bf16[128,512]{1,0:T(8,128)(2,1)} %param.7), channel_id=1, source_target_pairs={{0,4},{1,5},{2,6},{3,7}} | collective-permute-start | bytes 393224 | tf_op jit(solution)/shard_map/ppermute | solution.py:270
  7.0 0.8 constant_dynamic-slice_fusion.5
  7.8 2.0 %collective-permute-done.5 = bf16[128,512]{1,0:T(8,128)(2,1)S(1)} collective-permute-done((bf16[128,512]{1,0:T(8,128)(2,1)}, bf16[128,512]{1,0:T(8,128)(2,1)S(1)}, u32[]{:S(2)}, u32[]{:S(2)}) %collective-permute-start.5) | collective-permute-done | bytes 131104 | tf_op jit(solution)/shard_map/ppermute | solution.py:270
  9.9 1.7 %collective-permute-done.6 = bf16[128,512]{1,0:T(8,128)(2,1)S(1)} collective-permute-done((bf16[128,512]{1,0:T(8,128)(2,1)}, bf16[128,512]{1,0:T(8,128)(2,1)S(1)}, u32[]{:S(2)}, u32[]{:S(2)}) %collective-permute-start.6) | collective-permute-done | bytes 131104 | tf_op jit(solution)/shard_map/ppermute | solution.py:270
  11.5 1.0 %maximum_select_fusion.2 = bf16[128,1024]{1,0:T(8,128)(2,1)S(1)} fusion(bf16[128,512]{1,0:T(8,128)(2,1)S(1)} %collective-permute-done.6, bf16[128,512]{1,0:T(8,128)(2,1)S(1)} %collective-permute-done.5, bf16[128,512]{1,0:T(8,128)(2,1)} %param.7, bf16[128,512]{1,0:T(8,128)(2,1)} %param.6, pred[]{:T(512)S(6)} %eq.26), kind=kLoop, calls=%fused_computation.9 | loop fusion | flops 1179648 | bytes 786433 | tf_op jit(solution)/shard_map/jit(_where)/select_n | solution.py:272
  12.6 0.0 copy-start.1
  12.6 1.4 %collective-permute-start.7 = (bf16[128,1024]{1,0:T(8,128)(2,1)S(1)}, bf16[128,1024]{1,0:T(8,128)(2,1)S(1)}, u32[]{:S(2)}, u32[]{:S(2)}) collective-permute-start(bf16[128,1024]{1,0:T(8,128)(2,1)S(1)} %maximum_select_fusion.2), channel_id=1, source_target_pairs={{0,16},{4,20},{1,17},{5,21},{2,18},{6,22},{3,19},{7,23}} | collective-permute-start | bytes 786440 | tf_op jit(solution)/shard_map/ppermute | solution.py:267
  14.1 0.7 pad_maximum_fusion.2
  14.7 0.1 collective-permute-start.4
  14.8 1.5 %collective-permute-start.2 = (bf16[128,512]{1,0:T(8,128)(2,1)}, bf16[128,512]{1,0:T(8,128)(2,1)S(1)}, u32[]{:S(2)}, u32[]{:S(2)}) collective-permute-start(bf16[128,512]{1,0:T(8,128)(2,1)} %pad_maximum_fusion.2), channel_id=1, source_target_pairs={{0,1},{1,0},{2,3},{3,2},{4,5},{5,4},{6,7},{7,6},{8,9},{9,8},{10,11... | collective-permute-start | bytes 393224 | tf_op jit(solution)/shard_map/ppermute | solution.py:238
  16.4 0.0 copy-start
  16.4 0.6 collective-permute-start.3
  17.0 2.0 %collective-permute-done.7 = bf16[128,1024]{1,0:T(8,128)(2,1)S(1)} collective-permute-done((bf16[128,1024]{1,0:T(8,128)(2,1)S(1)}, bf16[128,1024]{1,0:T(8,128)(2,1)S(1)}, u32[]{:S(2)}, u32[]{:S(2)}) %collective-permute-start.7) | collective-permute-done | bytes 262176 | tf_op jit(solution)/shard_map/ppermute | solution.py:267
  19.0 2.0 %collective-permute-start.8 = (bf16[128,1024]{1,0:T(8,128)(2,1)S(1)}, bf16[128,1024]{1,0:T(8,128)(2,1)}, u32[]{:S(2)}, u32[]{:S(2)}) collective-permute-start(bf16[128,1024]{1,0:T(8,128)(2,1)S(1)} %broadcast_select_fusion), channel_id=1, source_target_pairs={{0,8},{16,24},{4,12},{20,28},{1,9},{17,25},{5,13},{21,29},{2,10},{... | collective-permute-start | bytes 786440 | tf_op jit(solution)/shard_map/ppermute | solution.py:267
  21.0 0.8 constant_dynamic-slice_fusion.16
  21.8 2.8 %collective-permute-done.8 = bf16[128,1024]{1,0:T(8,128)(2,1)} collective-permute-done((bf16[128,1024]{1,0:T(8,128)(2,1)S(1)}, bf16[128,1024]{1,0:T(8,128)(2,1)}, u32[]{:S(2)}, u32[]{:S(2)}) %collective-permute-start.8) | collective-permute-done | bytes 262176 | tf_op jit(solution)/shard_map/ppermute | solution.py:267
  24.6 0.0 copy-start.2
  24.7 0.1 constant_dynamic-slice_fusion
  24.8 0.0 copy-start.7
  24.8 0.6 copy-done.7
  25.4 0.5 collective-permute-start.9
  25.9 0.1 pad_add_fusion.ids
  26.1 0.0 copy-start.3
  26.1 1.2 %collective-permute-start.11 = (bf16[128,512]{1,0:T(8,128)(2,1)S(1)}, bf16[128,512]{1,0:T(8,128)(2,1)S(1)}, u32[]{:S(2)}, u32[]{:S(2)}) collective-permute-start(bf16[128,512]{1,0:T(8,128)(2,1)S(1)} %pad_maximum_fusion.4), channel_id=1, source_target_pairs={{0,3},{1,2},{2,1},{3,0},{4,7},{5,6},{6,5},{7,4},{8,11},{9,10},{10,... | collective-permute-start | bytes 393224 | tf_op jit(solution)/shard_map/ppermute | solution.py:238
  27.2 0.5 collective-permute-start.10
  27.8 0.0 copy-start.8
  27.8 0.9 %copy-done.8 = bf16[128,512]{1,0:T(8,128)(2,1)S(1)} copy-done((bf16[128,512]{1,0:T(8,128)(2,1)S(1)}, bf16[128,512]{1,0:T(8,128)(2,1)}, u32[]{:S(2)}) %copy-start.8) | copy-done | bytes 131096
  28.7 5.4 %shard_map.84.refs_2_ = f32[2,7,8,256]{3,2,1,0:T(8,128)S(1)} custom-call(s32[2]{0:T(128)S(1)} %pad_add_fusion.ids, s32[4,4]{1,0:T(4,128)S(1)} %copy-done.2, bf16[128,3584]{1,0:T(8,128)(2,1)S(1)} %copy-done, bf16[128,1792]{1,0:T(8,128)(2,1)S(1)} %collective-permute-done.qs, bf16[128,3584]{1,0:T(8,128)(2,1)S(1)} %copy-done.1, ...), custom_call_target="tpu_custom_call" | custom-call | flops 1409286144 | bytes 3670016 | tf_op jit(solution)/shard_map/pallas_call | solution.py:207
  34.1 0.6 collective-permute-done.10.refs_0_.refs_6_
  34.7 6.3 %shard_map.85 = (f32[2,7,8,256]{3,2,1,0:T(8,128)S(1)}, bf16[256,512]{1,0:T(8,128)(2,1)S(1)}) custom-call(s32[2]{0:T(128)S(1)} %pad_add_fusion.ids, s32[4,4]{1,0:T(4,128)S(1)} %copy-done.2, bf16[128,3584]{1,0:T(8,128)(2,1)S(1)} %copy-done, bf16[128,1792]{1,0:T(8,128)(2,1)S(1)} %collective-permute-done.qs, bf16[128,3584]{1,0:T(8,128)(2,1)S(1)} %copy-done.1, ...), custom_call_target="tpu_custom_call" | custom-call | flops 939524096 | bytes 3670016 | tf_op jit(solution)/shard_map/pallas_call | solution.py:207
  41.1 1.6 %collective-permute-start.12 = (bf16[256,512]{1,0:T(8,128)(2,1)S(1)}, bf16[256,512]{1,0:T(8,128)(2,1)}, u32[]{:S(2)}, u32[]{:S(2)}) collective-permute-start(bf16[256,512]{1,0:T(8,128)(2,1)S(1)} %get-tuple-element.21), channel_id=1, source_target_pairs={{0,2},{1,3},{2,0},{3,1},{4,6},{5,7},{6,4},{7,5},{8,10},{9,11},{10,... | collective-permute-start | bytes 786440 | tf_op jit(solution)/shard_map/ppermute | solution.py:238
  42.7 4.3 %shard_map.86 = f32[256,512]{1,0:T(8,128)S(1)} custom-call(s32[2]{0:T(128)S(1)} %pad_add_fusion.ids, s32[4,4]{1,0:T(4,128)S(1)} %copy-done.2, bf16[128,3584]{1,0:T(8,128)(2,1)S(1)} %copy-done, bf16[128,1792]{1,0:T(8,128)(2,1)S(1)} %collective-permute-done.qs, bf16[128,3584]{1,0:T(8,128)(2,1)S(1)} %copy-done.1, ...), custom_call_target="tpu_custom_call" | custom-call | flops 939524096 | bytes 3670016 | tf_op jit(solution)/shard_map/pallas_call | solution.py:207
  47.0 0.0 copy-start.4
  47.0 0.0 copy-start.6
  47.0 0.0 copy-start.9
  47.0 0.0 copy-start.13
  47.0 2.4 %collective-permute-done.12 = bf16[256,512]{1,0:T(8,128)(2,1)} collective-permute-done((bf16[256,512]{1,0:T(8,128)(2,1)S(1)}, bf16[256,512]{1,0:T(8,128)(2,1)}, u32[]{:S(2)}, u32[]{:S(2)}) %collective-permute-start.12) | collective-permute-done | bytes 262176 | tf_op jit(solution)/shard_map/ppermute | solution.py:238
  49.4 1.0 %add_convert_fusion.3.refs_9_ = bf16[256,512]{1,0:T(8,128)(2,1)S(1)} fusion(f32[256,512]{1,0:T(8,128)S(1)} %shard_map.86, bf16[256,512]{1,0:T(8,128)(2,1)} %collective-permute-done.12), kind=kLoop, calls=%fused_computation.8 | loop fusion | flops 393216 | bytes 1048576 | tf_op jit(solution)/shard_map/convert_element_type | solution.py:313
  50.4 1.5 %collective-permute-start.13 = (bf16[256,512]{1,0:T(8,128)(2,1)S(1)}, bf16[256,512]{1,0:T(8,128)(2,1)S(1)}, u32[]{:S(2)}, u32[]{:S(2)}) collective-permute-start(bf16[256,512]{1,0:T(8,128)(2,1)S(1)} %add_convert_fusion.3.refs_9_), channel_id=1, source_target_pairs={{4,0},{12,8},{20,16},{28,24},{5,1},{13,9},{21,17},{29,25},{6,2},{1... | collective-permute-start | bytes 786440 | tf_op jit(solution)/shard_map/ppermute | solution.py:320
  52.0 4.8 %shard_map.87 = (bf16[128,896]{1,0:T(8,128)(2,1)S(1)}, bf16[128,896]{1,0:T(8,128)(2,1)S(1)}, bf16[128,896]{1,0:T(8,128)(2,1)S(1)}, bf16[128,896]{1,0:T(8,128)(2,...) custom-call(s32[2]{0:T(128)S(1)} %pad_add_fusion.ids, ...), custom_call_target="tpu_custom_call" | custom-call | flops 3758096384 | bytes 1835008 | tf_op jit(solution)/shard_map/pallas_call | solution.py:207
  56.8 0.1 collective-permute-start.14
  56.9 0.5 collective-permute-start.16
  57.4 2.2 %collective-permute-done.13 = bf16[256,512]{1,0:T(8,128)(2,1)S(1)} collective-permute-done((bf16[256,512]{1,0:T(8,128)(2,1)S(1)}, bf16[256,512]{1,0:T(8,128)(2,1)S(1)}, u32[]{:S(2)}, u32[]{:S(2)}) %collective-permute-start.13) | collective-permute-done | bytes 262176 | tf_op jit(solution)/shard_map/ppermute | solution.py:320
  59.6 0.1 add_convert_fusion.2.refs_9_
  59.7 1.3 %collective-permute-start.19 = (bf16[256,512]{1,0:T(8,128)(2,1)S(1)}, bf16[256,512]{1,0:T(8,128)(2,1)S(1)}, u32[]{:S(2)}, u32[]{:S(2)}) collective-permute-start(bf16[256,512]{1,0:T(8,128)(2,1)S(1)} %add_convert_fusion.2.refs_9_), channel_id=1, source_target_pairs={{8,0},{24,16},{9,1},{25,17},{10,2},{26,18},{11,3},{27,19}} | collective-permute-start | bytes 786440 | tf_op jit(solution)/shard_map/ppermute | solution.py:320
  61.0 4.8 %shard_map.88 = (bf16[128,896]{1,0:T(8,128)(2,1)S(1)}, bf16[128,896]{1,0:T(8,128)(2,1)S(1)}, bf16[128,896]{1,0:T(8,128)(2,1)S(1)}, bf16[128,896]{1,0:T(8,128)(2,...) custom-call(s32[2]{0:T(128)S(1)} %pad_add_fusion.ids, ...), custom_call_target="tpu_custom_call" | custom-call | flops 3758096384 | bytes 1835008 | tf_op jit(solution)/shard_map/pallas_call | solution.py:207
  65.9 0.1 collective-permute-start.15
  66.0 0.5 collective-permute-start.17
  66.5 2.7 %collective-permute-done.19 = bf16[256,512]{1,0:T(8,128)(2,1)S(1)} collective-permute-done((bf16[256,512]{1,0:T(8,128)(2,1)S(1)}, bf16[256,512]{1,0:T(8,128)(2,1)S(1)}, u32[]{:S(2)}, u32[]{:S(2)}) %collective-permute-start.19) | collective-permute-done | bytes 262176 | tf_op jit(solution)/shard_map/ppermute | solution.py:320
  69.2 1.5 %collective-permute-start.18 = (bf16[256,512]{1,0:T(8,128)(2,1)S(1)}, bf16[256,512]{1,0:T(8,128)(2,1)S(1)}, u32[]{:S(2)}, u32[]{:S(2)}) collective-permute-start(bf16[256,512]{1,0:T(8,128)(2,1)S(1)} %pad_maximum_fusion), channel_id=1, source_target_pairs={{0,2},{1,3},{2,0},{3,1},{4,6},{5,7},{6,4},{7,5},{8,10},{9,11},{10,... | collective-permute-start | bytes 786440 | tf_op jit(solution)/shard_map/ppermute | solution.py:238
  70.7 0.1 add_convert_fusion.1
  70.8 1.3 %collective-permute-start.20 = (bf16[256,512]{1,0:T(8,128)(2,1)S(1)}, bf16[256,512]{1,0:T(8,128)(2,1)S(1)}, u32[]{:S(2)}, u32[]{:S(2)}) collective-permute-start(bf16[256,512]{1,0:T(8,128)(2,1)S(1)} %add_convert_fusion.1), channel_id=1, source_target_pairs={{16,0},{17,1},{18,2},{19,3}} | collective-permute-start | bytes 786440 | tf_op jit(solution)/shard_map/ppermute | solution.py:320
  72.1 1.1 %maximum_select_fusion = bf16[128,3584]{1,0:T(8,128)(2,1)} fusion(bf16[128,896]{1,0:T(8,128)(2,1)S(1)} %collective-permute-done.15, bf16[128,896]{1,0:T(8,128)(2,1)S(1)} %collective-permute-done.14, bf16[128,896]{1,0:T(8,128)(2,1)S(1)} %get-tuple-element.24, bf16[128,896]{1,0:T(8,128)(2,1)S(1)} %get-tuple-element.22, pred[]{:T(512)S(6)} %eq.23), kind=kLoop, calls=%fused_computation | loop fusion | flops 7798784 | bytes 1835009 | tf_op jit(solution)/shard_map/jit(_where)/select_n | solution.py:337
  73.3 2.3 %collective-permute-done.18 = bf16[256,512]{1,0:T(8,128)(2,1)S(1)} collective-permute-done((bf16[256,512]{1,0:T(8,128)(2,1)S(1)}, bf16[256,512]{1,0:T(8,128)(2,1)S(1)}, u32[]{:S(2)}, u32[]{:S(2)}) %collective-permute-start.18) | collective-permute-done | bytes 262176 | tf_op jit(solution)/shard_map/ppermute | solution.py:238
  75.5 4.4 %collective-permute-done.20 = bf16[256,512]{1,0:T(8,128)(2,1)S(1)} collective-permute-done((bf16[256,512]{1,0:T(8,128)(2,1)S(1)}, bf16[256,512]{1,0:T(8,128)(2,1)S(1)}, u32[]{:S(2)}, u32[]{:S(2)}) %collective-permute-start.20) | collective-permute-done | bytes 262176 | tf_op jit(solution)/shard_map/ppermute | solution.py:320
  80.0 0.1 fusion.1
  80.2 0.1 collective-permute-start.21
  80.3 1.2 %maximum_select_fusion.1 = bf16[128,3584]{1,0:T(8,128)(2,1)} fusion(bf16[128,896]{1,0:T(8,128)(2,1)S(1)} %collective-permute-done.17, bf16[128,896]{1,0:T(8,128)(2,1)S(1)} %collective-permute-done.16, bf16[128,896]{1,0:T(8,128)(2,1)S(1)} %get-tuple-element.28, bf16[128,896]{1,0:T(8,128)(2,1)S(1)} %get-tuple-element.27, pred[]{:T(512)S(6)} %eq.23), kind=kLoop, calls=%fused_computation.1 | loop fusion | flops 7798784 | bytes 1835009 | tf_op jit(solution)/shard_map/jit(_where)/select_n | solution.py:337
  81.4 0.2 collective-permute-done.21
  81.6 0.1 maximum_select_fusion.3
  81.7 0.7 pad_maximum_fusion.6
  82.4 0.7 pad_maximum_fusion.5
  (41 shorter events, 0.4 us)
Async XLA Ops:
  0.6 13.4 %copy-start.14 = (bf16[128,512]{1,0:T(8,128)(2,1)S(1)}, bf16[128,512]{1,0:T(8,128)(2,1)}, u32[]{:S(2)}) copy-start(bf16[128,512]{1,0:T(8,128)(2,1)} %param.7) | copy-start | bytes 393220
  0.6 9.2 %collective-permute-start.5 = (bf16[128,512]{1,0:T(8,128)(2,1)}, bf16[128,512]{1,0:T(8,128)(2,1)S(1)}, u32[]{:S(2)}, u32[]{:S(2)}) collective-permute-start(bf16[128,512]{1,0:T(8,128)(2,1)} %param.6), channel_id=1, source_target_pairs={{0,4},{1,5},{2,6},{3,7}} | collective-permute-start | bytes 393224 | tf_op jit(solution)/shard_map/ppermute | solution.py:270
  5.7 5.9 %collective-permute-start.6 = (bf16[128,512]{1,0:T(8,128)(2,1)}, bf16[128,512]{1,0:T(8,128)(2,1)S(1)}, u32[]{:S(2)}, u32[]{:S(2)}) collective-permute-start(bf16[128,512]{1,0:T(8,128)(2,1)} %param.7), channel_id=1, source_target_pairs={{0,4},{1,5},{2,6},{3,7}} | collective-permute-start | bytes 393224 | tf_op jit(solution)/shard_map/ppermute | solution.py:270
  12.6 8.4 %copy-start.1 = (bf16[128,3584]{1,0:T(8,128)(2,1)S(1)}, bf16[128,3584]{1,0:T(8,128)(2,1)}, u32[]{:S(2)}) copy-start(bf16[128,3584]{1,0:T(8,128)(2,1)} %cm.9) | copy-start | bytes 2752516
  12.6 6.4 %collective-permute-start.7 = (bf16[128,1024]{1,0:T(8,128)(2,1)S(1)}, bf16[128,1024]{1,0:T(8,128)(2,1)S(1)}, u32[]{:S(2)}, u32[]{:S(2)}) collective-permute-start(bf16[128,1024]{1,0:T(8,128)(2,1)S(1)} %maximum_select_fusion.2), channel_id=1, source_target_pairs={{0,16},{4,20},{1,17},{5,21},{2,18},{6,22},{3,19},{7,23}} | collective-permute-start | bytes 786440 | tf_op jit(solution)/shard_map/ppermute | solution.py:267
  14.7 11.3 %collective-permute-start.4 = (bf16[128,512]{1,0:T(8,128)(2,1)}, bf16[128,512]{1,0:T(8,128)(2,1)S(1)}, u32[]{:S(2)}, u32[]{:S(2)}) collective-permute-start(bf16[128,512]{1,0:T(8,128)(2,1)} %pad_maximum_fusion.2), channel_id=1, source_target_pairs={{0,3},{1,2},{2,1},{3,0},{4,7},{5,6},{6,5},{7,4},{8,11},{9,10},{10,... | collective-permute-start | bytes 393224 | tf_op jit(solution)/shard_map/ppermute | solution.py:238
  14.8 12.4 %collective-permute-start.2 = (bf16[128,512]{1,0:T(8,128)(2,1)}, bf16[128,512]{1,0:T(8,128)(2,1)S(1)}, u32[]{:S(2)}, u32[]{:S(2)}) collective-permute-start(bf16[128,512]{1,0:T(8,128)(2,1)} %pad_maximum_fusion.2), channel_id=1, source_target_pairs={{0,1},{1,0},{2,3},{3,2},{4,5},{5,4},{6,7},{7,6},{8,9},{9,8},{10,11... | collective-permute-start | bytes 393224 | tf_op jit(solution)/shard_map/ppermute | solution.py:238
  16.4 5.4 %copy-start = (bf16[128,3584]{1,0:T(8,128)(2,1)S(1)}, bf16[128,3584]{1,0:T(8,128)(2,1)}, u32[]{:S(2)}) copy-start(bf16[128,3584]{1,0:T(8,128)(2,1)} %qm.9) | copy-start | bytes 2752516
  16.4 8.4 %collective-permute-start.3 = (bf16[128,512]{1,0:T(8,128)(2,1)S(1)}, bf16[128,512]{1,0:T(8,128)(2,1)S(1)}, u32[]{:S(2)}, u32[]{:S(2)}) collective-permute-start(bf16[128,512]{1,0:T(8,128)(2,1)S(1)} %pad_maximum_fusion.1.refs_0_), channel_id=1, source_target_pairs={{0,2},{1,3},{2,0},{3,1},{4,6},{5,7},{6,4},{7,5},{8,10},{9,11},{10,... | collective-permute-start | bytes 393224 | tf_op jit(solution)/shard_map/ppermute | solution.py:238
  19.0 5.6 %collective-permute-start.8 = (bf16[128,1024]{1,0:T(8,128)(2,1)S(1)}, bf16[128,1024]{1,0:T(8,128)(2,1)}, u32[]{:S(2)}, u32[]{:S(2)}) collective-permute-start(bf16[128,1024]{1,0:T(8,128)(2,1)S(1)} %broadcast_select_fusion), channel_id=1, source_target_pairs={{0,8},{16,24},{4,12},{20,28},{1,9},{17,25},{5,13},{21,29},{2,10},{... | collective-permute-start | bytes 786440 | tf_op jit(solution)/shard_map/ppermute | solution.py:267
  21.8 6.0 %collective-permute-start.1 = (bf16[128,1792]{1,0:T(8,128)(2,1)}, bf16[128,1792]{1,0:T(8,128)(2,1)S(1)}, u32[]{:S(2)}, u32[]{:S(2)}) collective-permute-start(bf16[128,1792]{1,0:T(8,128)(2,1)} %constant_dynamic-slice_fusion.16), channel_id=1, source_target_pairs={{0,1},{1,0},{2,3},{3,2},{4,5},{5,4},{6,7},{7,6},{8,9},{9,8},{10,11... | collective-permute-start | bytes 1376264 | tf_op jit(solution)/shard_map/ppermute | solution.py:238
  24.6 3.2 %collective-permute-start = (bf16[128,1792]{1,0:T(8,128)(2,1)S(1)}, bf16[128,1792]{1,0:T(8,128)(2,1)S(1)}, u32[]{:S(2)}, u32[]{:S(2)}) collective-permute-start(bf16[128,1792]{1,0:T(8,128)(2,1)S(1)} %constant_dynamic-slice_fusion.17), channel_id=1, source_target_pairs={{0,1},{1,0},{2,3},{3,2},{4,5},{5,4},{6,7},{7,6},{8,9},{9,8},{10,11... | collective-permute-start | bytes 1376264 | tf_op jit(solution)/shard_map/ppermute | solution.py:238
  24.6 3.1 %copy-start.2 = (s32[4,4]{1,0:T(4,128)S(1)}, s32[4,4]{1,0:T(4,128)}, u32[]{:S(2)}) copy-start(s32[4,4]{1,0:T(4,128)} %tree.9) | copy-start | bytes 196
  24.8 0.7 copy-start.7
  25.4 2.3 %collective-permute-start.9 = (bf16[128,512]{1,0:T(8,128)(2,1)S(1)}, bf16[128,512]{1,0:T(8,128)(2,1)S(1)}, u32[]{:S(2)}, u32[]{:S(2)}) collective-permute-start(bf16[128,512]{1,0:T(8,128)(2,1)S(1)} %pad_maximum_fusion.4), channel_id=1, source_target_pairs={{0,1},{1,0},{2,3},{3,2},{4,5},{5,4},{6,7},{7,6},{8,9},{9,8},{10,11... | collective-permute-start | bytes 393224 | tf_op jit(solution)/shard_map/ppermute | solution.py:238
  26.1 8.0 %copy-start.3 = (bf16[128,512]{1,0:T(8,128)(2,1)}, bf16[128,512]{1,0:T(8,128)(2,1)S(1)}, u32[]{:S(2)}) copy-start(bf16[128,512]{1,0:T(8,128)(2,1)S(1)} %collective-permute-done.4.refs_3_) | copy-start | bytes 393220
  26.1 8.7 %collective-permute-start.11 = (bf16[128,512]{1,0:T(8,128)(2,1)S(1)}, bf16[128,512]{1,0:T(8,128)(2,1)S(1)}, u32[]{:S(2)}, u32[]{:S(2)}) collective-permute-start(bf16[128,512]{1,0:T(8,128)(2,1)S(1)} %pad_maximum_fusion.4), channel_id=1, source_target_pairs={{0,3},{1,2},{2,1},{3,0},{4,7},{5,6},{6,5},{7,4},{8,11},{9,10},{10,... | collective-permute-start | bytes 393224 | tf_op jit(solution)/shard_map/ppermute | solution.py:238
  27.2 6.9 %copy-start.5 = (bf16[128,512]{1,0:T(8,128)(2,1)}, bf16[128,512]{1,0:T(8,128)(2,1)S(1)}, u32[]{:S(2)}) copy-start(bf16[128,512]{1,0:T(8,128)(2,1)S(1)} %collective-permute-done.2.refs_1_) | copy-start | bytes 393220
  27.2 7.5 %collective-permute-start.10 = (bf16[128,512]{1,0:T(8,128)(2,1)S(1)}, bf16[128,512]{1,0:T(8,128)(2,1)S(1)}, u32[]{:S(2)}, u32[]{:S(2)}) collective-permute-start(bf16[128,512]{1,0:T(8,128)(2,1)S(1)} %pad_maximum_fusion.3.refs_4_.refs_0_), channel_id=1, source_target_pairs={{0,2},{1,3},{2,0},{3,1},{4,6},{5,7},{6,4},{7,5},{8,10},{9,11},{10,... | collective-permute-start | bytes 393224 | tf_op jit(solution)/shard_map/ppermute | solution.py:238
  27.8 0.9 %copy-start.8 = (bf16[128,512]{1,0:T(8,128)(2,1)S(1)}, bf16[128,512]{1,0:T(8,128)(2,1)}, u32[]{:S(2)}) copy-start(bf16[128,512]{1,0:T(8,128)(2,1)} %copy-done.7) | copy-start | bytes 393220
  34.7 6.4 %copy-start.12 = (bf16[128,512]{1,0:T(8,128)(2,1)}, bf16[128,512]{1,0:T(8,128)(2,1)S(1)}, u32[]{:S(2)}) copy-start(bf16[128,512]{1,0:T(8,128)(2,1)S(1)} %collective-permute-done.10.refs_0_.refs_6_) | copy-start | bytes 393220
  34.7 6.4 %copy-start.10 = (bf16[128,512]{1,0:T(8,128)(2,1)}, bf16[128,512]{1,0:T(8,128)(2,1)S(1)}, u32[]{:S(2)}) copy-start(bf16[128,512]{1,0:T(8,128)(2,1)S(1)} %collective-permute-done.11.refs_1_.refs_7_) | copy-start | bytes 393220
  41.1 8.3 %collective-permute-start.12 = (bf16[256,512]{1,0:T(8,128)(2,1)S(1)}, bf16[256,512]{1,0:T(8,128)(2,1)}, u32[]{:S(2)}, u32[]{:S(2)}) collective-permute-start(bf16[256,512]{1,0:T(8,128)(2,1)S(1)} %get-tuple-element.21), channel_id=1, source_target_pairs={{0,2},{1,3},{2,0},{3,1},{4,6},{5,7},{6,4},{7,5},{8,10},{9,11},{10,... | collective-permute-start | bytes 786440 | tf_op jit(solution)/shard_map/ppermute | solution.py:238
  47.0 5.0 %copy-start.4 = (bf16[128,512]{1,0:T(8,128)(2,1)S(1)}, bf16[128,512]{1,0:T(8,128)(2,1)}, u32[]{:S(2)}) copy-start(bf16[128,512]{1,0:T(8,128)(2,1)} %copy-done.3) | copy-start | bytes 393220
  47.0 5.0 %copy-start.6 = (bf16[128,512]{1,0:T(8,128)(2,1)S(1)}, bf16[128,512]{1,0:T(8,128)(2,1)}, u32[]{:S(2)}) copy-start(bf16[128,512]{1,0:T(8,128)(2,1)} %copy-done.5) | copy-start | bytes 393220
  47.0 4.9 %copy-start.9 = (bf16[128,512]{1,0:T(8,128)(2,1)S(1)}, bf16[128,512]{1,0:T(8,128)(2,1)}, u32[]{:S(2)}) copy-start(bf16[128,512]{1,0:T(8,128)(2,1)} %copy-done.7) | copy-start | bytes 393220
  47.0 4.9 %copy-start.11 = (bf16[128,512]{1,0:T(8,128)(2,1)S(1)}, bf16[128,512]{1,0:T(8,128)(2,1)}, u32[]{:S(2)}) copy-start(bf16[128,512]{1,0:T(8,128)(2,1)} %copy-done.10) | copy-start | bytes 393220
  47.0 4.9 %copy-start.13 = (bf16[128,512]{1,0:T(8,128)(2,1)S(1)}, bf16[128,512]{1,0:T(8,128)(2,1)}, u32[]{:S(2)}) copy-start(bf16[128,512]{1,0:T(8,128)(2,1)} %copy-done.12) | copy-start | bytes 393220
  50.4 9.2 %collective-permute-start.13 = (bf16[256,512]{1,0:T(8,128)(2,1)S(1)}, bf16[256,512]{1,0:T(8,128)(2,1)S(1)}, u32[]{:S(2)}, u32[]{:S(2)}) collective-permute-start(bf16[256,512]{1,0:T(8,128)(2,1)S(1)} %add_convert_fusion.3.refs_9_), channel_id=1, source_target_pairs={{4,0},{12,8},{20,16},{28,24},{5,1},{13,9},{21,17},{29,25},{6,2},{1... | collective-permute-start | bytes 786440 | tf_op jit(solution)/shard_map/ppermute | solution.py:320
  56.8 14.0 %collective-permute-start.14 = (bf16[128,896]{1,0:T(8,128)(2,1)S(1)}, bf16[128,896]{1,0:T(8,128)(2,1)S(1)}, u32[]{:S(2)}, u32[]{:S(2)}) collective-permute-start(bf16[128,896]{1,0:T(8,128)(2,1)S(1)} %get-tuple-element.25), channel_id=1, source_target_pairs={{0,1},{1,0},{2,3},{3,2},{4,5},{5,4},{6,7},{7,6},{8,9},{9,8},{10,11... | collective-permute-start | bytes 688136 | tf_op jit(solution)/shard_map/ppermute | solution.py:238
  56.9 23.3 %collective-permute-start.16 = (bf16[128,896]{1,0:T(8,128)(2,1)S(1)}, bf16[128,896]{1,0:T(8,128)(2,1)S(1)}, u32[]{:S(2)}, u32[]{:S(2)}) collective-permute-start(bf16[128,896]{1,0:T(8,128)(2,1)S(1)} %get-tuple-element.29), channel_id=1, source_target_pairs={{0,1},{1,0},{2,3},{3,2},{4,5},{5,4},{6,7},{7,6},{8,9},{9,8},{10,11... | collective-permute-start | bytes 688136 | tf_op jit(solution)/shard_map/ppermute | solution.py:238
  59.7 9.4 %collective-permute-start.19 = (bf16[256,512]{1,0:T(8,128)(2,1)S(1)}, bf16[256,512]{1,0:T(8,128)(2,1)S(1)}, u32[]{:S(2)}, u32[]{:S(2)}) collective-permute-start(bf16[256,512]{1,0:T(8,128)(2,1)S(1)} %add_convert_fusion.2.refs_9_), channel_id=1, source_target_pairs={{8,0},{24,16},{9,1},{25,17},{10,2},{26,18},{11,3},{27,19}} | collective-permute-start | bytes 786440 | tf_op jit(solution)/shard_map/ppermute | solution.py:320
  65.9 6.2 %collective-permute-start.15 = (bf16[128,896]{1,0:T(8,128)(2,1)S(1)}, bf16[128,896]{1,0:T(8,128)(2,1)S(1)}, u32[]{:S(2)}, u32[]{:S(2)}) collective-permute-start(bf16[128,896]{1,0:T(8,128)(2,1)S(1)} %get-tuple-element.26), channel_id=1, source_target_pairs={{0,1},{1,0},{2,3},{3,2},{4,5},{5,4},{6,7},{7,6},{8,9},{9,8},{10,11... | collective-permute-start | bytes 688136 | tf_op jit(solution)/shard_map/ppermute | solution.py:238
  66.0 14.3 %collective-permute-start.17 = (bf16[128,896]{1,0:T(8,128)(2,1)S(1)}, bf16[128,896]{1,0:T(8,128)(2,1)S(1)}, u32[]{:S(2)}, u32[]{:S(2)}) collective-permute-start(bf16[128,896]{1,0:T(8,128)(2,1)S(1)} %get-tuple-element.30), channel_id=1, source_target_pairs={{0,1},{1,0},{2,3},{3,2},{4,5},{5,4},{6,7},{7,6},{8,9},{9,8},{10,11... | collective-permute-start | bytes 688136 | tf_op jit(solution)/shard_map/ppermute | solution.py:238
  69.2 6.4 %collective-permute-start.18 = (bf16[256,512]{1,0:T(8,128)(2,1)S(1)}, bf16[256,512]{1,0:T(8,128)(2,1)S(1)}, u32[]{:S(2)}, u32[]{:S(2)}) collective-permute-start(bf16[256,512]{1,0:T(8,128)(2,1)S(1)} %pad_maximum_fusion), channel_id=1, source_target_pairs={{0,2},{1,3},{2,0},{3,1},{4,6},{5,7},{6,4},{7,5},{8,10},{9,11},{10,... | collective-permute-start | bytes 786440 | tf_op jit(solution)/shard_map/ppermute | solution.py:238
  70.8 9.2 %collective-permute-start.20 = (bf16[256,512]{1,0:T(8,128)(2,1)S(1)}, bf16[256,512]{1,0:T(8,128)(2,1)S(1)}, u32[]{:S(2)}, u32[]{:S(2)}) collective-permute-start(bf16[256,512]{1,0:T(8,128)(2,1)S(1)} %add_convert_fusion.1), channel_id=1, source_target_pairs={{16,0},{17,1},{18,2},{19,3}} | collective-permute-start | bytes 786440 | tf_op jit(solution)/shard_map/ppermute | solution.py:320
  80.2 1.4 %collective-permute-start.21 = (bf16[128,512]{1,0:T(8,128)(2,1)S(1)}, bf16[128,512]{1,0:T(8,128)(2,1)S(1)}, u32[]{:S(2)}, u32[]{:S(2)}) collective-permute-start(bf16[128,512]{1,0:T(8,128)(2,1)S(1)} %get-tuple-element.45), channel_id=1, source_target_pairs={{0,1},{1,0},{2,3},{3,2},{4,5},{5,4},{6,7},{7,6},{8,9},{9,8},{10,11... | collective-permute-start | bytes 393224 | tf_op jit(solution)/shard_map/ppermute | solution.py:238

commit v4 on v3

v4 whole, which is shorter than its diff:
```python
import functools
import math

import jax
import jax.numpy as jnp
from jax import lax
from jax.experimental import pallas as pl
from jax.experimental.pallas import tpu as pltpu
from jax.sharding import PartitionSpec as P

QUERY_HEADS = 28
KEY_VALUE_HEADS = 4
HEAD_SIZE = 128
GROUP = QUERY_HEADS // KEY_VALUE_HEADS
WIDTH = GROUP * HEAD_SIZE
HEADS = KEY_VALUE_HEADS // 2
SCALE = HEAD_SIZE ** (-0.5)
EXP2_SCALE = SCALE * math.log2(math.e)
MASKED = -1e30
VMEM_BYTES = 16 * 1024 * 1024


def dot_nt(a, b):
    return lax.dot_general(a, b, (((1,), (1,)), ((), ())), preferred_element_type=jnp.float32)


def dot_nn(a, b):
    return lax.dot_general(a, b, (((1,), (0,)), ((), ())), preferred_element_type=jnp.float32)


def group_rows(mine, sibling):
    parts = []
    for g in range(GROUP):
        columns = slice(g * HEAD_SIZE, (g + 1) * HEAD_SIZE)
        parts += [mine[:, columns], sibling[:, columns]]
    return jnp.concatenate(parts, axis=0)


def per_head(x):
    return jnp.concatenate([x] * GROUP, axis=1)


def own_bias(place, rows, ids, tree):
    h = ids[0]
    if place < 2:
        lane = lax.broadcasted_iota(jnp.int32, (rows, rows), 1)
        sub = lax.broadcasted_iota(jnp.int32, (rows, rows), 0)
        parts = []
        for a in range(2):
            ahead = lane - sub >= ((h ^ place) - (h ^ a)) * rows
            parts.append(jnp.where(ahead, jnp.float32(0.0), jnp.float32(MASKED)))
        return jnp.concatenate(parts, axis=1)
    return block_bias([(h ^ place) <= (h ^ a) for a in range(2)], rows)


def prompt_bias(place, rows, ids, tree):
    h, s = ids[0], ids[1]
    return block_bias([jnp.logical_and(tree[h ^ a, h ^ place] > 0, s > 0) for a in range(2)], rows)


def block_bias(reads, rows):
    lane = lax.broadcasted_iota(jnp.int32, (1, 2 * rows), 1)
    bias = [jnp.where(r, jnp.float32(0.0), jnp.float32(MASKED)) for r in reads]
    return jnp.where(lane < rows, bias[0], bias[1])


class Keys:
    def __init__(self, layout, ids, tree, qm, qs, cm, cs, refs):
        self.rows = qm.shape[0]
        self.q = group_rows(qm, qs)
        self.ct = group_rows(cm, cs)
        count = len(layout)
        self.keys = jnp.concatenate([b[:, :HEAD_SIZE] for b in refs[:count]], axis=0)
        self.values = jnp.concatenate([b[:, HEAD_SIZE:] for b in refs[:count]], axis=0)
        self.refs = refs[count:]
        self.bias = [bias(place, self.rows, ids, tree) for bias, place in layout]

    def blocks(self, x):
        return [x[i * self.rows : (i + 1) * self.rows] for i in range(len(self.bias))]

    def scores(self):
        out = []
        for x, bias in zip(self.blocks(dot_nt(self.keys, self.q)), self.bias):
            out.append(x if bias.shape[0] == 1 else x + per_head(bias))
        return out

    def dprobs(self):
        return self.blocks(dot_nt(self.values, self.ct))

    def top(self, scores):
        tops = []
        for x, bias in zip(scores, self.bias):
            top = jnp.max(x, axis=0, keepdims=True)
            tops.append(top + per_head(bias) if bias.shape[0] == 1 else top)
        return functools.reduce(jnp.maximum, tops)

    def weights(self, scores, top):
        out = []
        for x, bias in zip(scores, self.bias):
            row = top - per_head(bias) if bias.shape[0] == 1 else top
            out.append(jnp.exp2((x - row) * EXP2_SCALE))
        return out


def column_sum(parts):
    return functools.reduce(jnp.add, [jnp.sum(x, axis=0, keepdims=True) for x in parts])


def put_stats(stats, top, total, delta):
    stats[0, 0:1, :] = top
    stats[0, 1:2, :] = total
    stats[0, 2:3, :] = delta


def put_terms(out, dscore, probs, k):
    out[:, :HEAD_SIZE] = (dot_nn(dscore, k.q) * SCALE).astype(out.dtype)
    out[:, HEAD_SIZE:] = dot_nn(probs, k.ct).astype(out.dtype)


def rounded(parts):
    return jnp.concatenate([x.astype(jnp.bfloat16) for x in parts], axis=0)


def stats_kernel(layout, ids, tree, qm, qs, cm, cs, *refs):
    k = Keys(layout, ids, tree, qm, qs, cm, cs, refs)
    (stats,) = k.refs
    scores = k.scores()
    top = k.top(scores)
    e = k.weights(scores, top)
    delta = column_sum([x * y for x, y in zip(e, k.dprobs())])
    put_stats(stats, top, column_sum(e), delta)


def last_keys_kernel(layout, ids, tree, qm, qs, cm, cs, *refs):
    k = Keys(layout, ids, tree, qm, qs, cm, cs, refs)
    old, stats, terms = k.refs
    scores, dprobs = k.scores(), k.dprobs()
    old_top = old[0, 0:1, :]
    top = jnp.maximum(k.top(scores), old_top)
    keep = jnp.exp2((old_top - top) * EXP2_SCALE)
    e = k.weights(scores, top)
    inverse = 1.0 / (column_sum(e) + old[0, 1:2, :] * keep)
    delta = column_sum([x * y for x, y in zip(e, dprobs)]) + old[0, 2:3, :] * keep
    delta = delta * inverse
    put_stats(stats, top, inverse, delta)
    probs = [x * inverse for x in e]
    put_terms(terms, rounded([p * (d - delta) for p, d in zip(probs, dprobs)]), rounded(probs), k)


def probs_dscore(k, stats):
    inverse, delta = stats[0, 1:2, :], stats[0, 2:3, :]
    probs = [x * inverse for x in k.weights(k.scores(), stats[0, 0:1, :])]
    dscore = [p * (d - delta) for p, d in zip(probs, k.dprobs())]
    return rounded(probs), rounded(dscore)


def terms_kernel(layout, ids, tree, qm, qs, cm, cs, *refs):
    k = Keys(layout, ids, tree, qm, qs, cm, cs, refs)
    stats, terms = k.refs
    probs, dscore = probs_dscore(k, stats)
    put_terms(terms, dscore, probs, k)


def rows_kernel(layout, ids, tree, qm, qs, cm, cs, *refs):
    k = Keys(layout, ids, tree, qm, qs, cm, cs, refs)
    stats, _, att_m, att_s, dq_m, dq_s, near, far, token = k.refs
    token[...] = jnp.zeros_like(token)
    rows = k.rows
    probs, dscore = probs_dscore(k, stats)
    half = near.shape[0]
    put_terms(near, dscore[:half], probs[:half], k)
    put_terms(far, dscore[half : 2 * half], probs[half : 2 * half], k)
    att = dot_nn(k.values.T, probs)
    dq = dot_nn(k.keys.T, dscore) * SCALE
    for g in range(GROUP):
        columns = slice(g * HEAD_SIZE, (g + 1) * HEAD_SIZE)
        for i, (a, d) in enumerate(((att_m, dq_m), (att_s, dq_s))):
            part = slice((2 * g + i) * rows, (2 * g + i + 1) * rows)
            a[:, columns] = att[:, part].T.astype(jnp.bfloat16)
            d[:, columns] = dq[:, part].T.astype(jnp.bfloat16)


def call(kernel, layout, heads, scalars, work, blocks, inputs, outs, products, tie=None):
    rows = work[0].shape[0]
    first, count = heads

    def spec(shape, base):
        if len(shape) == 2:
            return pl.BlockSpec((shape[0], shape[1] // (HEADS if base is not None else count)), lambda i, *refs: (0, i + (base or 0)))
        return pl.BlockSpec((1, *shape[1:]), lambda i, *refs: (i + (base or 0),) + (0,) * (len(shape) - 1))

    sib = spec((rows, HEADS * WIDTH), first)
    specs = [sib] * 4 + [spec(x.shape, first) for x in (*blocks, *inputs)]
    operands = [*scalars, *work, *blocks, *inputs]
    out_specs = [spec(o.shape, None) for o in outs]
    if tie is not None:
        operands.append(tie)
        specs.append(pl.BlockSpec((16, HEAD_SIZE), lambda i, *refs: (0, 0)))
        outs = [*outs, jax.ShapeDtypeStruct(tie.shape, tie.dtype)]
        out_specs.append(pl.BlockSpec(tie.shape, lambda i, *refs: (0, 0)))
    flops = count * 2 * products * (2 * rows * GROUP) * (len(blocks) * rows) * HEAD_SIZE
    return pl.pallas_call(
        functools.partial(kernel, layout),
        grid_spec=pltpu.PrefetchScalarGridSpec(
            num_scalar_prefetch=2,
            grid=(count,),
            in_specs=specs,
            out_specs=out_specs,
        ),
        out_shape=outs,
        compiler_params=pltpu.CompilerParams(vmem_limit_bytes=VMEM_BYTES),
        cost_estimate=pl.CostEstimate(
            flops=flops, bytes_accessed=count * 4 * 2 * rows * WIDTH * 2, transcendentals=0
        ),
    )(*operands)


def after(x, *tokens):
    return lax.optimization_barrier((x, *tokens))[0]


def on_device(seq_count, head_count, queries, rotated_key_rows, value_matrix, cotangent, tree_mask):
    s = lax.axis_index("seq")
    h = lax.axis_index("head")
    rows = queries.shape[0]
    core = h & 1
    scalars = (jnp.stack([h, s]).astype(jnp.int32), tree_mask)
    f32, bf16 = jnp.float32, jnp.bfloat16
    shape = jax.ShapeDtypeStruct

    def send(x, mask):
        return lax.ppermute(x, "head", [(i, i ^ mask) for i in range(head_count)])

    def columns(x, place, width):
        return lax.dynamic_slice_in_dim(x, place * width, width, 1)

    def half(kv, place):
        k, v = [columns(x, place, HEADS * HEAD_SIZE) for x in kv]
        parts = []
        for j in range(HEADS):
            part = slice(j * HEAD_SIZE, (j + 1) * HEAD_SIZE)
            parts += [k[:, part], v[:, part]]
        return jnp.concatenate(parts, axis=1)

    def gathered(kv, place):
        mine, other = half(kv, place), half(kv, 1 - place)
        return [mine, send(other, 1), send(mine, 2), send(other, 3)]

    hops = [1]
    step = seq_count // 2
    while step > 1:
        hops.append(step)
        step //= 2
    held = (rotated_key_rows, value_matrix)
    for hop, step in enumerate(hops):
        reached = seq_count if hop == 0 else 2 * step
        sends = [(i, i + step) for i in range(0, seq_count, reached)]
        if hop:
            sends += [(i + 1, i + 1 + step) for i, _ in sends]
            place = s - s % 2
            got = lax.ppermute(held, "seq", sends)
        else:
            place = s
            got = jnp.concatenate([lax.ppermute(x, "seq", sends) for x in held], axis=1)
            held = lax.optimization_barrier(jnp.concatenate(held, axis=1))
        held = jnp.where(place % reached == step, got, held)
        if hop == 0:
            side = after(core, held[:16, :HEAD_SIZE])
            own_blocks = gathered((rotated_key_rows, value_matrix), side)
            q_sib = send(columns(queries, 1 - side, HEADS * WIDTH), 1)
            c_sib = send(columns(cotangent, 1 - side, HEADS * WIDTH), 1)
            q_mine, c_mine = [columns(x, side, HEADS * WIDTH) for x in (queries, cotangent)]
            work = (q_mine, q_sib, c_mine, c_sib)
    width = KEY_VALUE_HEADS * HEAD_SIZE
    prompt = (held[:, :width], held[:, width:])
    prompt_blocks = gathered(prompt, core)

    near, far = (0, 1), (2, 3)
    own_all = tuple((own_bias, b) for b in near + far)
    every, one = (0, HEADS), 1

    def stats_shape():
        return shape((HEADS, 8, 2 * GROUP * rows), f32)

    def terms_shape(count, dtype):
        return shape((2 * rows, 2 * count * HEAD_SIZE), dtype)

    layout = own_all + tuple((prompt_bias, b) for b in near)
    blocks = [*own_blocks, *prompt_blocks[:2]]
    stats = call(stats_kernel, layout, every, scalars, work, blocks, [], [stats_shape()], 2)[0]
    layout = tuple((prompt_bias, b) for b in far)
    outs = [stats_shape(), terms_shape(HEADS, bf16)]
    stats, terms_far = call(
        last_keys_kernel, layout, every, scalars, work, prompt_blocks[2:], [stats], outs, 4
    )
    layout = tuple((prompt_bias, b) for b in near)
    outs = [terms_shape(HEADS, bf16)]
    terms = call(
        terms_kernel, layout, every, scalars, work, prompt_blocks[:2], [stats], outs, 4
    )[0]

    def plus(a, b):
        return a.astype(f32) + b.astype(f32)

    def across(x, pairs):
        flat = []
        for h in range(head_count):
            flat += [(a * head_count + h, b * head_count + (h ^ mask)) for a, b, mask in pairs]
        return lax.ppermute(x, ("seq", "head"), flat)

    even = range(0, seq_count, 2)
    got_far = across(terms_far, [(i, i, 2) for i in even])
    got_next_far = across(terms_far, [(i + 1, i, 2) for i in even])
    got_next = across(terms, [(i + 1, i, 0) for i in even])
    layout = own_all + tuple((prompt_bias, b) for b in near + far)
    blocks = [*own_blocks, *prompt_blocks]
    att, dq, own_sums = [], [], []
    total, tie = None, terms
    step, hop = 1, 0
    while step < seq_count:
        if hop:
            got = lax.ppermute(total, "seq", [(i + step, i) for i in range(0, seq_count, 2 * step)])
        if hop < HEADS:
            outs = [shape((rows, WIDTH), bf16)] * 4 + [terms_shape(1, f32), terms_shape(1, bf16)]
            a_m, a_s, d_m, d_s, own_near, own_far, token = call(
                rows_kernel, layout, (hop, one), scalars, work, blocks, [stats], outs, 8, tie
            )
            att.append((a_m, send(a_s, 1)))
            dq.append((d_m, send(d_s, 1)))
            own_sums.append((own_near, own_far))
        else:
            token = jnp.zeros_like(total)
        if hop:
            total = total + (got + token)
        else:
            total = plus(plus(terms, got_far), plus(got_next_far, got_next)) + token.astype(f32)
            total = total.astype(bf16)
        tie = total
        step *= 2
        hop += 1

    def both_halves(parts):
        mine = jnp.concatenate([x for x, _ in parts], axis=1)
        theirs = jnp.concatenate([x for _, x in parts], axis=1)
        return jnp.where(
            core == 0,
            jnp.concatenate([mine, theirs], axis=1),
            jnp.concatenate([theirs, mine], axis=1),
        )

    attention, query_grad = both_halves(att), both_halves(dq)
    total = jnp.where(s == 0, total.astype(f32), jnp.float32(0.0))
    own_near, own_far = [jnp.concatenate(x, axis=1) for x in zip(*own_sums)]
    total = (plus(own_near, send(own_far, 2)) + total).astype(bf16)
    total = both_halves([(total[:rows], send(total[rows:], 1))])

    def gradient(first):
        parts = []
        for j in range(KEY_VALUE_HEADS):
            start = (2 * j + first) * HEAD_SIZE
            parts.append(total[:, start : start + HEAD_SIZE])
        return jnp.concatenate(parts, axis=1)

    return (attention, query_grad, gradient(0), gradient(1))


def solution(mesh):
    spec = P(("seq", "head"), None)
    return jax.shard_map(
        functools.partial(on_device, mesh.shape["seq"], mesh.shape["head"]),
        mesh=mesh,
        in_specs=(spec, spec, spec, spec, P("seq", None)),
        out_specs=(spec, spec, spec, spec),
        check_vma=False,
    )
```

time: 83.5 us -> 78.3 us (0.938)
  Pallas kernels: 25.7 us -> 22 us
  starting transfers between devices: 22.5 us -> 24.9 us
  waiting for transfers between devices: 23.3 us -> 21.4 us
  other arithmetic: 7 us -> 5.97 us
    ppermute x3 -> x5, starting transfers between devices: 4.06 us -> 8.75 us  [the longest x3 5.98 us: across(): return lax.ppermute(x, ('seq', 'head'), flat)]
    pallas_call x5, Pallas kernels: 25.7 us -> 22 us  [call(): pl.pallas_call(functools.partial(kernel, layout), grid_spec=pltpu.Prefetc...]
    ppermute x15 -> x14, starting transfers between devices: 8.71 us -> 6.25 us  [send(): return lax.ppermute(x, 'head', [(i, i ^ mask) for i in range(head_count)])]
    unnamed x30 -> x8, local copies, waits for them, and re-layouts: 1.62 us -> 0.02 us
    convert_element_type x3 -> x1, other arithmetic: 1.22 us -> 0.17 us  [on_device(): total = total.astype(bf16)]
    ppermute x2, waiting for transfers between devices: 3.69 us -> 2.7 us  [on_device(): got = jnp.concatenate([lax.ppermute(x, 'seq', sends) for x in held], axis=1)]
    concatenate x0 -> x1, other arithmetic: none -> 0.99 us  [on_device(): held = lax.optimization_barrier(jnp.concatenate(held, axis=1))]
    select_n x3, other arithmetic: 1.09 us -> 0.12 us  [on_device(): held = jnp.where(place % reached == step, got, held)]
  transfers between devices with their start and end apart: 22 -> 23, of which waited for: 11 -> 10; matrix products, arithmetic and copies ran while one was open for 6% -> 9% of each run, Pallas kernels for 23% -> 23%
where the time goes in v4:
time: 78.3 us; the launch traced here: 77.9 us
  starting transfers between devices  24.9 us (32%)
  Pallas kernels  22 us (28%)
  waiting for transfers between devices  21.4 us (27%)
  other arithmetic  5.97 us (8%)
  local copies, waits for them, and re-layouts  2.7 us (3%)
  between operations  0.99 us (1%)
    pallas_call x5, Pallas kernels, call(): pl.pallas_call(functools.partial(kernel, layout), grid_spec=pltpu.Prefetc...  22 us
    ppermute x2, starting transfers between devices, on_device(): got = jnp.concatenate([lax.ppermute(x, 'seq', sends) for x in held], axis=1)  6.31 us
    ppermute x14, starting transfers between devices, send(): return lax.ppermute(x, 'head', [(i, i ^ mask) for i in range(head_count)])  6.25 us
    ppermute x2, waiting for transfers between devices, on_device(): lax.ppermute(total, 'seq', [(i + step, i) for i in range(0, seq_count, 2...  6.24 us
    ppermute x3, starting transfers between devices, across(): return lax.ppermute(x, ('seq', 'head'), flat)  5.98 us
    ppermute x14, waiting for transfers between devices, send(): return lax.ppermute(x, 'head', [(i, i ^ mask) for i in range(head_count)])  5.75 us
    ppermute x2, waiting for transfers between devices, on_device(): got = lax.ppermute(held, 'seq', sends)  3.94 us
    ppermute x2, starting transfers between devices, on_device(): got = lax.ppermute(held, 'seq', sends)  3.56 us
  transfers between devices with their start and end apart: 23, of which 10 were waited for; matrix products, arithmetic and copies ran while one was open for 9% of the time, Pallas kernels for 23%

profile of v4, /device:TPU:0, one launch (start us, length us, event | category | flops | bytes accessed | tf_op | source)
XLA Modules:
  0.0 77.9 jit_solution(12910703112120305663)
XLA Ops:
  0.6 5.0 %collective-permute-start.5 = (bf16[128,512]{1,0:T(8,128)(2,1)}, bf16[128,512]{1,0:T(8,128)(2,1)S(1)}, u32[]{:S(2)}, u32[]{:S(2)}) collective-permute-start(bf16[128,512]{1,0:T(8,128)(2,1)} %param.6), channel_id=1, source_target_pairs={{0,4},{1,5},{2,6},{3,7}} | collective-permute-start | bytes 393224 | tf_op jit(solution)/shard_map/ppermute | solution.py:264
  5.7 1.3 %collective-permute-start.6 = (bf16[128,512]{1,0:T(8,128)(2,1)}, bf16[128,512]{1,0:T(8,128)(2,1)S(1)}, u32[]{:S(2)}, u32[]{:S(2)}) collective-permute-start(bf16[128,512]{1,0:T(8,128)(2,1)} %param.7), channel_id=1, source_target_pairs={{0,4},{1,5},{2,6},{3,7}} | collective-permute-start | bytes 393224 | tf_op jit(solution)/shard_map/ppermute | solution.py:264
  7.0 1.0 %pad_maximum_fusion = bf16[128,1024]{1,0:T(8,128)(2,1)S(1)} fusion(bf16[128,512]{1,0:T(8,128)(2,1)} %param.7, bf16[128,512]{1,0:T(8,128)(2,1)} %param.6), kind=kLoop, calls=%fused_computation.7 | loop fusion | flops 524288 | bytes 524288 | tf_op jit(solution)/shard_map/concatenate | solution.py:265
  8.0 0.8 %constant_dynamic-slice_fusion.5 = (bf16[128,128]{1,0:T(8,128)(2,1)S(1)}, bf16[128,128]{1,0:T(8,128)(2,1)S(1)}, bf16[128,128]{1,0:T(8,128)(2,1)S(1)}, bf16[128,128]{1,0:T(8,128)(2,1)S(1)}) fusion(bf16[128,512]{1,0:T(8,128)(2,1)} %param.6, s32[]{:T(128)S(6)} %select_n.95, s32[]{:T(128)S(6)} %select_n.94, s32[]{:T(128)S(6)} %add.87, s32[]{:T(128)S(6)} %add.85), kind=kLoop, calls=%fused_computation.24 | loop fusion | bytes 262160 | tf_op jit(solution)/shard_map/slice | solution.py:242
  8.8 1.0 %collective-permute-done.5 = bf16[128,512]{1,0:T(8,128)(2,1)S(1)} collective-permute-done((bf16[128,512]{1,0:T(8,128)(2,1)}, bf16[128,512]{1,0:T(8,128)(2,1)S(1)}, u32[]{:S(2)}, u32[]{:S(2)}) %collective-permute-start.5) | collective-permute-done | bytes 131104 | tf_op jit(solution)/shard_map/ppermute | solution.py:264
  9.9 1.7 %collective-permute-done.6 = bf16[128,512]{1,0:T(8,128)(2,1)S(1)} collective-permute-done((bf16[128,512]{1,0:T(8,128)(2,1)}, bf16[128,512]{1,0:T(8,128)(2,1)S(1)}, u32[]{:S(2)}, u32[]{:S(2)}) %collective-permute-start.6) | collective-permute-done | bytes 131104 | tf_op jit(solution)/shard_map/ppermute | solution.py:264
  11.5 0.1 maximum_select_fusion.2
  11.6 0.0 copy-start.1
  11.6 1.4 %collective-permute-start.7 = (bf16[128,1024]{1,0:T(8,128)(2,1)S(1)}, bf16[128,1024]{1,0:T(8,128)(2,1)S(1)}, u32[]{:S(2)}, u32[]{:S(2)}) collective-permute-start(bf16[128,1024]{1,0:T(8,128)(2,1)S(1)} %maximum_select_fusion.2), channel_id=1, source_target_pairs={{0,16},{4,20},{1,17},{5,21},{2,18},{6,22},{3,19},{7,23}} | collective-permute-start | bytes 786440 | tf_op jit(solution)/shard_map/ppermute | solution.py:261
  13.1 0.7 pad_maximum_fusion.3
  13.8 0.1 collective-permute-start.4
  13.8 1.5 %collective-permute-start.2 = (bf16[128,512]{1,0:T(8,128)(2,1)}, bf16[128,512]{1,0:T(8,128)(2,1)S(1)}, u32[]{:S(2)}, u32[]{:S(2)}) collective-permute-start(bf16[128,512]{1,0:T(8,128)(2,1)} %pad_maximum_fusion.3), channel_id=1, source_target_pairs={{0,1},{1,0},{2,3},{3,2},{4,5},{5,4},{6,7},{7,6},{8,9},{9,8},{10,11... | collective-permute-start | bytes 393224 | tf_op jit(solution)/shard_map/ppermute | solution.py:232
  15.4 0.6 collective-permute-start.3
  16.0 2.0 %collective-permute-done.7 = bf16[128,1024]{1,0:T(8,128)(2,1)S(1)} collective-permute-done((bf16[128,1024]{1,0:T(8,128)(2,1)S(1)}, bf16[128,1024]{1,0:T(8,128)(2,1)S(1)}, u32[]{:S(2)}, u32[]{:S(2)}) %collective-permute-start.7) | collective-permute-done | bytes 262176 | tf_op jit(solution)/shard_map/ppermute | solution.py:261
  18.0 0.0 copy-start.2
  18.0 2.1 %collective-permute-start.8 = (bf16[128,1024]{1,0:T(8,128)(2,1)S(1)}, bf16[128,1024]{1,0:T(8,128)(2,1)}, u32[]{:S(2)}, u32[]{:S(2)}) collective-permute-start(bf16[128,1024]{1,0:T(8,128)(2,1)S(1)} %broadcast_select_fusion), channel_id=1, source_target_pairs={{0,8},{16,24},{4,12},{20,28},{1,9},{17,25},{5,13},{21,29},{2,10},{... | collective-permute-start | bytes 786440 | tf_op jit(solution)/shard_map/ppermute | solution.py:261
  20.1 0.8 %constant_dynamic-slice_fusion.18 = (bf16[128,1792]{1,0:T(8,128)(2,1)}, bf16[128,1792]{1,0:T(8,128)(2,1)S(1)}) fusion(bf16[128,3584]{1,0:T(8,128)(2,1)S(1)} %copy-done.1, s32[]{:T(128)S(6)} %select_n.93, s32[]{:T(128)S(6)} %select_n.92), kind=kLoop, calls=%fused_computation.37 | loop fusion | bytes 1835016 | tf_op jit(solution)/shard_map/dynamic_slice | solution.py:235
  21.0 0.0 collective-permute-start
  21.0 0.8 %constant_dynamic-slice_fusion.16 = (bf16[128,1792]{1,0:T(8,128)(2,1)}, bf16[128,1792]{1,0:T(8,128)(2,1)S(1)}) fusion(bf16[128,3584]{1,0:T(8,128)(2,1)S(1)} %copy-done.2, s32[]{:T(128)S(6)} %select_n.93, s32[]{:T(128)S(6)} %select_n.92), kind=kLoop, calls=%fused_computation.35 | loop fusion | bytes 1835016 | tf_op jit(solution)/shard_map/dynamic_slice | solution.py:235
  21.8 2.0 %collective-permute-done.8 = bf16[128,1024]{1,0:T(8,128)(2,1)} collective-permute-done((bf16[128,1024]{1,0:T(8,128)(2,1)S(1)}, bf16[128,1024]{1,0:T(8,128)(2,1)}, u32[]{:S(2)}, u32[]{:S(2)}) %collective-permute-start.8) | collective-permute-done | bytes 262176 | tf_op jit(solution)/shard_map/ppermute | solution.py:261
  23.8 0.0 collective-permute-start.1
  23.8 0.0 copy-start
  23.8 0.1 constant_dynamic-slice_fusion
  23.9 0.0 collective-permute-done.3.refs_2_
  24.0 0.6 collective-permute-start.9
  24.5 0.1 pad_add_fusion.ids
  24.6 0.0 collective-permute-done.4.refs_3_
  24.6 1.2 %collective-permute-start.11 = (bf16[128,512]{1,0:T(8,128)(2,1)S(1)}, bf16[128,512]{1,0:T(8,128)(2,1)S(1)}, u32[]{:S(2)}, u32[]{:S(2)}) collective-permute-start(bf16[128,512]{1,0:T(8,128)(2,1)S(1)} %pad_maximum_fusion.5), channel_id=1, source_target_pairs={{0,3},{1,2},{2,1},{3,0},{4,7},{5,6},{6,5},{7,4},{8,11},{9,10},{10,... | collective-permute-start | bytes 393224 | tf_op jit(solution)/shard_map/ppermute | solution.py:232
  25.8 0.0 collective-permute-done.2.refs_1_
  25.8 0.5 collective-permute-start.10
  26.4 0.0 collective-permute-done.qs
  26.4 4.7 %shard_map.84.refs_2_ = f32[2,8,1792]{2,1,0:T(8,128)S(1)} custom-call(s32[2]{0:T(128)S(1)} %pad_add_fusion.ids, s32[4,4]{1,0:T(4,128)S(1)} %copy-done, bf16[128,1792]{1,0:T(8,128)(2,1)S(1)} %get-tuple-element.39.qm, bf16[128,1792]{1,0:T(8,128)(2,1)S(1)} %collective-permute-done.qs, bf16[128,1792]{1,0:T(8,128)(2,1)S(1)} %get-tuple-element.37.cm, ...), custom_call_target="tpu_custom_call" | custom-call | flops 1409286144 | bytes 3670016 | tf_op jit(solution)/shard_map/pallas_call | solution.py:202
  31.1 2.2 %collective-permute-done.10.refs_0_.refs_6_ = bf16[128,512]{1,0:T(8,128)(2,1)S(1)} collective-permute-done((bf16[128,512]{1,0:T(8,128)(2,1)S(1)}, bf16[128,512]{1,0:T(8,128)(2,1)S(1)}, u32[]{:S(2)}, u32[]{:S(2)}) %collective-permute-start.10) | collective-permute-done | bytes 131104 | tf_op jit(solution)/shard_map/ppermute | solution.py:232
  33.3 3.9 %shard_map.85 = (f32[2,8,1792]{2,1,0:T(8,128)S(1)}, bf16[256,512]{1,0:T(8,128)(2,1)S(1)}) custom-call(s32[2]{0:T(128)S(1)} %pad_add_fusion.ids, s32[4,4]{1,0:T(4,128)S(1)} %copy-done, bf16[128,1792]{1,0:T(8,128)(2,1)S(1)} %get-tuple-element.39.qm, bf16[128,1792]{1,0:T(8,128)(2,1)S(1)} %collective-permute-done.qs, ...), custom_call_target="tpu_custom_call" | custom-call | flops 939524096 | bytes 3670016 | tf_op jit(solution)/shard_map/pallas_call | solution.py:202
  37.2 1.3 %collective-permute-start.13 = (bf16[256,512]{1,0:T(8,128)(2,1)S(1)}, bf16[256,512]{1,0:T(8,128)(2,1)S(1)}, u32[]{:S(2)}, u32[]{:S(2)}) collective-permute-start(bf16[256,512]{1,0:T(8,128)(2,1)S(1)} %get-tuple-element.22), channel_id=1, source_target_pairs={{4,2},{12,10},{20,18},{28,26},{5,3},{13,11},{21,19},{29,27},{6,0},... | collective-permute-start | bytes 786440 | tf_op jit(solution)/shard_map/ppermute | solution.py:309
  38.5 3.4 %collective-permute-start.12 = (bf16[256,512]{1,0:T(8,128)(2,1)S(1)}, bf16[256,512]{1,0:T(8,128)(2,1)S(1)}, u32[]{:S(2)}, u32[]{:S(2)}) collective-permute-start(bf16[256,512]{1,0:T(8,128)(2,1)S(1)} %get-tuple-element.22), channel_id=1, source_target_pairs={{0,2},{8,10},{16,18},{24,26},{1,3},{9,11},{17,19},{25,27},{2,0},{1... | collective-permute-start | bytes 786440 | tf_op jit(solution)/shard_map/ppermute | solution.py:309
  41.9 3.2 %shard_map.86.refs_9_ = bf16[256,512]{1,0:T(8,128)(2,1)S(1)} custom-call(s32[2]{0:T(128)S(1)} %pad_add_fusion.ids, s32[4,4]{1,0:T(4,128)S(1)} %copy-done, bf16[128,1792]{1,0:T(8,128)(2,1)S(1)} %get-tuple-element.39.qm, bf16[128,1792]{1,0:T(8,128)(2,1)S(1)} %collective-permute-done.qs, bf16[128,1792]{1,0:T(8,128)(2,1)S(1)} %get-tuple-element.37.cm, ...), custom_call_target="tpu_custom_call" | custom-call | flops 939524096 | bytes 3670016 | tf_op jit(solution)/shard_map/pallas_call | solution.py:202
  45.1 1.3 %collective-permute-start.14 = (bf16[256,512]{1,0:T(8,128)(2,1)S(1)}, bf16[256,512]{1,0:T(8,128)(2,1)S(1)}, u32[]{:S(2)}, u32[]{:S(2)}) collective-permute-start(bf16[256,512]{1,0:T(8,128)(2,1)S(1)} %shard_map.86.refs_9_), channel_id=1, source_target_pairs={{4,0},{12,8},{20,16},{28,24},{5,1},{13,9},{21,17},{29,25},{6,2},{1... | collective-permute-start | bytes 786440 | tf_op jit(solution)/shard_map/ppermute | solution.py:309
  46.4 5.1 %shard_map.87 = (bf16[128,896]{1,0:T(8,128)(2,1)S(1)}, bf16[128,896]{1,0:T(8,128)(2,1)S(1)}, bf16[128,896]{1,0:T(8,128)(2,1)S(1)}, bf16[128,896]{1,0:T(8,128)(2,...) custom-call(s32[2]{0:T(128)S(1)} %pad_add_fusion.ids, ...), custom_call_target="tpu_custom_call" | custom-call | flops 3758096384 | bytes 1835008 | tf_op jit(solution)/shard_map/pallas_call | solution.py:202
  51.5 0.1 collective-permute-start.15
  51.6 0.5 collective-permute-start.17
  52.1 2.8 %collective-permute-done.14 = bf16[256,512]{1,0:T(8,128)(2,1)S(1)} collective-permute-done((bf16[256,512]{1,0:T(8,128)(2,1)S(1)}, bf16[256,512]{1,0:T(8,128)(2,1)S(1)}, u32[]{:S(2)}, u32[]{:S(2)}) %collective-permute-start.14) | collective-permute-done | bytes 262176 | tf_op jit(solution)/shard_map/ppermute | solution.py:309
  54.9 0.0 collective-permute-done.13
  54.9 0.0 collective-permute-done.12
  54.9 0.2 add_convert_fusion.refs_9_
  55.1 1.5 %collective-permute-start.20 = (bf16[256,512]{1,0:T(8,128)(2,1)S(1)}, bf16[256,512]{1,0:T(8,128)(2,1)S(1)}, u32[]{:S(2)}, u32[]{:S(2)}) collective-permute-start(bf16[256,512]{1,0:T(8,128)(2,1)S(1)} %add_convert_fusion.refs_9_), channel_id=1, source_target_pairs={{8,0},{24,16},{9,1},{25,17},{10,2},{26,18},{11,3},{27,19}} | collective-permute-start | bytes 786440 | tf_op jit(solution)/shard_map/ppermute | solution.py:322
  56.5 5.1 %shard_map.88 = (bf16[128,896]{1,0:T(8,128)(2,1)S(1)}, bf16[128,896]{1,0:T(8,128)(2,1)S(1)}, bf16[128,896]{1,0:T(8,128)(2,1)S(1)}, bf16[128,896]{1,0:T(8,128)(2,...) custom-call(s32[2]{0:T(128)S(1)} %pad_add_fusion.ids, ...), custom_call_target="tpu_custom_call" | custom-call | flops 3758096384 | bytes 1835008 | tf_op jit(solution)/shard_map/pallas_call | solution.py:202
  61.6 0.1 collective-permute-start.16
  61.7 0.5 collective-permute-start.18
  62.2 2.9 %collective-permute-done.20 = bf16[256,512]{1,0:T(8,128)(2,1)S(1)} collective-permute-done((bf16[256,512]{1,0:T(8,128)(2,1)S(1)}, bf16[256,512]{1,0:T(8,128)(2,1)S(1)}, u32[]{:S(2)}, u32[]{:S(2)}) %collective-permute-start.20) | collective-permute-done | bytes 262176 | tf_op jit(solution)/shard_map/ppermute | solution.py:322
  65.1 0.5 collective-permute-start.19
  65.7 1.3 %collective-permute-start.21 = (bf16[256,512]{1,0:T(8,128)(2,1)S(1)}, bf16[256,512]{1,0:T(8,128)(2,1)S(1)}, u32[]{:S(2)}, u32[]{:S(2)}) collective-permute-start(bf16[256,512]{1,0:T(8,128)(2,1)S(1)} %add_add_fusion), channel_id=1, source_target_pairs={{16,0},{17,1},{18,2},{19,3}} | collective-permute-start | bytes 786440 | tf_op jit(solution)/shard_map/ppermute | solution.py:322
  67.0 0.0 collective-permute-done.16
  67.0 1.1 %maximum_select_fusion = bf16[128,3584]{1,0:T(8,128)(2,1)} fusion(bf16[128,896]{1,0:T(8,128)(2,1)S(1)} %collective-permute-done.16, bf16[128,896]{1,0:T(8,128)(2,1)S(1)} %collective-permute-done.15, bf16[128,896]{1,0:T(8,128)(2,1)S(1)} %get-tuple-element.24, bf16[128,896]{1,0:T(8,128)(2,1)S(1)} %get-tuple-element.21, pred[]{:T(512)S(6)} %eq.23), kind=kLoop, calls=%fused_computation | loop fusion | flops 7798784 | bytes 1835009 | tf_op jit(solution)/shard_map/jit(_where)/select_n | solution.py:345
  68.1 3.3 %collective-permute-done.19 = bf16[256,512]{1,0:T(8,128)(2,1)S(1)} collective-permute-done((bf16[256,512]{1,0:T(8,128)(2,1)S(1)}, bf16[256,512]{1,0:T(8,128)(2,1)S(1)}, u32[]{:S(2)}, u32[]{:S(2)}) %collective-permute-start.19) | collective-permute-done | bytes 262176 | tf_op jit(solution)/shard_map/ppermute | solution.py:232
  71.4 3.4 %collective-permute-done.21 = bf16[256,512]{1,0:T(8,128)(2,1)S(1)} collective-permute-done((bf16[256,512]{1,0:T(8,128)(2,1)S(1)}, bf16[256,512]{1,0:T(8,128)(2,1)S(1)}, u32[]{:S(2)}, u32[]{:S(2)}) %collective-permute-start.21) | collective-permute-done | bytes 262176 | tf_op jit(solution)/shard_map/ppermute | solution.py:322
  74.8 0.1 fusion.1
  75.0 0.1 collective-permute-start.22
  75.1 0.0 collective-permute-done.17
  75.1 1.1 %maximum_select_fusion.1 = bf16[128,3584]{1,0:T(8,128)(2,1)} fusion(bf16[128,896]{1,0:T(8,128)(2,1)S(1)} %collective-permute-done.18, bf16[128,896]{1,0:T(8,128)(2,1)S(1)} %collective-permute-done.17, bf16[128,896]{1,0:T(8,128)(2,1)S(1)} %get-tuple-element.28, bf16[128,896]{1,0:T(8,128)(2,1)S(1)} %get-tuple-element.27, pred[]{:T(512)S(6)} %eq.23), kind=kLoop, calls=%fused_computation.1 | loop fusion | flops 7798784 | bytes 1835009 | tf_op jit(solution)/shard_map/jit(_where)/select_n | solution.py:345
  76.2 0.2 collective-permute-done.22
  76.4 0.1 maximum_select_fusion.3
  76.6 0.7 pad_maximum_fusion.7
  77.2 0.7 pad_maximum_fusion.6
  (21 shorter events, 0.3 us)
Async XLA Ops:
  0.6 12.4 %copy-start.3 = (bf16[128,512]{1,0:T(8,128)(2,1)S(1)}, bf16[128,512]{1,0:T(8,128)(2,1)}, u32[]{:S(2)}) copy-start(bf16[128,512]{1,0:T(8,128)(2,1)} %param.7) | copy-start | bytes 393220
  0.6 9.2 %collective-permute-start.5 = (bf16[128,512]{1,0:T(8,128)(2,1)}, bf16[128,512]{1,0:T(8,128)(2,1)S(1)}, u32[]{:S(2)}, u32[]{:S(2)}) collective-permute-start(bf16[128,512]{1,0:T(8,128)(2,1)} %param.6), channel_id=1, source_target_pairs={{0,4},{1,5},{2,6},{3,7}} | collective-permute-start | bytes 393224 | tf_op jit(solution)/shard_map/ppermute | solution.py:264
  5.7 5.9 %collective-permute-start.6 = (bf16[128,512]{1,0:T(8,128)(2,1)}, bf16[128,512]{1,0:T(8,128)(2,1)S(1)}, u32[]{:S(2)}, u32[]{:S(2)}) collective-permute-start(bf16[128,512]{1,0:T(8,128)(2,1)} %param.7), channel_id=1, source_target_pairs={{0,4},{1,5},{2,6},{3,7}} | collective-permute-start | bytes 393224 | tf_op jit(solution)/shard_map/ppermute | solution.py:264
  11.6 8.6 %copy-start.1 = (bf16[128,3584]{1,0:T(8,128)(2,1)S(1)}, bf16[128,3584]{1,0:T(8,128)(2,1)}, u32[]{:S(2)}) copy-start(bf16[128,3584]{1,0:T(8,128)(2,1)} %param.5) | copy-start | bytes 2752516
  11.6 6.4 %collective-permute-start.7 = (bf16[128,1024]{1,0:T(8,128)(2,1)S(1)}, bf16[128,1024]{1,0:T(8,128)(2,1)S(1)}, u32[]{:S(2)}, u32[]{:S(2)}) collective-permute-start(bf16[128,1024]{1,0:T(8,128)(2,1)S(1)} %maximum_select_fusion.2), channel_id=1, source_target_pairs={{0,16},{4,20},{1,17},{5,21},{2,18},{6,22},{3,19},{7,23}} | collective-permute-start | bytes 786440 | tf_op jit(solution)/shard_map/ppermute | solution.py:261
  13.8 10.9 %collective-permute-start.4 = (bf16[128,512]{1,0:T(8,128)(2,1)}, bf16[128,512]{1,0:T(8,128)(2,1)S(1)}, u32[]{:S(2)}, u32[]{:S(2)}) collective-permute-start(bf16[128,512]{1,0:T(8,128)(2,1)} %pad_maximum_fusion.3), channel_id=1, source_target_pairs={{0,3},{1,2},{2,1},{3,0},{4,7},{5,6},{6,5},{7,4},{8,11},{9,10},{10,... | collective-permute-start | bytes 393224 | tf_op jit(solution)/shard_map/ppermute | solution.py:232
  13.8 12.0 %collective-permute-start.2 = (bf16[128,512]{1,0:T(8,128)(2,1)}, bf16[128,512]{1,0:T(8,128)(2,1)S(1)}, u32[]{:S(2)}, u32[]{:S(2)}) collective-permute-start(bf16[128,512]{1,0:T(8,128)(2,1)} %pad_maximum_fusion.3), channel_id=1, source_target_pairs={{0,1},{1,0},{2,3},{3,2},{4,5},{5,4},{6,7},{7,6},{8,9},{9,8},{10,11... | collective-permute-start | bytes 393224 | tf_op jit(solution)/shard_map/ppermute | solution.py:232
  15.4 8.6 %collective-permute-start.3 = (bf16[128,512]{1,0:T(8,128)(2,1)S(1)}, bf16[128,512]{1,0:T(8,128)(2,1)S(1)}, u32[]{:S(2)}, u32[]{:S(2)}) collective-permute-start(bf16[128,512]{1,0:T(8,128)(2,1)S(1)} %pad_maximum_fusion.2.refs_0_), channel_id=1, source_target_pairs={{0,2},{1,3},{2,0},{3,1},{4,6},{5,7},{6,4},{7,5},{8,10},{9,11},{10,... | collective-permute-start | bytes 393224 | tf_op jit(solution)/shard_map/ppermute | solution.py:232
  18.0 3.0 %copy-start.2 = (bf16[128,3584]{1,0:T(8,128)(2,1)S(1)}, bf16[128,3584]{1,0:T(8,128)(2,1)}, u32[]{:S(2)}) copy-start(bf16[128,3584]{1,0:T(8,128)(2,1)} %param.8) | copy-start | bytes 2752516
  18.0 5.7 %collective-permute-start.8 = (bf16[128,1024]{1,0:T(8,128)(2,1)S(1)}, bf16[128,1024]{1,0:T(8,128)(2,1)}, u32[]{:S(2)}, u32[]{:S(2)}) collective-permute-start(bf16[128,1024]{1,0:T(8,128)(2,1)S(1)} %broadcast_select_fusion), channel_id=1, source_target_pairs={{0,8},{16,24},{4,12},{20,28},{1,9},{17,25},{5,13},{21,29},{2,10},{... | collective-permute-start | bytes 786440 | tf_op jit(solution)/shard_map/ppermute | solution.py:261
  21.0 5.4 %collective-permute-start = (bf16[128,1792]{1,0:T(8,128)(2,1)}, bf16[128,1792]{1,0:T(8,128)(2,1)S(1)}, u32[]{:S(2)}, u32[]{:S(2)}) collective-permute-start(bf16[128,1792]{1,0:T(8,128)(2,1)} %get-tuple-element.38), channel_id=1, source_target_pairs={{0,1},{1,0},{2,3},{3,2},{4,5},{5,4},{6,7},{7,6},{8,9},{9,8},{10,11... | collective-permute-start | bytes 1376264 | tf_op jit(solution)/shard_map/ppermute | solution.py:232
  23.8 2.6 %collective-permute-start.1 = (bf16[128,1792]{1,0:T(8,128)(2,1)}, bf16[128,1792]{1,0:T(8,128)(2,1)S(1)}, u32[]{:S(2)}, u32[]{:S(2)}) collective-permute-start(bf16[128,1792]{1,0:T(8,128)(2,1)} %get-tuple-element.36), channel_id=1, source_target_pairs={{0,1},{1,0},{2,3},{3,2},{4,5},{5,4},{6,7},{7,6},{8,9},{9,8},{10,11... | collective-permute-start | bytes 1376264 | tf_op jit(solution)/shard_map/ppermute | solution.py:232
  23.8 2.6 %copy-start = (s32[4,4]{1,0:T(4,128)S(1)}, s32[4,4]{1,0:T(4,128)}, u32[]{:S(2)}) copy-start(s32[4,4]{1,0:T(4,128)} %tree.9) | copy-start | bytes 196
  24.0 2.4 %collective-permute-start.9 = (bf16[128,512]{1,0:T(8,128)(2,1)S(1)}, bf16[128,512]{1,0:T(8,128)(2,1)S(1)}, u32[]{:S(2)}, u32[]{:S(2)}) collective-permute-start(bf16[128,512]{1,0:T(8,128)(2,1)S(1)} %pad_maximum_fusion.5), channel_id=1, source_target_pairs={{0,1},{1,0},{2,3},{3,2},{4,5},{5,4},{6,7},{7,6},{8,9},{9,8},{10,11... | collective-permute-start | bytes 393224 | tf_op jit(solution)/shard_map/ppermute | solution.py:232
  24.6 8.7 %collective-permute-start.11 = (bf16[128,512]{1,0:T(8,128)(2,1)S(1)}, bf16[128,512]{1,0:T(8,128)(2,1)S(1)}, u32[]{:S(2)}, u32[]{:S(2)}) collective-permute-start(bf16[128,512]{1,0:T(8,128)(2,1)S(1)} %pad_maximum_fusion.5), channel_id=1, source_target_pairs={{0,3},{1,2},{2,1},{3,0},{4,7},{5,6},{6,5},{7,4},{8,11},{9,10},{10,... | collective-permute-start | bytes 393224 | tf_op jit(solution)/shard_map/ppermute | solution.py:232
  25.8 7.5 %collective-permute-start.10 = (bf16[128,512]{1,0:T(8,128)(2,1)S(1)}, bf16[128,512]{1,0:T(8,128)(2,1)S(1)}, u32[]{:S(2)}, u32[]{:S(2)}) collective-permute-start(bf16[128,512]{1,0:T(8,128)(2,1)S(1)} %pad_maximum_fusion.4.refs_4_.refs_0_), channel_id=1, source_target_pairs={{0,2},{1,3},{2,0},{3,1},{4,6},{5,7},{6,4},{7,5},{8,10},{9,11},{10,... | collective-permute-start | bytes 393224 | tf_op jit(solution)/shard_map/ppermute | solution.py:232
  37.2 17.7 %collective-permute-start.13 = (bf16[256,512]{1,0:T(8,128)(2,1)S(1)}, bf16[256,512]{1,0:T(8,128)(2,1)S(1)}, u32[]{:S(2)}, u32[]{:S(2)}) collective-permute-start(bf16[256,512]{1,0:T(8,128)(2,1)S(1)} %get-tuple-element.22), channel_id=1, source_target_pairs={{4,2},{12,10},{20,18},{28,26},{5,3},{13,11},{21,19},{29,27},{6,0},... | collective-permute-start | bytes 786440 | tf_op jit(solution)/shard_map/ppermute | solution.py:309
  38.5 16.4 %collective-permute-start.12 = (bf16[256,512]{1,0:T(8,128)(2,1)S(1)}, bf16[256,512]{1,0:T(8,128)(2,1)S(1)}, u32[]{:S(2)}, u32[]{:S(2)}) collective-permute-start(bf16[256,512]{1,0:T(8,128)(2,1)S(1)} %get-tuple-element.22), channel_id=1, source_target_pairs={{0,2},{8,10},{16,18},{24,26},{1,3},{9,11},{17,19},{25,27},{2,0},{1... | collective-permute-start | bytes 786440 | tf_op jit(solution)/shard_map/ppermute | solution.py:309
  45.1 9.7 %collective-permute-start.14 = (bf16[256,512]{1,0:T(8,128)(2,1)S(1)}, bf16[256,512]{1,0:T(8,128)(2,1)S(1)}, u32[]{:S(2)}, u32[]{:S(2)}) collective-permute-start(bf16[256,512]{1,0:T(8,128)(2,1)S(1)} %shard_map.86.refs_9_), channel_id=1, source_target_pairs={{4,0},{12,8},{20,16},{28,24},{5,1},{13,9},{21,17},{29,25},{6,2},{1... | collective-permute-start | bytes 786440 | tf_op jit(solution)/shard_map/ppermute | solution.py:309
  51.5 14.2 %collective-permute-start.15 = (bf16[128,896]{1,0:T(8,128)(2,1)S(1)}, bf16[128,896]{1,0:T(8,128)(2,1)S(1)}, u32[]{:S(2)}, u32[]{:S(2)}) collective-permute-start(bf16[128,896]{1,0:T(8,128)(2,1)S(1)} %get-tuple-element.25), channel_id=1, source_target_pairs={{0,1},{1,0},{2,3},{3,2},{4,5},{5,4},{6,7},{7,6},{8,9},{9,8},{10,11... | collective-permute-start | bytes 688136 | tf_op jit(solution)/shard_map/ppermute | solution.py:232
  51.6 23.5 %collective-permute-start.17 = (bf16[128,896]{1,0:T(8,128)(2,1)S(1)}, bf16[128,896]{1,0:T(8,128)(2,1)S(1)}, u32[]{:S(2)}, u32[]{:S(2)}) collective-permute-start(bf16[128,896]{1,0:T(8,128)(2,1)S(1)} %get-tuple-element.29), channel_id=1, source_target_pairs={{0,1},{1,0},{2,3},{3,2},{4,5},{5,4},{6,7},{7,6},{8,9},{9,8},{10,11... | collective-permute-start | bytes 688136 | tf_op jit(solution)/shard_map/ppermute | solution.py:232
  55.1 10.0 %collective-permute-start.20 = (bf16[256,512]{1,0:T(8,128)(2,1)S(1)}, bf16[256,512]{1,0:T(8,128)(2,1)S(1)}, u32[]{:S(2)}, u32[]{:S(2)}) collective-permute-start(bf16[256,512]{1,0:T(8,128)(2,1)S(1)} %add_convert_fusion.refs_9_), channel_id=1, source_target_pairs={{8,0},{24,16},{9,1},{25,17},{10,2},{26,18},{11,3},{27,19}} | collective-permute-start | bytes 786440 | tf_op jit(solution)/shard_map/ppermute | solution.py:322
  61.6 5.4 %collective-permute-start.16 = (bf16[128,896]{1,0:T(8,128)(2,1)S(1)}, bf16[128,896]{1,0:T(8,128)(2,1)S(1)}, u32[]{:S(2)}, u32[]{:S(2)}) collective-permute-start(bf16[128,896]{1,0:T(8,128)(2,1)S(1)} %get-tuple-element.26), channel_id=1, source_target_pairs={{0,1},{1,0},{2,3},{3,2},{4,5},{5,4},{6,7},{7,6},{8,9},{9,8},{10,11... | collective-permute-start | bytes 688136 | tf_op jit(solution)/shard_map/ppermute | solution.py:232
  61.7 13.4 %collective-permute-start.18 = (bf16[128,896]{1,0:T(8,128)(2,1)S(1)}, bf16[128,896]{1,0:T(8,128)(2,1)S(1)}, u32[]{:S(2)}, u32[]{:S(2)}) collective-permute-start(bf16[128,896]{1,0:T(8,128)(2,1)S(1)} %get-tuple-element.30), channel_id=1, source_target_pairs={{0,1},{1,0},{2,3},{3,2},{4,5},{5,4},{6,7},{7,6},{8,9},{9,8},{10,11... | collective-permute-start | bytes 688136 | tf_op jit(solution)/shard_map/ppermute | solution.py:232
  65.1 6.4 %collective-permute-start.19 = (bf16[256,512]{1,0:T(8,128)(2,1)S(1)}, bf16[256,512]{1,0:T(8,128)(2,1)S(1)}, u32[]{:S(2)}, u32[]{:S(2)}) collective-permute-start(bf16[256,512]{1,0:T(8,128)(2,1)S(1)} %pad_maximum_fusion.1), channel_id=1, source_target_pairs={{0,2},{1,3},{2,0},{3,1},{4,6},{5,7},{6,4},{7,5},{8,10},{9,11},{10,... | collective-permute-start | bytes 786440 | tf_op jit(solution)/shard_map/ppermute | solution.py:232
  65.7 9.2 %collective-permute-start.21 = (bf16[256,512]{1,0:T(8,128)(2,1)S(1)}, bf16[256,512]{1,0:T(8,128)(2,1)S(1)}, u32[]{:S(2)}, u32[]{:S(2)}) collective-permute-start(bf16[256,512]{1,0:T(8,128)(2,1)S(1)} %add_add_fusion), channel_id=1, source_target_pairs={{16,0},{17,1},{18,2},{19,3}} | collective-permute-start | bytes 786440 | tf_op jit(solution)/shard_map/ppermute | solution.py:322
  75.0 1.4 %collective-permute-start.22 = (bf16[128,512]{1,0:T(8,128)(2,1)S(1)}, bf16[128,512]{1,0:T(8,128)(2,1)S(1)}, u32[]{:S(2)}, u32[]{:S(2)}) collective-permute-start(bf16[128,512]{1,0:T(8,128)(2,1)S(1)} %get-tuple-element.49), channel_id=1, source_target_pairs={{0,1},{1,0},{2,3},{3,2},{4,5},{5,4},{6,7},{7,6},{8,9},{9,8},{10,11... | collective-permute-start | bytes 393224 | tf_op jit(solution)/shard_map/ppermute | solution.py:232

commit v5 on v4

--- a/solution.py
+++ b/solution.py
@@ -180,39 +180,74 @@
             d[:, columns] = dq[:, part].T.astype(jnp.bfloat16)
 
 
+def halves_kernel(side, q, c, q_mine, q_other, c_mine, c_other, done):
+    width = q_mine.shape[1]
+    copies = []
+    for x, out, place in (
+        (q, q_other, 1 - side[0]),
+        (c, c_other, 1 - side[0]),
+        (q, q_mine, side[0]),
+        (c, c_mine, side[0]),
+    ):
+        part = pl.ds(pl.multiple_of(place * width, HEAD_SIZE), width)
+        copies.append(pltpu.make_async_copy(x.at[:, part], out, done.at[len(copies)]))
+    for copy in copies:
+        copy.start()
+    for copy in copies:
+        copy.wait()
+
+
+def halves(side, q, c):
+    half = jax.ShapeDtypeStruct((q.shape[0], q.shape[1] // 2), q.dtype)
+    hbm = pl.BlockSpec(memory_space=pltpu.MemorySpace.HBM)
+    return pl.pallas_call(
+        halves_kernel,
+        in_specs=[pl.BlockSpec(memory_space=pltpu.SMEM), hbm, hbm],
+        out_specs=[pl.BlockSpec(memory_space=pltpu.VMEM)] * 4,
+        out_shape=[half] * 4,
+        scratch_shapes=[pltpu.SemaphoreType.DMA((4,))],
+        cost_estimate=pl.CostEstimate(flops=0, bytes_accessed=8 * q.size, transcendentals=0),
+    )(side.astype(jnp.int32).reshape(1), q, c)
+
+
 def call(kernel, layout, heads, scalars, work, blocks, inputs, outs, products, tie=None):
     rows = work[0].shape[0]
     first, count = heads
-
-    def spec(shape, base):
-        if len(shape) == 2:
-            return pl.BlockSpec((shape[0], shape[1] // (HEADS if base is not None else count)), lambda i, *refs: (0, i + (base or 0)))
-        return pl.BlockSpec((1, *shape[1:]), lambda i, *refs: (i + (base or 0),) + (0,) * (len(shape) - 1))
-
-    sib = spec((rows, HEADS * WIDTH), first)
-    specs = [sib] * 4 + [spec(x.shape, first) for x in (*blocks, *inputs)]
-    operands = [*scalars, *work, *blocks, *inputs]
-    out_specs = [spec(o.shape, None) for o in outs]
+    ins = [*work, *blocks, *inputs]
     if tie is not None:
-        operands.append(tie)
-        specs.append(pl.BlockSpec((16, HEAD_SIZE), lambda i, *refs: (0, 0)))
+        ins.append(tie)
         outs = [*outs, jax.ShapeDtypeStruct(tie.shape, tie.dtype)]
-        out_specs.append(pl.BlockSpec(tie.shape, lambda i, *refs: (0, 0)))
+
+    def part(ref, j, held):
+        if len(ref.shape) == 3:
+            return ref.at[j : j + 1]
+        width = ref.shape[1] // held
+        return ref.at[:, j * width : (j + 1) * width]
+
+    def body(ids, tree, *refs):
+        given, made = refs[: len(ins)], refs[len(ins) :]
+        for i in range(count):
+            views = [part(r, first + i, HEADS) for r in given] + [part(r, i, count) for r in made]
+            if tie is not None:
+                views[len(ins) - 1], views[-1] = given[-1], made[-1]
+            kernel(layout, ids, tree, *views)
+
+    vmem = pl.BlockSpec(memory_space=pltpu.VMEM)
+    smem = pl.BlockSpec(memory_space=pltpu.SMEM)
+    specs = [smem, smem, *[vmem] * len(ins)]
+    if tie is not None:
+        specs[-1] = pl.BlockSpec(memory_space=pl.ANY)
     flops = count * 2 * products * (2 * rows * GROUP) * (len(blocks) * rows) * HEAD_SIZE
     return pl.pallas_call(
-        functools.partial(kernel, layout),
-        grid_spec=pltpu.PrefetchScalarGridSpec(
-            num_scalar_prefetch=2,
-            grid=(count,),
-            in_specs=specs,
-            out_specs=out_specs,
-        ),
+        body,
+        in_specs=specs,
+        out_specs=[vmem] * len(outs),
         out_shape=outs,
         compiler_params=pltpu.CompilerParams(vmem_limit_bytes=VMEM_BYTES),
         cost_estimate=pl.CostEstimate(
             flops=flops, bytes_accessed=count * 4 * 2 * rows * WIDTH * 2, transcendentals=0
         ),
-    )(*operands)
+    )(*scalars, *ins)
 
 
 def after(x, *tokens):
@@ -267,12 +302,13 @@
         if hop == 0:
             side = after(core, held[:16, :HEAD_SIZE])
             own_blocks = gathered((rotated_key_rows, value_matrix), side)
-            q_sib = send(columns(queries, 1 - side, HEADS * WIDTH), 1)
-            c_sib = send(columns(cotangent, 1 - side, HEADS * WIDTH), 1)
-            q_mine, c_mine = [columns(x, side, HEADS * WIDTH) for x in (queries, cotangent)]
-            work = (q_mine, q_sib, c_mine, c_sib)
+            q_mine, q_other, c_mine, c_other = halves(side, queries, cotangent)
+            q_sib, c_sib = send(q_other, 1), send(c_other, 1)
+        if hop == 1:
+            held, q_mine, q_sib, c_sib = lax.optimization_barrier((held, q_mine, q_sib, c_sib))
     width = KEY_VALUE_HEADS * HEAD_SIZE
     prompt = (held[:, :width], held[:, width:])
+    work = (q_mine, q_sib, c_mine, c_sib)
     prompt_blocks = gathered(prompt, core)
 
     near, far = (0, 1), (2, 3)

time: 78.3 us -> 77.4 us (0.989)
  local copies, waits for them, and re-layouts: 2.7 us -> 0.24 us
  Pallas kernels: 22 us -> 23.8 us
  starting transfers between devices: 24.9 us -> 25.8 us
    ppermute x14, starting transfers between devices: 6.25 us -> 8.22 us  [send(): return lax.ppermute(x, 'head', [(i, i ^ mask) for i in range(head_count)])]
    pallas_call x5 -> x6, Pallas kernels: 22 us -> 23.8 us  [the longest x5 21.1 us: call(): pl.pallas_call(body, in_specs=specs, out_specs=[vmem] * len(outs), out_sh...]
    dynamic_slice x2 -> x0, local copies, waits for them, and re-layouts: 1.65 us -> none  [columns(): return lax.dynamic_slice_in_dim(x, place * width, width, 1)]
    ppermute x2, waiting for transfers between devices: 6.24 us -> 4.8 us  [on_device(): lax.ppermute(total, 'seq', [(i + step, i) for i in range(0, seq_count, 2...]
    ppermute x2, waiting for transfers between devices: 3.94 us -> 5.28 us  [on_device(): got = lax.ppermute(held, 'seq', sends)]
    ppermute x2, starting transfers between devices: 3.56 us -> 2.6 us  [on_device(): got = lax.ppermute(held, 'seq', sends)]
    ppermute x2, waiting for transfers between devices: 2.7 us -> 3.53 us  [on_device(): got = jnp.concatenate([lax.ppermute(x, 'seq', sends) for x in held], axis=1)]
    slice x3, local copies, waits for them, and re-layouts: 0.93 us -> 0.13 us  [half(): parts += [k[:, part], v[:, part]]]
  transfers between devices with their start and end apart: 23 -> 23, of which waited for: 10 -> 12; matrix products, arithmetic and copies ran while one was open for 9% -> 5% of each run, Pallas kernels for 23% -> 26%
where the time goes in v5:
time: 77.4 us; the launch traced here: 77.1 us
  starting transfers between devices  25.8 us (33%)
  Pallas kernels  23.8 us (31%)
  waiting for transfers between devices  20.9 us (27%)
  other arithmetic  5.32 us (7%)
  between operations  1.04 us (1%)
    pallas_call x5, Pallas kernels, call(): pl.pallas_call(body, in_specs=specs, out_specs=[vmem] * len(outs), out_sh...  21.1 us
    ppermute x14, starting transfers between devices, send(): return lax.ppermute(x, 'head', [(i, i ^ mask) for i in range(head_count)])  8.22 us
    ppermute x2, starting transfers between devices, on_device(): got = jnp.concatenate([lax.ppermute(x, 'seq', sends) for x in held], axis=1)  6.18 us
    ppermute x3, starting transfers between devices, across(): return lax.ppermute(x, ('seq', 'head'), flat)  6.17 us
    ppermute x2, waiting for transfers between devices, on_device(): got = lax.ppermute(held, 'seq', sends)  5.28 us
    ppermute x14, waiting for transfers between devices, send(): return lax.ppermute(x, 'head', [(i, i ^ mask) for i in range(head_count)])  5.17 us
    ppermute x2, waiting for transfers between devices, on_device(): lax.ppermute(total, 'seq', [(i + step, i) for i in range(0, seq_count, 2...  4.8 us
    ppermute x2, waiting for transfers between devices, on_device(): got = jnp.concatenate([lax.ppermute(x, 'seq', sends) for x in held], axis=1)  3.53 us
  transfers between devices with their start and end apart: 23, of which 12 were waited for; matrix products, arithmetic and copies ran while one was open for 5% of the time, Pallas kernels for 26%

profile of v5, /device:TPU:0, one launch (start us, length us, event | category | flops | bytes accessed | tf_op | source)
XLA Modules:
  0.0 77.1 jit_solution(4389458363272050545)
XLA Ops:
  0.6 4.9 %collective-permute-start = (bf16[128,512]{1,0:T(8,128)(2,1)}, bf16[128,512]{1,0:T(8,128)(2,1)S(1)}, u32[]{:S(2)}, u32[]{:S(2)}) collective-permute-start(bf16[128,512]{1,0:T(8,128)(2,1)} %param.6), channel_id=1, source_target_pairs={{0,4},{1,5},{2,6},{3,7}} | collective-permute-start | bytes 393224 | tf_op jit(solution)/shard_map/ppermute | solution.py:299
  5.5 1.3 %collective-permute-start.1 = (bf16[128,512]{1,0:T(8,128)(2,1)}, bf16[128,512]{1,0:T(8,128)(2,1)S(1)}, u32[]{:S(2)}, u32[]{:S(2)}) collective-permute-start(bf16[128,512]{1,0:T(8,128)(2,1)} %param.7), channel_id=1, source_target_pairs={{0,4},{1,5},{2,6},{3,7}} | collective-permute-start | bytes 393224 | tf_op jit(solution)/shard_map/ppermute | solution.py:299
  6.8 1.0 %pad_maximum_fusion = bf16[128,1024]{1,0:T(8,128)(2,1)S(1)} fusion(bf16[128,512]{1,0:T(8,128)(2,1)} %param.7, bf16[128,512]{1,0:T(8,128)(2,1)} %param.6), kind=kLoop, calls=%fused_computation.7 | loop fusion | flops 524288 | bytes 524288 | tf_op jit(solution)/shard_map/concatenate | solution.py:300
  7.8 1.9 %collective-permute-done = bf16[128,512]{1,0:T(8,128)(2,1)S(1)} collective-permute-done((bf16[128,512]{1,0:T(8,128)(2,1)}, bf16[128,512]{1,0:T(8,128)(2,1)S(1)}, u32[]{:S(2)}, u32[]{:S(2)}) %collective-permute-start) | collective-permute-done | bytes 131104 | tf_op jit(solution)/shard_map/ppermute | solution.py:299
  9.7 1.7 %collective-permute-done.1 = bf16[128,512]{1,0:T(8,128)(2,1)S(1)} collective-permute-done((bf16[128,512]{1,0:T(8,128)(2,1)}, bf16[128,512]{1,0:T(8,128)(2,1)S(1)}, u32[]{:S(2)}, u32[]{:S(2)}) %collective-permute-start.1) | collective-permute-done | bytes 131104 | tf_op jit(solution)/shard_map/ppermute | solution.py:299
  11.4 0.1 maximum_select_fusion.2
  11.4 1.3 %collective-permute-start.2 = (bf16[128,1024]{1,0:T(8,128)(2,1)S(1)}, bf16[128,1024]{1,0:T(8,128)(2,1)S(1)}, u32[]{:S(2)}, u32[]{:S(2)}) collective-permute-start(bf16[128,1024]{1,0:T(8,128)(2,1)S(1)} %maximum_select_fusion.2), channel_id=1, source_target_pairs={{0,16},{4,20},{1,17},{5,21},{2,18},{6,22},{3,19},{7,23}} | collective-permute-start | bytes 786440 | tf_op jit(solution)/shard_map/ppermute | solution.py:296
  12.8 0.0 copy-start.3
  12.8 2.8 %shard_map.84 = (bf16[128,1792]{1,0:T(8,128)(2,1)}, bf16[128,1792]{1,0:T(8,128)(2,1)}, bf16[128,1792]{1,0:T(8,128)(2,1)}, bf16[128,1792]{1,0:T(8,128)(2,1)}) custom-call(s32[1]{0:T(128)} %bitcast.2.side, bf16[128,3584]{1,0:T(8,128)(2,1)} %q.1, bf16[128,3584]{1,0:T(8,128)(2,1)} %c.1), custom_call_target="tpu_custom_call" | custom-call | bytes 3670016 | tf_op jit(solution)/shard_map/pallas_call | solution.py:203
  15.5 0.0 copy-start.4
  15.5 0.1 collective-permute-start.3
  15.6 0.5 collective-permute-start.4
  16.1 1.5 %collective-permute-done.2 = bf16[128,1024]{1,0:T(8,128)(2,1)S(1)} collective-permute-done((bf16[128,1024]{1,0:T(8,128)(2,1)S(1)}, bf16[128,1024]{1,0:T(8,128)(2,1)S(1)}, u32[]{:S(2)}, u32[]{:S(2)}) %collective-permute-start.2) | collective-permute-done | bytes 262176 | tf_op jit(solution)/shard_map/ppermute | solution.py:296
  17.7 0.0 collective-permute-done.3.refs_1_
  17.7 0.6 collective-permute-done.4.refs_3_
  18.3 1.3 %collective-permute-start.8 = (bf16[128,1024]{1,0:T(8,128)(2,1)S(1)}, bf16[128,1024]{1,0:T(8,128)(2,1)S(1)}, u32[]{:S(2)}, u32[]{:S(2)}) collective-permute-start(bf16[128,1024]{1,0:T(8,128)(2,1)S(1)} %broadcast_select_fusion.1), channel_id=1, source_target_pairs={{0,8},{16,24},{4,12},{20,28},{1,9},{17,25},{5,13},{21,29},{2,10},{... | collective-permute-start | bytes 786440 | tf_op jit(solution)/shard_map/ppermute | solution.py:296
  19.7 1.3 %collective-permute-start.7 = (bf16[128,512]{1,0:T(8,128)(2,1)S(1)}, bf16[128,512]{1,0:T(8,128)(2,1)S(1)}, u32[]{:S(2)}, u32[]{:S(2)}) collective-permute-start(bf16[128,512]{1,0:T(8,128)(2,1)S(1)} %pad_maximum_fusion.3), channel_id=1, source_target_pairs={{0,3},{1,2},{2,1},{3,0},{4,7},{5,6},{6,5},{7,4},{8,11},{9,10},{10,... | collective-permute-start | bytes 393224 | tf_op jit(solution)/shard_map/ppermute | solution.py:267
  21.0 0.4 collective-permute-start.5
  21.4 0.6 collective-permute-start.6
  22.0 3.7 %collective-permute-done.8 = bf16[128,1024]{1,0:T(8,128)(2,1)S(1)} collective-permute-done((bf16[128,1024]{1,0:T(8,128)(2,1)S(1)}, bf16[128,1024]{1,0:T(8,128)(2,1)S(1)}, u32[]{:S(2)}, u32[]{:S(2)}) %collective-permute-start.8) | collective-permute-done | bytes 262176 | tf_op jit(solution)/shard_map/ppermute | solution.py:296
  25.7 0.0 copy-start
  25.8 0.0 copy-start.2
  25.8 0.1 constant_dynamic-slice_fusion
  25.9 0.1 collective-permute-start.9
  26.0 0.1 pad_add_fusion.ids
  26.1 1.6 %collective-permute-start.11 = (bf16[128,512]{1,0:T(8,128)(2,1)S(1)}, bf16[128,512]{1,0:T(8,128)(2,1)S(1)}, u32[]{:S(2)}, u32[]{:S(2)}) collective-permute-start(bf16[128,512]{1,0:T(8,128)(2,1)S(1)} %pad_maximum_fusion.5), channel_id=1, source_target_pairs={{0,3},{1,2},{2,1},{3,0},{4,7},{5,6},{6,5},{7,4},{8,11},{9,10},{10,... | collective-permute-start | bytes 393224 | tf_op jit(solution)/shard_map/ppermute | solution.py:267
  27.7 0.7 collective-permute-done.6.refs_6_
  28.3 1.5 %collective-permute-start.10 = (bf16[128,512]{1,0:T(8,128)(2,1)S(1)}, bf16[128,512]{1,0:T(8,128)(2,1)S(1)}, u32[]{:S(2)}, u32[]{:S(2)}) collective-permute-start(bf16[128,512]{1,0:T(8,128)(2,1)S(1)} %pad_maximum_fusion.4.refs_8_.refs_4_), channel_id=1, source_target_pairs={{0,2},{1,3},{2,0},{3,1},{4,6},{5,7},{6,4},{7,5},{8,10},{9,11},{10,... | collective-permute-start | bytes 393224 | tf_op jit(solution)/shard_map/ppermute | solution.py:267
  29.8 0.0 collective-permute-done.7.refs_7_
  29.8 0.0 collective-permute-done.5.refs_5_
  29.9 4.4 %shard_map.85.refs_6_ = f32[2,8,1792]{2,1,0:T(8,128)S(1)} custom-call(s32[2]{0:T(128)S(1)} %pad_add_fusion.ids, s32[4,4]{1,0:T(4,128)S(1)} %copy-done.2, bf16[128,1792]{1,0:T(8,128)(2,1)S(1)} %copy-done, bf16[128,1792]{1,0:T(8,128)(2,1)S(1)} %collective-permute-done.3.refs_1_, bf16[128,1792]{1,0:T(8,128)(2,1)S(1)} %copy-done.1, ...), custom_call_target="tpu_custom_call" | custom-call | flops 1409286144 | bytes 3670016 | tf_op jit(solution)/shard_map/pallas_call | solution.py:241
  34.3 0.4 collective-permute-done.10.refs_4_.refs_10_
  34.7 0.0 collective-permute-done.11.refs_5_.refs_11_
  34.7 3.5 %shard_map.86 = (f32[2,8,1792]{2,1,0:T(8,128)S(1)}, bf16[256,512]{1,0:T(8,128)(2,1)S(1)}) custom-call(s32[2]{0:T(128)S(1)} %pad_add_fusion.ids, s32[4,4]{1,0:T(4,128)S(1)} %copy-done.2, bf16[128,1792]{1,0:T(8,128)(2,1)S(1)} %copy-done, bf16[128,1792]{1,0:T(8,128)(2,1)S(1)} %collective-permute-done.3.refs_1_, bf16[128,1792]{1,0:T(8,128)(2,1)S(1)} %copy-done.1, ...), custom_call_target="tpu_custom_call" | custom-call | flops 939524096 | bytes 3670016 | tf_op jit(solution)/shard_map/pallas_call | solution.py:241
  38.2 1.3 %collective-permute-start.13 = (bf16[256,512]{1,0:T(8,128)(2,1)S(1)}, bf16[256,512]{1,0:T(8,128)(2,1)S(1)}, u32[]{:S(2)}, u32[]{:S(2)}) collective-permute-start(bf16[256,512]{1,0:T(8,128)(2,1)S(1)} %get-tuple-element.38), channel_id=1, source_target_pairs={{4,2},{12,10},{20,18},{28,26},{5,3},{13,11},{21,19},{29,27},{6,0},... | collective-permute-start | bytes 786440 | tf_op jit(solution)/shard_map/ppermute | solution.py:345
  39.5 3.4 %collective-permute-start.12 = (bf16[256,512]{1,0:T(8,128)(2,1)S(1)}, bf16[256,512]{1,0:T(8,128)(2,1)S(1)}, u32[]{:S(2)}, u32[]{:S(2)}) collective-permute-start(bf16[256,512]{1,0:T(8,128)(2,1)S(1)} %get-tuple-element.38), channel_id=1, source_target_pairs={{0,2},{8,10},{16,18},{24,26},{1,3},{9,11},{17,19},{25,27},{2,0},{1... | collective-permute-start | bytes 786440 | tf_op jit(solution)/shard_map/ppermute | solution.py:345
  42.9 2.8 %shard_map.87.refs_13_ = bf16[256,512]{1,0:T(8,128)(2,1)S(1)} custom-call(s32[2]{0:T(128)S(1)} %pad_add_fusion.ids, s32[4,4]{1,0:T(4,128)S(1)} %copy-done.2, bf16[128,1792]{1,0:T(8,128)(2,1)S(1)} %copy-done, bf16[128,1792]{1,0:T(8,128)(2,1)S(1)} %collective-permute-done.3.refs_1_, bf16[128,1792]{1,0:T(8,128)(2,1)S(1)} %copy-done.1, ...), custom_call_target="tpu_custom_call" | custom-call | flops 939524096 | bytes 3670016 | tf_op jit(solution)/shard_map/pallas_call | solution.py:241
  45.7 1.5 %collective-permute-start.14 = (bf16[256,512]{1,0:T(8,128)(2,1)S(1)}, bf16[256,512]{1,0:T(8,128)(2,1)S(1)}, u32[]{:S(2)}, u32[]{:S(2)}) collective-permute-start(bf16[256,512]{1,0:T(8,128)(2,1)S(1)} %shard_map.87.refs_13_), channel_id=1, source_target_pairs={{4,0},{12,8},{20,16},{28,24},{5,1},{13,9},{21,17},{29,25},{6,2},{1... | collective-permute-start | bytes 786440 | tf_op jit(solution)/shard_map/ppermute | solution.py:345
  47.2 5.2 %shard_map.88 = (bf16[128,896]{1,0:T(8,128)(2,1)S(1)}, bf16[128,896]{1,0:T(8,128)(2,1)S(1)}, bf16[128,896]{1,0:T(8,128)(2,1)S(1)}, bf16[128,896]{1,0:T(8,128)(2,...) custom-call(s32[2]{0:T(128)S(1)} %pad_add_fusion.ids, ...), custom_call_target="tpu_custom_call" | custom-call | flops 3758096384 | bytes 1835008 | tf_op jit(solution)/shard_map/pallas_call | solution.py:241
  52.4 0.1 collective-permute-start.15
  52.4 0.5 collective-permute-start.17
  52.9 2.1 %collective-permute-done.14 = bf16[256,512]{1,0:T(8,128)(2,1)S(1)} collective-permute-done((bf16[256,512]{1,0:T(8,128)(2,1)S(1)}, bf16[256,512]{1,0:T(8,128)(2,1)S(1)}, u32[]{:S(2)}, u32[]{:S(2)}) %collective-permute-start.14) | collective-permute-done | bytes 262176 | tf_op jit(solution)/shard_map/ppermute | solution.py:345
  55.0 0.0 collective-permute-done.13
  55.0 0.0 collective-permute-done.12
  55.0 0.2 add_convert_fusion.refs_13_
  55.2 1.3 %collective-permute-start.20 = (bf16[256,512]{1,0:T(8,128)(2,1)S(1)}, bf16[256,512]{1,0:T(8,128)(2,1)S(1)}, u32[]{:S(2)}, u32[]{:S(2)}) collective-permute-start(bf16[256,512]{1,0:T(8,128)(2,1)S(1)} %add_convert_fusion.refs_13_), channel_id=1, source_target_pairs={{8,0},{24,16},{9,1},{25,17},{10,2},{26,18},{11,3},{27,19}} | collective-permute-start | bytes 786440 | tf_op jit(solution)/shard_map/ppermute | solution.py:358
  56.5 5.2 %shard_map.89 = (bf16[128,896]{1,0:T(8,128)(2,1)S(1)}, bf16[128,896]{1,0:T(8,128)(2,1)S(1)}, bf16[128,896]{1,0:T(8,128)(2,1)S(1)}, bf16[128,896]{1,0:T(8,128)(2,...) custom-call(s32[2]{0:T(128)S(1)} %pad_add_fusion.ids, ...), custom_call_target="tpu_custom_call" | custom-call | flops 3758096384 | bytes 1835008 | tf_op jit(solution)/shard_map/pallas_call | solution.py:241
  61.7 0.1 collective-permute-start.16
  61.8 0.5 collective-permute-start.18
  62.3 1.5 %collective-permute-done.20 = bf16[256,512]{1,0:T(8,128)(2,1)S(1)} collective-permute-done((bf16[256,512]{1,0:T(8,128)(2,1)S(1)}, bf16[256,512]{1,0:T(8,128)(2,1)S(1)}, u32[]{:S(2)}, u32[]{:S(2)}) %collective-permute-start.20) | collective-permute-done | bytes 262176 | tf_op jit(solution)/shard_map/ppermute | solution.py:358
  63.7 1.0 %collective-permute-start.19 = (bf16[256,512]{1,0:T(8,128)(2,1)S(1)}, bf16[256,512]{1,0:T(8,128)(2,1)S(1)}, u32[]{:S(2)}, u32[]{:S(2)}) collective-permute-start(bf16[256,512]{1,0:T(8,128)(2,1)S(1)} %pad_maximum_fusion.1), channel_id=1, source_target_pairs={{0,2},{1,3},{2,0},{3,1},{4,6},{5,7},{6,4},{7,5},{8,10},{9,11},{10,... | collective-permute-start | bytes 786440 | tf_op jit(solution)/shard_map/ppermute | solution.py:267
  64.8 1.3 %collective-permute-start.21 = (bf16[256,512]{1,0:T(8,128)(2,1)S(1)}, bf16[256,512]{1,0:T(8,128)(2,1)S(1)}, u32[]{:S(2)}, u32[]{:S(2)}) collective-permute-start(bf16[256,512]{1,0:T(8,128)(2,1)S(1)} %add_add_fusion), channel_id=1, source_target_pairs={{16,0},{17,1},{18,2},{19,3}} | collective-permute-start | bytes 786440 | tf_op jit(solution)/shard_map/ppermute | solution.py:358
  66.1 0.0 collective-permute-done.16
  66.1 1.1 %maximum_select_fusion = bf16[128,3584]{1,0:T(8,128)(2,1)} fusion(bf16[128,896]{1,0:T(8,128)(2,1)S(1)} %collective-permute-done.16, bf16[128,896]{1,0:T(8,128)(2,1)S(1)} %collective-permute-done.15, bf16[128,896]{1,0:T(8,128)(2,1)S(1)} %get-tuple-element.40, bf16[128,896]{1,0:T(8,128)(2,1)S(1)} %get-tuple-element.37, pred[]{:T(512)S(6)} %eq.23), kind=kLoop, calls=%fused_computation | loop fusion | flops 7798784 | bytes 1835009 | tf_op jit(solution)/shard_map/jit(_where)/select_n | solution.py:381
  67.3 3.4 %collective-permute-done.19 = bf16[256,512]{1,0:T(8,128)(2,1)S(1)} collective-permute-done((bf16[256,512]{1,0:T(8,128)(2,1)S(1)}, bf16[256,512]{1,0:T(8,128)(2,1)S(1)}, u32[]{:S(2)}, u32[]{:S(2)}) %collective-permute-start.19) | collective-permute-done | bytes 262176 | tf_op jit(solution)/shard_map/ppermute | solution.py:267
  70.6 3.3 %collective-permute-done.21 = bf16[256,512]{1,0:T(8,128)(2,1)S(1)} collective-permute-done((bf16[256,512]{1,0:T(8,128)(2,1)S(1)}, bf16[256,512]{1,0:T(8,128)(2,1)S(1)}, u32[]{:S(2)}, u32[]{:S(2)}) %collective-permute-start.21) | collective-permute-done | bytes 262176 | tf_op jit(solution)/shard_map/ppermute | solution.py:358
  74.0 0.1 fusion.1
  74.2 0.1 collective-permute-start.22
  74.2 0.0 collective-permute-done.18
  74.3 1.1 %maximum_select_fusion.1 = bf16[128,3584]{1,0:T(8,128)(2,1)} fusion(bf16[128,896]{1,0:T(8,128)(2,1)S(1)} %collective-permute-done.18, bf16[128,896]{1,0:T(8,128)(2,1)S(1)} %collective-permute-done.17, bf16[128,896]{1,0:T(8,128)(2,1)S(1)} %get-tuple-element.44, bf16[128,896]{1,0:T(8,128)(2,1)S(1)} %get-tuple-element.43, pred[]{:T(512)S(6)} %eq.23), kind=kLoop, calls=%fused_computation.1 | loop fusion | flops 7798784 | bytes 1835009 | tf_op jit(solution)/shard_map/jit(_where)/select_n | solution.py:381
  75.4 0.2 collective-permute-done.22
  75.6 0.1 maximum_select_fusion.3
  75.7 0.7 pad_maximum_fusion.7
  76.4 0.7 pad_maximum_fusion.6
  (22 shorter events, 0.4 us)
Async XLA Ops:
  0.6 9.1 %collective-permute-start = (bf16[128,512]{1,0:T(8,128)(2,1)}, bf16[128,512]{1,0:T(8,128)(2,1)S(1)}, u32[]{:S(2)}, u32[]{:S(2)}) collective-permute-start(bf16[128,512]{1,0:T(8,128)(2,1)} %param.6), channel_id=1, source_target_pairs={{0,4},{1,5},{2,6},{3,7}} | collective-permute-start | bytes 393224 | tf_op jit(solution)/shard_map/ppermute | solution.py:299
  5.5 5.9 %collective-permute-start.1 = (bf16[128,512]{1,0:T(8,128)(2,1)}, bf16[128,512]{1,0:T(8,128)(2,1)S(1)}, u32[]{:S(2)}, u32[]{:S(2)}) collective-permute-start(bf16[128,512]{1,0:T(8,128)(2,1)} %param.7), channel_id=1, source_target_pairs={{0,4},{1,5},{2,6},{3,7}} | collective-permute-start | bytes 393224 | tf_op jit(solution)/shard_map/ppermute | solution.py:299
  11.4 6.3 %collective-permute-start.2 = (bf16[128,1024]{1,0:T(8,128)(2,1)S(1)}, bf16[128,1024]{1,0:T(8,128)(2,1)S(1)}, u32[]{:S(2)}, u32[]{:S(2)}) collective-permute-start(bf16[128,1024]{1,0:T(8,128)(2,1)S(1)} %maximum_select_fusion.2), channel_id=1, source_target_pairs={{0,16},{4,20},{1,17},{5,21},{2,18},{6,22},{3,19},{7,23}} | collective-permute-start | bytes 786440 | tf_op jit(solution)/shard_map/ppermute | solution.py:296
  12.8 3.4 %copy-start.3 = (bf16[128,512]{1,0:T(8,128)(2,1)S(1)}, bf16[128,512]{1,0:T(8,128)(2,1)}, u32[]{:S(2)}) copy-start(bf16[128,512]{1,0:T(8,128)(2,1)} %param.6) | copy-start | bytes 393220
  15.5 4.1 %copy-start.4 = (bf16[128,512]{1,0:T(8,128)(2,1)S(1)}, bf16[128,512]{1,0:T(8,128)(2,1)}, u32[]{:S(2)}) copy-start(bf16[128,512]{1,0:T(8,128)(2,1)} %param.7) | copy-start | bytes 393220
  15.5 2.2 %collective-permute-start.3 = (bf16[128,1792]{1,0:T(8,128)(2,1)}, bf16[128,1792]{1,0:T(8,128)(2,1)S(1)}, u32[]{:S(2)}, u32[]{:S(2)}) collective-permute-start(bf16[128,1792]{1,0:T(8,128)(2,1)} %get-tuple-element.29), channel_id=1, source_target_pairs={{0,1},{1,0},{2,3},{3,2},{4,5},{5,4},{6,7},{7,6},{8,9},{9,8},{10,11... | collective-permute-start | bytes 1376264 | tf_op jit(solution)/shard_map/ppermute | solution.py:267
  15.6 2.7 %collective-permute-start.4 = (bf16[128,1792]{1,0:T(8,128)(2,1)}, bf16[128,1792]{1,0:T(8,128)(2,1)S(1)}, u32[]{:S(2)}, u32[]{:S(2)}) collective-permute-start(bf16[128,1792]{1,0:T(8,128)(2,1)} %get-tuple-element.30), channel_id=1, source_target_pairs={{0,1},{1,0},{2,3},{3,2},{4,5},{5,4},{6,7},{7,6},{8,9},{9,8},{10,11... | collective-permute-start | bytes 1376264 | tf_op jit(solution)/shard_map/ppermute | solution.py:267
  18.3 7.4 %collective-permute-start.8 = (bf16[128,1024]{1,0:T(8,128)(2,1)S(1)}, bf16[128,1024]{1,0:T(8,128)(2,1)S(1)}, u32[]{:S(2)}, u32[]{:S(2)}) collective-permute-start(bf16[128,1024]{1,0:T(8,128)(2,1)S(1)} %broadcast_select_fusion.1), channel_id=1, source_target_pairs={{0,8},{16,24},{4,12},{20,28},{1,9},{17,25},{5,13},{21,29},{2,10},{... | collective-permute-start | bytes 786440 | tf_op jit(solution)/shard_map/ppermute | solution.py:296
  19.7 10.2 %collective-permute-start.7 = (bf16[128,512]{1,0:T(8,128)(2,1)S(1)}, bf16[128,512]{1,0:T(8,128)(2,1)S(1)}, u32[]{:S(2)}, u32[]{:S(2)}) collective-permute-start(bf16[128,512]{1,0:T(8,128)(2,1)S(1)} %pad_maximum_fusion.3), channel_id=1, source_target_pairs={{0,3},{1,2},{2,1},{3,0},{4,7},{5,6},{6,5},{7,4},{8,11},{9,10},{10,... | collective-permute-start | bytes 393224 | tf_op jit(solution)/shard_map/ppermute | solution.py:267
  21.0 8.9 %collective-permute-start.5 = (bf16[128,512]{1,0:T(8,128)(2,1)S(1)}, bf16[128,512]{1,0:T(8,128)(2,1)S(1)}, u32[]{:S(2)}, u32[]{:S(2)}) collective-permute-start(bf16[128,512]{1,0:T(8,128)(2,1)S(1)} %pad_maximum_fusion.3), channel_id=1, source_target_pairs={{0,1},{1,0},{2,3},{3,2},{4,5},{5,4},{6,7},{7,6},{8,9},{9,8},{10,11... | collective-permute-start | bytes 393224 | tf_op jit(solution)/shard_map/ppermute | solution.py:267
  21.4 7.0 %collective-permute-start.6 = (bf16[128,512]{1,0:T(8,128)(2,1)S(1)}, bf16[128,512]{1,0:T(8,128)(2,1)S(1)}, u32[]{:S(2)}, u32[]{:S(2)}) collective-permute-start(bf16[128,512]{1,0:T(8,128)(2,1)S(1)} %pad_maximum_fusion.2.refs_4_), channel_id=1, source_target_pairs={{0,2},{1,3},{2,0},{3,1},{4,6},{5,7},{6,4},{7,5},{8,10},{9,11},{10,... | collective-permute-start | bytes 393224 | tf_op jit(solution)/shard_map/ppermute | solution.py:267
  25.7 4.1 %copy-start = (bf16[128,1792]{1,0:T(8,128)(2,1)S(1)}, bf16[128,1792]{1,0:T(8,128)(2,1)}, u32[]{:S(2)}) copy-start(bf16[128,1792]{1,0:T(8,128)(2,1)} %get-tuple-element.31.refs_0_) | copy-start | bytes 1376260
  25.8 4.1 %copy-start.1 = (bf16[128,1792]{1,0:T(8,128)(2,1)S(1)}, bf16[128,1792]{1,0:T(8,128)(2,1)}, u32[]{:S(2)}) copy-start(bf16[128,1792]{1,0:T(8,128)(2,1)} %get-tuple-element.33.refs_2_) | copy-start | bytes 1376260
  25.8 4.1 %copy-start.2 = (s32[4,4]{1,0:T(4,128)S(1)}, s32[4,4]{1,0:T(4,128)}, u32[]{:S(2)}) copy-start(s32[4,4]{1,0:T(4,128)} %tree.9) | copy-start | bytes 196
  25.9 4.0 %collective-permute-start.9 = (bf16[128,512]{1,0:T(8,128)(2,1)S(1)}, bf16[128,512]{1,0:T(8,128)(2,1)S(1)}, u32[]{:S(2)}, u32[]{:S(2)}) collective-permute-start(bf16[128,512]{1,0:T(8,128)(2,1)S(1)} %pad_maximum_fusion.5), channel_id=1, source_target_pairs={{0,1},{1,0},{2,3},{3,2},{4,5},{5,4},{6,7},{7,6},{8,9},{9,8},{10,11... | collective-permute-start | bytes 393224 | tf_op jit(solution)/shard_map/ppermute | solution.py:267
  26.1 8.6 %collective-permute-start.11 = (bf16[128,512]{1,0:T(8,128)(2,1)S(1)}, bf16[128,512]{1,0:T(8,128)(2,1)S(1)}, u32[]{:S(2)}, u32[]{:S(2)}) collective-permute-start(bf16[128,512]{1,0:T(8,128)(2,1)S(1)} %pad_maximum_fusion.5), channel_id=1, source_target_pairs={{0,3},{1,2},{2,1},{3,0},{4,7},{5,6},{6,5},{7,4},{8,11},{9,10},{10,... | collective-permute-start | bytes 393224 | tf_op jit(solution)/shard_map/ppermute | solution.py:267
  28.3 6.3 %collective-permute-start.10 = (bf16[128,512]{1,0:T(8,128)(2,1)S(1)}, bf16[128,512]{1,0:T(8,128)(2,1)S(1)}, u32[]{:S(2)}, u32[]{:S(2)}) collective-permute-start(bf16[128,512]{1,0:T(8,128)(2,1)S(1)} %pad_maximum_fusion.4.refs_8_.refs_4_), channel_id=1, source_target_pairs={{0,2},{1,3},{2,0},{3,1},{4,6},{5,7},{6,4},{7,5},{8,10},{9,11},{10,... | collective-permute-start | bytes 393224 | tf_op jit(solution)/shard_map/ppermute | solution.py:267
  38.2 16.8 %collective-permute-start.13 = (bf16[256,512]{1,0:T(8,128)(2,1)S(1)}, bf16[256,512]{1,0:T(8,128)(2,1)S(1)}, u32[]{:S(2)}, u32[]{:S(2)}) collective-permute-start(bf16[256,512]{1,0:T(8,128)(2,1)S(1)} %get-tuple-element.38), channel_id=1, source_target_pairs={{4,2},{12,10},{20,18},{28,26},{5,3},{13,11},{21,19},{29,27},{6,0},... | collective-permute-start | bytes 786440 | tf_op jit(solution)/shard_map/ppermute | solution.py:345
  39.5 15.5 %collective-permute-start.12 = (bf16[256,512]{1,0:T(8,128)(2,1)S(1)}, bf16[256,512]{1,0:T(8,128)(2,1)S(1)}, u32[]{:S(2)}, u32[]{:S(2)}) collective-permute-start(bf16[256,512]{1,0:T(8,128)(2,1)S(1)} %get-tuple-element.38), channel_id=1, source_target_pairs={{0,2},{8,10},{16,18},{24,26},{1,3},{9,11},{17,19},{25,27},{2,0},{1... | collective-permute-start | bytes 786440 | tf_op jit(solution)/shard_map/ppermute | solution.py:345
  45.7 9.3 %collective-permute-start.14 = (bf16[256,512]{1,0:T(8,128)(2,1)S(1)}, bf16[256,512]{1,0:T(8,128)(2,1)S(1)}, u32[]{:S(2)}, u32[]{:S(2)}) collective-permute-start(bf16[256,512]{1,0:T(8,128)(2,1)S(1)} %shard_map.87.refs_13_), channel_id=1, source_target_pairs={{4,0},{12,8},{20,16},{28,24},{5,1},{13,9},{21,17},{29,25},{6,2},{1... | collective-permute-start | bytes 786440 | tf_op jit(solution)/shard_map/ppermute | solution.py:345
  52.4 12.5 %collective-permute-start.15 = (bf16[128,896]{1,0:T(8,128)(2,1)S(1)}, bf16[128,896]{1,0:T(8,128)(2,1)S(1)}, u32[]{:S(2)}, u32[]{:S(2)}) collective-permute-start(bf16[128,896]{1,0:T(8,128)(2,1)S(1)} %get-tuple-element.41), channel_id=1, source_target_pairs={{0,1},{1,0},{2,3},{3,2},{4,5},{5,4},{6,7},{7,6},{8,9},{9,8},{10,11... | collective-permute-start | bytes 688136 | tf_op jit(solution)/shard_map/ppermute | solution.py:267
  52.4 21.8 %collective-permute-start.17 = (bf16[128,896]{1,0:T(8,128)(2,1)S(1)}, bf16[128,896]{1,0:T(8,128)(2,1)S(1)}, u32[]{:S(2)}, u32[]{:S(2)}) collective-permute-start(bf16[128,896]{1,0:T(8,128)(2,1)S(1)} %get-tuple-element.45), channel_id=1, source_target_pairs={{0,1},{1,0},{2,3},{3,2},{4,5},{5,4},{6,7},{7,6},{8,9},{9,8},{10,11... | collective-permute-start | bytes 688136 | tf_op jit(solution)/shard_map/ppermute | solution.py:267
  55.2 8.5 %collective-permute-start.20 = (bf16[256,512]{1,0:T(8,128)(2,1)S(1)}, bf16[256,512]{1,0:T(8,128)(2,1)S(1)}, u32[]{:S(2)}, u32[]{:S(2)}) collective-permute-start(bf16[256,512]{1,0:T(8,128)(2,1)S(1)} %add_convert_fusion.refs_13_), channel_id=1, source_target_pairs={{8,0},{24,16},{9,1},{25,17},{10,2},{26,18},{11,3},{27,19}} | collective-permute-start | bytes 786440 | tf_op jit(solution)/shard_map/ppermute | solution.py:358
  61.7 4.4 %collective-permute-start.16 = (bf16[128,896]{1,0:T(8,128)(2,1)S(1)}, bf16[128,896]{1,0:T(8,128)(2,1)S(1)}, u32[]{:S(2)}, u32[]{:S(2)}) collective-permute-start(bf16[128,896]{1,0:T(8,128)(2,1)S(1)} %get-tuple-element.42), channel_id=1, source_target_pairs={{0,1},{1,0},{2,3},{3,2},{4,5},{5,4},{6,7},{7,6},{8,9},{9,8},{10,11... | collective-permute-start | bytes 688136 | tf_op jit(solution)/shard_map/ppermute | solution.py:267
  61.8 12.5 %collective-permute-start.18 = (bf16[128,896]{1,0:T(8,128)(2,1)S(1)}, bf16[128,896]{1,0:T(8,128)(2,1)S(1)}, u32[]{:S(2)}, u32[]{:S(2)}) collective-permute-start(bf16[128,896]{1,0:T(8,128)(2,1)S(1)} %get-tuple-element.46), channel_id=1, source_target_pairs={{0,1},{1,0},{2,3},{3,2},{4,5},{5,4},{6,7},{7,6},{8,9},{9,8},{10,11... | collective-permute-start | bytes 688136 | tf_op jit(solution)/shard_map/ppermute | solution.py:267
  63.7 6.9 %collective-permute-start.19 = (bf16[256,512]{1,0:T(8,128)(2,1)S(1)}, bf16[256,512]{1,0:T(8,128)(2,1)S(1)}, u32[]{:S(2)}, u32[]{:S(2)}) collective-permute-start(bf16[256,512]{1,0:T(8,128)(2,1)S(1)} %pad_maximum_fusion.1), channel_id=1, source_target_pairs={{0,2},{1,3},{2,0},{3,1},{4,6},{5,7},{6,4},{7,5},{8,10},{9,11},{10,... | collective-permute-start | bytes 786440 | tf_op jit(solution)/shard_map/ppermute | solution.py:267
  64.8 9.2 %collective-permute-start.21 = (bf16[256,512]{1,0:T(8,128)(2,1)S(1)}, bf16[256,512]{1,0:T(8,128)(2,1)S(1)}, u32[]{:S(2)}, u32[]{:S(2)}) collective-permute-start(bf16[256,512]{1,0:T(8,128)(2,1)S(1)} %add_add_fusion), channel_id=1, source_target_pairs={{16,0},{17,1},{18,2},{19,3}} | collective-permute-start | bytes 786440 | tf_op jit(solution)/shard_map/ppermute | solution.py:358
  74.2 1.4 %collective-permute-start.22 = (bf16[128,512]{1,0:T(8,128)(2,1)S(1)}, bf16[128,512]{1,0:T(8,128)(2,1)S(1)}, u32[]{:S(2)}, u32[]{:S(2)}) collective-permute-start(bf16[128,512]{1,0:T(8,128)(2,1)S(1)} %get-tuple-element.61), channel_id=1, source_target_pairs={{0,1},{1,0},{2,3},{3,2},{4,5},{5,4},{6,7},{7,6},{8,9},{9,8},{10,11... | collective-permute-start | bytes 393224 | tf_op jit(solution)/shard_map/ppermute | solution.py:267

commit v6 on v5

--- a/solution.py
+++ b/solution.py
@@ -17,7 +17,7 @@
 SCALE = HEAD_SIZE ** (-0.5)
 EXP2_SCALE = SCALE * math.log2(math.e)
 MASKED = -1e30
-VMEM_BYTES = 16 * 1024 * 1024
+VMEM_BYTES = 32 * 1024 * 1024
 
 
 def dot_nt(a, b):
@@ -121,30 +121,32 @@
     return jnp.concatenate([x.astype(jnp.bfloat16) for x in parts], axis=0)
 
 
-def stats_kernel(layout, ids, tree, qm, qs, cm, cs, *refs):
+def put_rows(x, mine, sibling, rows):
+    for g in range(GROUP):
+        columns = slice(g * HEAD_SIZE, (g + 1) * HEAD_SIZE)
+        for i, out in enumerate((mine, sibling)):
+            part = slice((2 * g + i) * rows, (2 * g + i + 1) * rows)
+            out[:, columns] = x[:, part].T.astype(out.dtype)
+
+
+def forward_kernel(layout, ids, tree, qm, qs, cm, cs, *refs):
     k = Keys(layout, ids, tree, qm, qs, cm, cs, refs)
-    (stats,) = k.refs
+    stats, terms, att_m, att_s = k.refs
     scores = k.scores()
     top = k.top(scores)
     e = k.weights(scores, top)
-    delta = column_sum([x * y for x, y in zip(e, k.dprobs())])
-    put_stats(stats, top, column_sum(e), delta)
-
-
-def last_keys_kernel(layout, ids, tree, qm, qs, cm, cs, *refs):
-    k = Keys(layout, ids, tree, qm, qs, cm, cs, refs)
-    old, stats, terms = k.refs
-    scores, dprobs = k.scores(), k.dprobs()
-    old_top = old[0, 0:1, :]
-    top = jnp.maximum(k.top(scores), old_top)
-    keep = jnp.exp2((old_top - top) * EXP2_SCALE)
-    e = k.weights(scores, top)
-    inverse = 1.0 / (column_sum(e) + old[0, 1:2, :] * keep)
-    delta = column_sum([x * y for x, y in zip(e, dprobs)]) + old[0, 2:3, :] * keep
-    delta = delta * inverse
+    inverse = 1.0 / column_sum(e)
+    probs = [x * inverse for x in e]
+    all_rounded = rounded(probs)
+    att = dot_nn(k.values.T, all_rounded).astype(jnp.bfloat16).astype(jnp.float32)
+    delta = jnp.sum(att * k.ct.T.astype(jnp.float32), axis=0, keepdims=True)
     put_stats(stats, top, inverse, delta)
-    probs = [x * inverse for x in e]
-    put_terms(terms, rounded([p * (d - delta) for p, d in zip(probs, dprobs)]), rounded(probs), k)
+    last = terms.shape[0] // k.rows
+    dprobs = dot_nt(k.values[-terms.shape[0] :], k.ct)
+    dprobs = [dprobs[i * k.rows : (i + 1) * k.rows] for i in range(last)]
+    dscore = rounded([p * (d - delta) for p, d in zip(probs[-last:], dprobs)])
+    put_terms(terms, dscore, all_rounded[-terms.shape[0] :], k)
+    put_rows(att, att_m, att_s, k.rows)
 
 
 def probs_dscore(k, stats):
@@ -163,21 +165,14 @@
 
 def rows_kernel(layout, ids, tree, qm, qs, cm, cs, *refs):
     k = Keys(layout, ids, tree, qm, qs, cm, cs, refs)
-    stats, _, att_m, att_s, dq_m, dq_s, near, far, token = k.refs
+    stats, _, dq_m, dq_s, near, far, token = k.refs
     token[...] = jnp.zeros_like(token)
     rows = k.rows
     probs, dscore = probs_dscore(k, stats)
     half = near.shape[0]
     put_terms(near, dscore[:half], probs[:half], k)
     put_terms(far, dscore[half : 2 * half], probs[half : 2 * half], k)
-    att = dot_nn(k.values.T, probs)
-    dq = dot_nn(k.keys.T, dscore) * SCALE
-    for g in range(GROUP):
-        columns = slice(g * HEAD_SIZE, (g + 1) * HEAD_SIZE)
-        for i, (a, d) in enumerate(((att_m, dq_m), (att_s, dq_s))):
-            part = slice((2 * g + i) * rows, (2 * g + i + 1) * rows)
-            a[:, columns] = att[:, part].T.astype(jnp.bfloat16)
-            d[:, columns] = dq[:, part].T.astype(jnp.bfloat16)
+    put_rows(dot_nn(k.keys.T, dscore) * SCALE, dq_m, dq_s, rows)
 
 
 def halves_kernel(side, q, c, q_mine, q_other, c_mine, c_other, done):
@@ -321,13 +316,12 @@
     def terms_shape(count, dtype):
         return shape((2 * rows, 2 * count * HEAD_SIZE), dtype)
 
-    layout = own_all + tuple((prompt_bias, b) for b in near)
-    blocks = [*own_blocks, *prompt_blocks[:2]]
-    stats = call(stats_kernel, layout, every, scalars, work, blocks, [], [stats_shape()], 2)[0]
-    layout = tuple((prompt_bias, b) for b in far)
-    outs = [stats_shape(), terms_shape(HEADS, bf16)]
-    stats, terms_far = call(
-        last_keys_kernel, layout, every, scalars, work, prompt_blocks[2:], [stats], outs, 4
+    layout = own_all + tuple((prompt_bias, b) for b in near + far)
+    blocks = [*own_blocks, *prompt_blocks]
+    rows_shape = shape((rows, HEADS * WIDTH), bf16)
+    outs = [stats_shape(), terms_shape(HEADS, bf16), rows_shape, rows_shape]
+    stats, terms_far, att_m, att_s = call(
+        forward_kernel, layout, every, scalars, work, blocks, [], outs, 5
     )
     layout = tuple((prompt_bias, b) for b in near)
     outs = [terms_shape(HEADS, bf16)]
@@ -350,18 +344,17 @@
     got_next = across(terms, [(i + 1, i, 0) for i in even])
     layout = own_all + tuple((prompt_bias, b) for b in near + far)
     blocks = [*own_blocks, *prompt_blocks]
-    att, dq, own_sums = [], [], []
+    dq, own_sums = [], []
     total, tie = None, terms
     step, hop = 1, 0
     while step < seq_count:
         if hop:
             got = lax.ppermute(total, "seq", [(i + step, i) for i in range(0, seq_count, 2 * step)])
         if hop < HEADS:
-            outs = [shape((rows, WIDTH), bf16)] * 4 + [terms_shape(1, f32), terms_shape(1, bf16)]
-            a_m, a_s, d_m, d_s, own_near, own_far, token = call(
+            outs = [shape((rows, WIDTH), bf16)] * 2 + [terms_shape(1, f32), terms_shape(1, bf16)]
+            d_m, d_s, own_near, own_far, token = call(
                 rows_kernel, layout, (hop, one), scalars, work, blocks, [stats], outs, 8, tie
             )
-            att.append((a_m, send(a_s, 1)))
             dq.append((d_m, send(d_s, 1)))
             own_sums.append((own_near, own_far))
         else:
@@ -384,7 +377,7 @@
             jnp.concatenate([theirs, mine], axis=1),
         )
 
-    attention, query_grad = both_halves(att), both_halves(dq)
+    attention, query_grad = both_halves([(att_m, send(att_s, 1))]), both_halves(dq)
     total = jnp.where(s == 0, total.astype(f32), jnp.float32(0.0))
     own_near, own_far = [jnp.concatenate(x, axis=1) for x in zip(*own_sums)]
     total = (plus(own_near, send(own_far, 2)) + total).astype(bf16)

time: 77.4 us -> 82.8 us (1.070)
  waiting for transfers between devices: 20.9 us -> 30.7 us
  starting transfers between devices: 25.8 us -> 23.2 us
  Pallas kernels: 23.8 us -> 22 us
    ppermute x2, waiting for transfers between devices: 4.8 us -> 9.41 us  [on_device(): lax.ppermute(total, 'seq', [(i + step, i) for i in range(0, seq_count, 2...]
    ppermute x14 -> x13, waiting for transfers between devices: 5.17 us -> 8.36 us  [send(): return lax.ppermute(x, 'head', [(i, i ^ mask) for i in range(head_count)])]
    ppermute x3, waiting for transfers between devices: 2.1 us -> 4.11 us  [across(): return lax.ppermute(x, ('seq', 'head'), flat)]
    ppermute x14 -> x13, starting transfers between devices: 8.22 us -> 6.31 us  [send(): return lax.ppermute(x, 'head', [(i, i ^ mask) for i in range(head_count)])]
    pallas_call x5 -> x4, Pallas kernels: 21.1 us -> 19.2 us  [call(): pl.pallas_call(body, in_specs=specs, out_specs=[vmem] * len(outs), out_sh...]
  transfers between devices with their start and end apart: 23 -> 22, of which waited for: 12 -> 13; matrix products, arithmetic and copies ran while one was open for 5% -> 5% of each run, Pallas kernels for 26% -> 17%
where the time goes in v6:
time: 82.8 us; the launch traced here: 82.5 us
  waiting for transfers between devices  30.7 us (37%)
  starting transfers between devices  23.2 us (28%)
  Pallas kernels  22 us (27%)
  other arithmetic  5.34 us (6%)
  between operations  1.01 us (1%)
    pallas_call x4, Pallas kernels, call(): pl.pallas_call(body, in_specs=specs, out_specs=[vmem] * len(outs), out_sh...  19.2 us
    ppermute x2, waiting for transfers between devices, on_device(): lax.ppermute(total, 'seq', [(i + step, i) for i in range(0, seq_count, 2...  9.41 us
    ppermute x13, waiting for transfers between devices, send(): return lax.ppermute(x, 'head', [(i, i ^ mask) for i in range(head_count)])  8.36 us
    ppermute x13, starting transfers between devices, send(): return lax.ppermute(x, 'head', [(i, i ^ mask) for i in range(head_count)])  6.31 us
    ppermute x2, starting transfers between devices, on_device(): got = jnp.concatenate([lax.ppermute(x, 'seq', sends) for x in held], axis=1)  6.18 us
    ppermute x3, starting transfers between devices, across(): return lax.ppermute(x, ('seq', 'head'), flat)  5.57 us
    ppermute x2, waiting for transfers between devices, on_device(): got = lax.ppermute(held, 'seq', sends)  5.28 us
    ppermute x3, waiting for transfers between devices, across(): return lax.ppermute(x, ('seq', 'head'), flat)  4.11 us
  transfers between devices with their start and end apart: 22, of which 13 were waited for; matrix products, arithmetic and copies ran while one was open for 5% of the time, Pallas kernels for 17%

profile of v6, /device:TPU:0, one launch (start us, length us, event | category | flops | bytes accessed | tf_op | source)
XLA Modules:
  0.0 82.5 jit_solution(8979946641680742712)
XLA Ops:
  0.6 4.9 %collective-permute-start = (bf16[128,512]{1,0:T(8,128)(2,1)}, bf16[128,512]{1,0:T(8,128)(2,1)S(1)}, u32[]{:S(2)}, u32[]{:S(2)}) collective-permute-start(bf16[128,512]{1,0:T(8,128)(2,1)} %param.6), channel_id=1, source_target_pairs={{0,4},{1,5},{2,6},{3,7}} | collective-permute-start | bytes 393224 | tf_op jit(solution)/shard_map/ppermute | solution.py:294
  5.5 1.3 %collective-permute-start.1 = (bf16[128,512]{1,0:T(8,128)(2,1)}, bf16[128,512]{1,0:T(8,128)(2,1)S(1)}, u32[]{:S(2)}, u32[]{:S(2)}) collective-permute-start(bf16[128,512]{1,0:T(8,128)(2,1)} %param.7), channel_id=1, source_target_pairs={{0,4},{1,5},{2,6},{3,7}} | collective-permute-start | bytes 393224 | tf_op jit(solution)/shard_map/ppermute | solution.py:294
  6.8 1.0 %pad_maximum_fusion = bf16[128,1024]{1,0:T(8,128)(2,1)S(1)} fusion(bf16[128,512]{1,0:T(8,128)(2,1)} %param.7, bf16[128,512]{1,0:T(8,128)(2,1)} %param.6), kind=kLoop, calls=%fused_computation.7 | loop fusion | flops 524288 | bytes 524288 | tf_op jit(solution)/shard_map/concatenate | solution.py:295
  7.8 1.9 %collective-permute-done = bf16[128,512]{1,0:T(8,128)(2,1)S(1)} collective-permute-done((bf16[128,512]{1,0:T(8,128)(2,1)}, bf16[128,512]{1,0:T(8,128)(2,1)S(1)}, u32[]{:S(2)}, u32[]{:S(2)}) %collective-permute-start) | collective-permute-done | bytes 131104 | tf_op jit(solution)/shard_map/ppermute | solution.py:294
  9.7 1.7 %collective-permute-done.1 = bf16[128,512]{1,0:T(8,128)(2,1)S(1)} collective-permute-done((bf16[128,512]{1,0:T(8,128)(2,1)}, bf16[128,512]{1,0:T(8,128)(2,1)S(1)}, u32[]{:S(2)}, u32[]{:S(2)}) %collective-permute-start.1) | collective-permute-done | bytes 131104 | tf_op jit(solution)/shard_map/ppermute | solution.py:294
  11.4 0.1 maximum_select_fusion.2
  11.4 1.3 %collective-permute-start.2 = (bf16[128,1024]{1,0:T(8,128)(2,1)S(1)}, bf16[128,1024]{1,0:T(8,128)(2,1)S(1)}, u32[]{:S(2)}, u32[]{:S(2)}) collective-permute-start(bf16[128,1024]{1,0:T(8,128)(2,1)S(1)} %maximum_select_fusion.2), channel_id=1, source_target_pairs={{0,16},{4,20},{1,17},{5,21},{2,18},{6,22},{3,19},{7,23}} | collective-permute-start | bytes 786440 | tf_op jit(solution)/shard_map/ppermute | solution.py:291
  12.8 0.0 copy-start.3
  12.8 2.8 %shard_map.84 = (bf16[128,1792]{1,0:T(8,128)(2,1)}, bf16[128,1792]{1,0:T(8,128)(2,1)}, bf16[128,1792]{1,0:T(8,128)(2,1)}, bf16[128,1792]{1,0:T(8,128)(2,1)}) custom-call(s32[1]{0:T(128)} %bitcast.2.side, bf16[128,3584]{1,0:T(8,128)(2,1)} %q.1, bf16[128,3584]{1,0:T(8,128)(2,1)} %c.1), custom_call_target="tpu_custom_call" | custom-call | bytes 3670016 | tf_op jit(solution)/shard_map/pallas_call | solution.py:198
  15.5 0.0 copy-start.4
  15.5 0.1 collective-permute-start.3
  15.6 0.5 collective-permute-start.4
  16.2 1.5 %collective-permute-done.2 = bf16[128,1024]{1,0:T(8,128)(2,1)S(1)} collective-permute-done((bf16[128,1024]{1,0:T(8,128)(2,1)S(1)}, bf16[128,1024]{1,0:T(8,128)(2,1)S(1)}, u32[]{:S(2)}, u32[]{:S(2)}) %collective-permute-start.2) | collective-permute-done | bytes 262176 | tf_op jit(solution)/shard_map/ppermute | solution.py:291
  17.7 0.0 collective-permute-done.3.refs_1_
  17.7 0.6 collective-permute-done.4.refs_3_
  18.3 1.3 %collective-permute-start.8 = (bf16[128,1024]{1,0:T(8,128)(2,1)S(1)}, bf16[128,1024]{1,0:T(8,128)(2,1)S(1)}, u32[]{:S(2)}, u32[]{:S(2)}) collective-permute-start(bf16[128,1024]{1,0:T(8,128)(2,1)S(1)} %broadcast_select_fusion.1), channel_id=1, source_target_pairs={{0,8},{16,24},{4,12},{20,28},{1,9},{17,25},{5,13},{21,29},{2,10},{... | collective-permute-start | bytes 786440 | tf_op jit(solution)/shard_map/ppermute | solution.py:291
  19.7 1.3 %collective-permute-start.7 = (bf16[128,512]{1,0:T(8,128)(2,1)S(1)}, bf16[128,512]{1,0:T(8,128)(2,1)S(1)}, u32[]{:S(2)}, u32[]{:S(2)}) collective-permute-start(bf16[128,512]{1,0:T(8,128)(2,1)S(1)} %pad_maximum_fusion.3), channel_id=1, source_target_pairs={{0,3},{1,2},{2,1},{3,0},{4,7},{5,6},{6,5},{7,4},{8,11},{9,10},{10,... | collective-permute-start | bytes 393224 | tf_op jit(solution)/shard_map/ppermute | solution.py:262
  21.0 0.4 collective-permute-start.5
  21.4 0.6 collective-permute-start.6
  22.0 3.7 %collective-permute-done.8 = bf16[128,1024]{1,0:T(8,128)(2,1)S(1)} collective-permute-done((bf16[128,1024]{1,0:T(8,128)(2,1)S(1)}, bf16[128,1024]{1,0:T(8,128)(2,1)S(1)}, u32[]{:S(2)}, u32[]{:S(2)}) %collective-permute-start.8) | collective-permute-done | bytes 262176 | tf_op jit(solution)/shard_map/ppermute | solution.py:291
  25.7 0.0 copy-start
  25.8 0.0 copy-start.2
  25.8 0.1 constant_dynamic-slice_fusion
  25.9 1.6 %collective-permute-start.10 = (bf16[128,512]{1,0:T(8,128)(2,1)S(1)}, bf16[128,512]{1,0:T(8,128)(2,1)S(1)}, u32[]{:S(2)}, u32[]{:S(2)}) collective-permute-start(bf16[128,512]{1,0:T(8,128)(2,1)S(1)} %pad_maximum_fusion.4.refs_8_.refs_4_), channel_id=1, source_target_pairs={{0,2},{1,3},{2,0},{3,1},{4,6},{5,7},{6,4},{7,5},{8,10},{9,11},{10,... | collective-permute-start | bytes 393224 | tf_op jit(solution)/shard_map/ppermute | solution.py:262
  27.5 0.1 collective-permute-start.11
  27.6 0.9 %collective-permute-done.6.refs_6_ = bf16[128,512]{1,0:T(8,128)(2,1)S(1)} collective-permute-done((bf16[128,512]{1,0:T(8,128)(2,1)S(1)}, bf16[128,512]{1,0:T(8,128)(2,1)S(1)}, u32[]{:S(2)}, u32[]{:S(2)}) %collective-permute-start.6) | collective-permute-done | bytes 131104 | tf_op jit(solution)/shard_map/ppermute | solution.py:262
  28.4 0.0 collective-permute-start.9
  28.5 0.1 pad_add_fusion.ids
  28.5 0.0 collective-permute-done.7.refs_7_
  28.5 0.0 collective-permute-done.5.refs_5_
  28.5 3.3 %collective-permute-done.10.refs_10_ = bf16[128,512]{1,0:T(8,128)(2,1)S(1)} collective-permute-done((bf16[128,512]{1,0:T(8,128)(2,1)S(1)}, bf16[128,512]{1,0:T(8,128)(2,1)S(1)}, u32[]{:S(2)}, u32[]{:S(2)}) %collective-permute-start.10) | collective-permute-done | bytes 131104 | tf_op jit(solution)/shard_map/ppermute | solution.py:262
  31.8 1.6 %collective-permute-done.11.refs_11_ = bf16[128,512]{1,0:T(8,128)(2,1)S(1)} collective-permute-done((bf16[128,512]{1,0:T(8,128)(2,1)S(1)}, bf16[128,512]{1,0:T(8,128)(2,1)S(1)}, u32[]{:S(2)}, u32[]{:S(2)}) %collective-permute-start.11) | collective-permute-done | bytes 131104 | tf_op jit(solution)/shard_map/ppermute | solution.py:262
  33.3 0.0 collective-permute-done.9.refs_9_.refs_5_
  33.4 7.7 %shard_map.85 = (f32[2,8,1792]{2,1,0:T(8,128)S(1)}, bf16[256,512]{1,0:T(8,128)(2,1)S(1)}, bf16[128,1792]{1,0:T(8,128)(2,1)S(1)}, bf16[128,1792]{1,0:T(8,128)(2,1)S(1)}) custom-call(s32[2]{0:T(128)S(1)} %pad_add_fusion.ids, s32[4,4]{1,0:T(4,128)S(1)} %copy-done.2, bf16[128,1792]{1,0:T(8,128)(2,1)S(1)} %copy-done, ...), custom_call_target="tpu_custom_call" | custom-call | flops 4697620480 | bytes 3670016 | tf_op jit(solution)/shard_map/pallas_call | solution.py:236
  41.1 1.3 %collective-permute-start.14 = (bf16[256,512]{1,0:T(8,128)(2,1)S(1)}, bf16[256,512]{1,0:T(8,128)(2,1)S(1)}, u32[]{:S(2)}, u32[]{:S(2)}) collective-permute-start(bf16[256,512]{1,0:T(8,128)(2,1)S(1)} %get-tuple-element.38), channel_id=1, source_target_pairs={{4,2},{12,10},{20,18},{28,26},{5,3},{13,11},{21,19},{29,27},{6,0},... | collective-permute-start | bytes 786440 | tf_op jit(solution)/shard_map/ppermute | solution.py:339
  42.4 2.8 %collective-permute-start.13 = (bf16[256,512]{1,0:T(8,128)(2,1)S(1)}, bf16[256,512]{1,0:T(8,128)(2,1)S(1)}, u32[]{:S(2)}, u32[]{:S(2)}) collective-permute-start(bf16[256,512]{1,0:T(8,128)(2,1)S(1)} %get-tuple-element.38), channel_id=1, source_target_pairs={{0,2},{8,10},{16,18},{24,26},{1,3},{9,11},{17,19},{25,27},{2,0},{1... | collective-permute-start | bytes 786440 | tf_op jit(solution)/shard_map/ppermute | solution.py:339
  45.2 2.8 %shard_map.86.refs_13_ = bf16[256,512]{1,0:T(8,128)(2,1)S(1)} custom-call(s32[2]{0:T(128)S(1)} %pad_add_fusion.ids, s32[4,4]{1,0:T(4,128)S(1)} %copy-done.2, bf16[128,1792]{1,0:T(8,128)(2,1)S(1)} %copy-done, bf16[128,1792]{1,0:T(8,128)(2,1)S(1)} %collective-permute-done.3.refs_1_, bf16[128,1792]{1,0:T(8,128)(2,1)S(1)} %copy-done.1, ...), custom_call_target="tpu_custom_call" | custom-call | flops 939524096 | bytes 3670016 | tf_op jit(solution)/shard_map/pallas_call | solution.py:236
  48.0 1.5 %collective-permute-start.15 = (bf16[256,512]{1,0:T(8,128)(2,1)S(1)}, bf16[256,512]{1,0:T(8,128)(2,1)S(1)}, u32[]{:S(2)}, u32[]{:S(2)}) collective-permute-start(bf16[256,512]{1,0:T(8,128)(2,1)S(1)} %shard_map.86.refs_13_), channel_id=1, source_target_pairs={{4,0},{12,8},{20,16},{28,24},{5,1},{13,9},{21,17},{29,25},{6,2},{1... | collective-permute-start | bytes 786440 | tf_op jit(solution)/shard_map/ppermute | solution.py:339
  49.5 0.8 %collective-permute-start.12 = (bf16[128,1792]{1,0:T(8,128)(2,1)S(1)}, bf16[128,1792]{1,0:T(8,128)(2,1)S(1)}, u32[]{:S(2)}, u32[]{:S(2)}) collective-permute-start(bf16[128,1792]{1,0:T(8,128)(2,1)S(1)} %get-tuple-element.35), channel_id=1, source_target_pairs={{0,1},{1,0},{2,3},{3,2},{4,5},{5,4},{6,7},{7,6},{8,9},{9,8},{10,11... | collective-permute-start | bytes 1376264 | tf_op jit(solution)/shard_map/ppermute | solution.py:262
  50.3 4.4 %shard_map.87 = (bf16[128,896]{1,0:T(8,128)(2,1)S(1)}, bf16[128,896]{1,0:T(8,128)(2,1)S(1)}, f32[256,256]{1,0:T(8,128)S(1)}, bf16[256,256]{1,0:T(8,128)(2,1)S(1)}, bf16[256,512]{1,0:T(8,128)(2,1)S(1)}) custom-call(s32[2]{0:T(128)S(1)} %pad_add_fusion.ids, s32[4,4]{1,0:T(4,128)S(1)} %copy-done.2, bf16[128,1792]{1,0:T(8,128)(2,1)S(1)} %copy-done, ...), custom_call_target="tpu_custom_call" | custom-call | flops 3758096384 | bytes 1835008 | tf_op jit(solution)/shard_map/pallas_call | solution.py:236
  54.7 0.1 collective-permute-start.16
  54.7 4.1 %collective-permute-done.15 = bf16[256,512]{1,0:T(8,128)(2,1)S(1)} collective-permute-done((bf16[256,512]{1,0:T(8,128)(2,1)S(1)}, bf16[256,512]{1,0:T(8,128)(2,1)S(1)}, u32[]{:S(2)}, u32[]{:S(2)}) %collective-permute-start.15) | collective-permute-done | bytes 262176 | tf_op jit(solution)/shard_map/ppermute | solution.py:339
  58.9 0.0 collective-permute-done.14
  58.9 0.0 collective-permute-done.13
  58.9 0.2 add_convert_fusion.refs_13_
  59.0 1.3 %collective-permute-start.19 = (bf16[256,512]{1,0:T(8,128)(2,1)S(1)}, bf16[256,512]{1,0:T(8,128)(2,1)S(1)}, u32[]{:S(2)}, u32[]{:S(2)}) collective-permute-start(bf16[256,512]{1,0:T(8,128)(2,1)S(1)} %add_convert_fusion.refs_13_), channel_id=1, source_target_pairs={{8,0},{24,16},{9,1},{25,17},{10,2},{26,18},{11,3},{27,19}} | collective-permute-start | bytes 786440 | tf_op jit(solution)/shard_map/ppermute | solution.py:352
  60.3 4.4 %shard_map.88 = (bf16[128,896]{1,0:T(8,128)(2,1)S(1)}, bf16[128,896]{1,0:T(8,128)(2,1)S(1)}, f32[256,256]{1,0:T(8,128)S(1)}, bf16[256,256]{1,0:T(8,128)(2,1)S(1)}, bf16[256,512]{1,0:T(8,128)(2,1)S(1)}) custom-call(s32[2]{0:T(128)S(1)} %pad_add_fusion.ids, s32[4,4]{1,0:T(4,128)S(1)} %copy-done.2, bf16[128,1792]{1,0:T(8,128)(2,1)S(1)} %copy-done, ...), custom_call_target="tpu_custom_call" | custom-call | flops 3758096384 | bytes 1835008 | tf_op jit(solution)/shard_map/pallas_call | solution.py:236
  64.7 0.1 collective-permute-start.17
  64.8 0.8 collective-permute-start.18
  65.6 3.6 %collective-permute-done.19 = bf16[256,512]{1,0:T(8,128)(2,1)S(1)} collective-permute-done((bf16[256,512]{1,0:T(8,128)(2,1)S(1)}, bf16[256,512]{1,0:T(8,128)(2,1)S(1)}, u32[]{:S(2)}, u32[]{:S(2)}) %collective-permute-start.19) | collective-permute-done | bytes 262176 | tf_op jit(solution)/shard_map/ppermute | solution.py:352
  69.2 1.3 %collective-permute-start.20 = (bf16[256,512]{1,0:T(8,128)(2,1)S(1)}, bf16[256,512]{1,0:T(8,128)(2,1)S(1)}, u32[]{:S(2)}, u32[]{:S(2)}) collective-permute-start(bf16[256,512]{1,0:T(8,128)(2,1)S(1)} %add_add_fusion), channel_id=1, source_target_pairs={{16,0},{17,1},{18,2},{19,3}} | collective-permute-start | bytes 786440 | tf_op jit(solution)/shard_map/ppermute | solution.py:352
  70.5 0.0 collective-permute-done.12
  70.5 1.1 %maximum_select_fusion = bf16[128,3584]{1,0:T(8,128)(2,1)} fusion(bf16[128,1792]{1,0:T(8,128)(2,1)S(1)} %collective-permute-done.12, bf16[128,1792]{1,0:T(8,128)(2,1)S(1)} %get-tuple-element.34, pred[]{:T(512)S(6)} %eq.23), kind=kLoop, calls=%fused_computation | loop fusion | flops 4128768 | bytes 1835009 | tf_op jit(solution)/shard_map/jit(_where)/select_n | solution.py:374
  71.7 1.9 %collective-permute-done.18 = bf16[256,512]{1,0:T(8,128)(2,1)S(1)} collective-permute-done((bf16[256,512]{1,0:T(8,128)(2,1)S(1)}, bf16[256,512]{1,0:T(8,128)(2,1)S(1)}, u32[]{:S(2)}, u32[]{:S(2)}) %collective-permute-start.18) | collective-permute-done | bytes 262176 | tf_op jit(solution)/shard_map/ppermute | solution.py:262
  73.6 5.8 %collective-permute-done.20 = bf16[256,512]{1,0:T(8,128)(2,1)S(1)} collective-permute-done((bf16[256,512]{1,0:T(8,128)(2,1)S(1)}, bf16[256,512]{1,0:T(8,128)(2,1)S(1)}, u32[]{:S(2)}, u32[]{:S(2)}) %collective-permute-start.20) | collective-permute-done | bytes 262176 | tf_op jit(solution)/shard_map/ppermute | solution.py:352
  79.4 0.1 fusion.1
  79.6 0.1 collective-permute-start.21
  79.7 0.0 collective-permute-done.16
  79.7 0.0 collective-permute-done.17
  79.7 1.1 %maximum_select_fusion.1 = bf16[128,3584]{1,0:T(8,128)(2,1)} fusion(bf16[128,896]{1,0:T(8,128)(2,1)S(1)} %collective-permute-done.17, bf16[128,896]{1,0:T(8,128)(2,1)S(1)} %collective-permute-done.16, bf16[128,896]{1,0:T(8,128)(2,1)S(1)} %get-tuple-element.40, bf16[128,896]{1,0:T(8,128)(2,1)S(1)} %get-tuple-element.37, pred[]{:T(512)S(6)} %eq.23), kind=kLoop, calls=%fused_computation.1 | loop fusion | flops 7798784 | bytes 1835009 | tf_op jit(solution)/shard_map/jit(_where)/select_n | solution.py:374
  80.8 0.2 collective-permute-done.21
  81.0 0.1 maximum_select_fusion.3
  81.1 0.7 pad_maximum_fusion.7
  81.8 0.7 pad_maximum_fusion.6
  (19 shorter events, 0.4 us)
Async XLA Ops:
  0.6 9.1 %collective-permute-start = (bf16[128,512]{1,0:T(8,128)(2,1)}, bf16[128,512]{1,0:T(8,128)(2,1)S(1)}, u32[]{:S(2)}, u32[]{:S(2)}) collective-permute-start(bf16[128,512]{1,0:T(8,128)(2,1)} %param.6), channel_id=1, source_target_pairs={{0,4},{1,5},{2,6},{3,7}} | collective-permute-start | bytes 393224 | tf_op jit(solution)/shard_map/ppermute | solution.py:294
  5.5 5.9 %collective-permute-start.1 = (bf16[128,512]{1,0:T(8,128)(2,1)}, bf16[128,512]{1,0:T(8,128)(2,1)S(1)}, u32[]{:S(2)}, u32[]{:S(2)}) collective-permute-start(bf16[128,512]{1,0:T(8,128)(2,1)} %param.7), channel_id=1, source_target_pairs={{0,4},{1,5},{2,6},{3,7}} | collective-permute-start | bytes 393224 | tf_op jit(solution)/shard_map/ppermute | solution.py:294
  11.4 6.3 %collective-permute-start.2 = (bf16[128,1024]{1,0:T(8,128)(2,1)S(1)}, bf16[128,1024]{1,0:T(8,128)(2,1)S(1)}, u32[]{:S(2)}, u32[]{:S(2)}) collective-permute-start(bf16[128,1024]{1,0:T(8,128)(2,1)S(1)} %maximum_select_fusion.2), channel_id=1, source_target_pairs={{0,16},{4,20},{1,17},{5,21},{2,18},{6,22},{3,19},{7,23}} | collective-permute-start | bytes 786440 | tf_op jit(solution)/shard_map/ppermute | solution.py:291
  12.8 3.4 %copy-start.3 = (bf16[128,512]{1,0:T(8,128)(2,1)S(1)}, bf16[128,512]{1,0:T(8,128)(2,1)}, u32[]{:S(2)}) copy-start(bf16[128,512]{1,0:T(8,128)(2,1)} %param.6) | copy-start | bytes 393220
  15.5 4.1 %copy-start.4 = (bf16[128,512]{1,0:T(8,128)(2,1)S(1)}, bf16[128,512]{1,0:T(8,128)(2,1)}, u32[]{:S(2)}) copy-start(bf16[128,512]{1,0:T(8,128)(2,1)} %param.7) | copy-start | bytes 393220
  15.5 2.2 %collective-permute-start.3 = (bf16[128,1792]{1,0:T(8,128)(2,1)}, bf16[128,1792]{1,0:T(8,128)(2,1)S(1)}, u32[]{:S(2)}, u32[]{:S(2)}) collective-permute-start(bf16[128,1792]{1,0:T(8,128)(2,1)} %get-tuple-element.27), channel_id=1, source_target_pairs={{0,1},{1,0},{2,3},{3,2},{4,5},{5,4},{6,7},{7,6},{8,9},{9,8},{10,11... | collective-permute-start | bytes 1376264 | tf_op jit(solution)/shard_map/ppermute | solution.py:262
  15.6 2.7 %collective-permute-start.4 = (bf16[128,1792]{1,0:T(8,128)(2,1)}, bf16[128,1792]{1,0:T(8,128)(2,1)S(1)}, u32[]{:S(2)}, u32[]{:S(2)}) collective-permute-start(bf16[128,1792]{1,0:T(8,128)(2,1)} %get-tuple-element.28), channel_id=1, source_target_pairs={{0,1},{1,0},{2,3},{3,2},{4,5},{5,4},{6,7},{7,6},{8,9},{9,8},{10,11... | collective-permute-start | bytes 1376264 | tf_op jit(solution)/shard_map/ppermute | solution.py:262
  18.3 7.4 %collective-permute-start.8 = (bf16[128,1024]{1,0:T(8,128)(2,1)S(1)}, bf16[128,1024]{1,0:T(8,128)(2,1)S(1)}, u32[]{:S(2)}, u32[]{:S(2)}) collective-permute-start(bf16[128,1024]{1,0:T(8,128)(2,1)S(1)} %broadcast_select_fusion.1), channel_id=1, source_target_pairs={{0,8},{16,24},{4,12},{20,28},{1,9},{17,25},{5,13},{21,29},{2,10},{... | collective-permute-start | bytes 786440 | tf_op jit(solution)/shard_map/ppermute | solution.py:291
  19.7 8.8 %collective-permute-start.7 = (bf16[128,512]{1,0:T(8,128)(2,1)S(1)}, bf16[128,512]{1,0:T(8,128)(2,1)S(1)}, u32[]{:S(2)}, u32[]{:S(2)}) collective-permute-start(bf16[128,512]{1,0:T(8,128)(2,1)S(1)} %pad_maximum_fusion.3), channel_id=1, source_target_pairs={{0,3},{1,2},{2,1},{3,0},{4,7},{5,6},{6,5},{7,4},{8,11},{9,10},{10,... | collective-permute-start | bytes 393224 | tf_op jit(solution)/shard_map/ppermute | solution.py:262
  21.0 7.6 %collective-permute-start.5 = (bf16[128,512]{1,0:T(8,128)(2,1)S(1)}, bf16[128,512]{1,0:T(8,128)(2,1)S(1)}, u32[]{:S(2)}, u32[]{:S(2)}) collective-permute-start(bf16[128,512]{1,0:T(8,128)(2,1)S(1)} %pad_maximum_fusion.3), channel_id=1, source_target_pairs={{0,1},{1,0},{2,3},{3,2},{4,5},{5,4},{6,7},{7,6},{8,9},{9,8},{10,11... | collective-permute-start | bytes 393224 | tf_op jit(solution)/shard_map/ppermute | solution.py:262
  21.4 7.1 %collective-permute-start.6 = (bf16[128,512]{1,0:T(8,128)(2,1)S(1)}, bf16[128,512]{1,0:T(8,128)(2,1)S(1)}, u32[]{:S(2)}, u32[]{:S(2)}) collective-permute-start(bf16[128,512]{1,0:T(8,128)(2,1)S(1)} %pad_maximum_fusion.2.refs_4_), channel_id=1, source_target_pairs={{0,2},{1,3},{2,0},{3,1},{4,6},{5,7},{6,4},{7,5},{8,10},{9,11},{10,... | collective-permute-start | bytes 393224 | tf_op jit(solution)/shard_map/ppermute | solution.py:262
  25.7 7.6 %copy-start = (bf16[128,1792]{1,0:T(8,128)(2,1)S(1)}, bf16[128,1792]{1,0:T(8,128)(2,1)}, u32[]{:S(2)}) copy-start(bf16[128,1792]{1,0:T(8,128)(2,1)} %get-tuple-element.29.refs_0_) | copy-start | bytes 1376260
  25.8 7.6 %copy-start.1 = (bf16[128,1792]{1,0:T(8,128)(2,1)S(1)}, bf16[128,1792]{1,0:T(8,128)(2,1)}, u32[]{:S(2)}) copy-start(bf16[128,1792]{1,0:T(8,128)(2,1)} %get-tuple-element.31.refs_2_) | copy-start | bytes 1376260
  25.8 7.6 %copy-start.2 = (s32[4,4]{1,0:T(4,128)S(1)}, s32[4,4]{1,0:T(4,128)}, u32[]{:S(2)}) copy-start(s32[4,4]{1,0:T(4,128)} %tree.7) | copy-start | bytes 196
  25.9 5.9 %collective-permute-start.10 = (bf16[128,512]{1,0:T(8,128)(2,1)S(1)}, bf16[128,512]{1,0:T(8,128)(2,1)S(1)}, u32[]{:S(2)}, u32[]{:S(2)}) collective-permute-start(bf16[128,512]{1,0:T(8,128)(2,1)S(1)} %pad_maximum_fusion.4.refs_8_.refs_4_), channel_id=1, source_target_pairs={{0,2},{1,3},{2,0},{3,1},{4,6},{5,7},{6,4},{7,5},{8,10},{9,11},{10,... | collective-permute-start | bytes 393224 | tf_op jit(solution)/shard_map/ppermute | solution.py:262
  27.5 5.9 %collective-permute-start.11 = (bf16[128,512]{1,0:T(8,128)(2,1)S(1)}, bf16[128,512]{1,0:T(8,128)(2,1)S(1)}, u32[]{:S(2)}, u32[]{:S(2)}) collective-permute-start(bf16[128,512]{1,0:T(8,128)(2,1)S(1)} %pad_maximum_fusion.5), channel_id=1, source_target_pairs={{0,3},{1,2},{2,1},{3,0},{4,7},{5,6},{6,5},{7,4},{8,11},{9,10},{10,... | collective-permute-start | bytes 393224 | tf_op jit(solution)/shard_map/ppermute | solution.py:262
  28.4 4.9 %collective-permute-start.9 = (bf16[128,512]{1,0:T(8,128)(2,1)S(1)}, bf16[128,512]{1,0:T(8,128)(2,1)S(1)}, u32[]{:S(2)}, u32[]{:S(2)}) collective-permute-start(bf16[128,512]{1,0:T(8,128)(2,1)S(1)} %pad_maximum_fusion.5), channel_id=1, source_target_pairs={{0,1},{1,0},{2,3},{3,2},{4,5},{5,4},{6,7},{7,6},{8,9},{9,8},{10,11... | collective-permute-start | bytes 393224 | tf_op jit(solution)/shard_map/ppermute | solution.py:262
  41.1 17.8 %collective-permute-start.14 = (bf16[256,512]{1,0:T(8,128)(2,1)S(1)}, bf16[256,512]{1,0:T(8,128)(2,1)S(1)}, u32[]{:S(2)}, u32[]{:S(2)}) collective-permute-start(bf16[256,512]{1,0:T(8,128)(2,1)S(1)} %get-tuple-element.38), channel_id=1, source_target_pairs={{4,2},{12,10},{20,18},{28,26},{5,3},{13,11},{21,19},{29,27},{6,0},... | collective-permute-start | bytes 786440 | tf_op jit(solution)/shard_map/ppermute | solution.py:339
  42.4 16.5 %collective-permute-start.13 = (bf16[256,512]{1,0:T(8,128)(2,1)S(1)}, bf16[256,512]{1,0:T(8,128)(2,1)S(1)}, u32[]{:S(2)}, u32[]{:S(2)}) collective-permute-start(bf16[256,512]{1,0:T(8,128)(2,1)S(1)} %get-tuple-element.38), channel_id=1, source_target_pairs={{0,2},{8,10},{16,18},{24,26},{1,3},{9,11},{17,19},{25,27},{2,0},{1... | collective-permute-start | bytes 786440 | tf_op jit(solution)/shard_map/ppermute | solution.py:339
  48.0 10.9 %collective-permute-start.15 = (bf16[256,512]{1,0:T(8,128)(2,1)S(1)}, bf16[256,512]{1,0:T(8,128)(2,1)S(1)}, u32[]{:S(2)}, u32[]{:S(2)}) collective-permute-start(bf16[256,512]{1,0:T(8,128)(2,1)S(1)} %shard_map.86.refs_13_), channel_id=1, source_target_pairs={{4,0},{12,8},{20,16},{28,24},{5,1},{13,9},{21,17},{29,25},{6,2},{1... | collective-permute-start | bytes 786440 | tf_op jit(solution)/shard_map/ppermute | solution.py:339
  49.5 21.1 %collective-permute-start.12 = (bf16[128,1792]{1,0:T(8,128)(2,1)S(1)}, bf16[128,1792]{1,0:T(8,128)(2,1)S(1)}, u32[]{:S(2)}, u32[]{:S(2)}) collective-permute-start(bf16[128,1792]{1,0:T(8,128)(2,1)S(1)} %get-tuple-element.35), channel_id=1, source_target_pairs={{0,1},{1,0},{2,3},{3,2},{4,5},{5,4},{6,7},{7,6},{8,9},{9,8},{10,11... | collective-permute-start | bytes 1376264 | tf_op jit(solution)/shard_map/ppermute | solution.py:262
  54.7 25.0 %collective-permute-start.16 = (bf16[128,896]{1,0:T(8,128)(2,1)S(1)}, bf16[128,896]{1,0:T(8,128)(2,1)S(1)}, u32[]{:S(2)}, u32[]{:S(2)}) collective-permute-start(bf16[128,896]{1,0:T(8,128)(2,1)S(1)} %get-tuple-element.41), channel_id=1, source_target_pairs={{0,1},{1,0},{2,3},{3,2},{4,5},{5,4},{6,7},{7,6},{8,9},{9,8},{10,11... | collective-permute-start | bytes 688136 | tf_op jit(solution)/shard_map/ppermute | solution.py:262
  59.0 10.1 %collective-permute-start.19 = (bf16[256,512]{1,0:T(8,128)(2,1)S(1)}, bf16[256,512]{1,0:T(8,128)(2,1)S(1)}, u32[]{:S(2)}, u32[]{:S(2)}) collective-permute-start(bf16[256,512]{1,0:T(8,128)(2,1)S(1)} %add_convert_fusion.refs_13_), channel_id=1, source_target_pairs={{8,0},{24,16},{9,1},{25,17},{10,2},{26,18},{11,3},{27,19}} | collective-permute-start | bytes 786440 | tf_op jit(solution)/shard_map/ppermute | solution.py:352
  64.7 15.0 %collective-permute-start.17 = (bf16[128,896]{1,0:T(8,128)(2,1)S(1)}, bf16[128,896]{1,0:T(8,128)(2,1)S(1)}, u32[]{:S(2)}, u32[]{:S(2)}) collective-permute-start(bf16[128,896]{1,0:T(8,128)(2,1)S(1)} %get-tuple-element.42), channel_id=1, source_target_pairs={{0,1},{1,0},{2,3},{3,2},{4,5},{5,4},{6,7},{7,6},{8,9},{9,8},{10,11... | collective-permute-start | bytes 688136 | tf_op jit(solution)/shard_map/ppermute | solution.py:262
  64.8 8.8 %collective-permute-start.18 = (bf16[256,512]{1,0:T(8,128)(2,1)S(1)}, bf16[256,512]{1,0:T(8,128)(2,1)S(1)}, u32[]{:S(2)}, u32[]{:S(2)}) collective-permute-start(bf16[256,512]{1,0:T(8,128)(2,1)S(1)} %pad_maximum_fusion.1), channel_id=1, source_target_pairs={{0,2},{1,3},{2,0},{3,1},{4,6},{5,7},{6,4},{7,5},{8,10},{9,11},{10,... | collective-permute-start | bytes 786440 | tf_op jit(solution)/shard_map/ppermute | solution.py:262
  69.2 10.2 %collective-permute-start.20 = (bf16[256,512]{1,0:T(8,128)(2,1)S(1)}, bf16[256,512]{1,0:T(8,128)(2,1)S(1)}, u32[]{:S(2)}, u32[]{:S(2)}) collective-permute-start(bf16[256,512]{1,0:T(8,128)(2,1)S(1)} %add_add_fusion), channel_id=1, source_target_pairs={{16,0},{17,1},{18,2},{19,3}} | collective-permute-start | bytes 786440 | tf_op jit(solution)/shard_map/ppermute | solution.py:352
  79.6 1.4 %collective-permute-start.21 = (bf16[128,512]{1,0:T(8,128)(2,1)S(1)}, bf16[128,512]{1,0:T(8,128)(2,1)S(1)}, u32[]{:S(2)}, u32[]{:S(2)}) collective-permute-start(bf16[128,512]{1,0:T(8,128)(2,1)S(1)} %get-tuple-element.57), channel_id=1, source_target_pairs={{0,1},{1,0},{2,3},{3,2},{4,5},{5,4},{6,7},{7,6},{8,9},{9,8},{10,11... | collective-permute-start | bytes 393224 | tf_op jit(solution)/shard_map/ppermute | solution.py:262

commit v7 on v6

--- a/solution.py
+++ b/solution.py
@@ -131,14 +131,16 @@
 
 def forward_kernel(layout, ids, tree, qm, qs, cm, cs, *refs):
     k = Keys(layout, ids, tree, qm, qs, cm, cs, refs)
-    stats, terms, att_m, att_s = k.refs
+    stats, terms, att_t = k.refs
     scores = k.scores()
     top = k.top(scores)
     e = k.weights(scores, top)
     inverse = 1.0 / column_sum(e)
     probs = [x * inverse for x in e]
     all_rounded = rounded(probs)
-    att = dot_nn(k.values.T, all_rounded).astype(jnp.bfloat16).astype(jnp.float32)
+    att = dot_nn(k.values.T, all_rounded).astype(jnp.bfloat16)
+    att_t[0] = att
+    att = att.astype(jnp.float32)
     delta = jnp.sum(att * k.ct.T.astype(jnp.float32), axis=0, keepdims=True)
     put_stats(stats, top, inverse, delta)
     last = terms.shape[0] // k.rows
@@ -146,7 +148,6 @@
     dprobs = [dprobs[i * k.rows : (i + 1) * k.rows] for i in range(last)]
     dscore = rounded([p * (d - delta) for p, d in zip(probs[-last:], dprobs)])
     put_terms(terms, dscore, all_rounded[-terms.shape[0] :], k)
-    put_rows(att, att_m, att_s, k.rows)
 
 
 def probs_dscore(k, stats):
@@ -165,13 +166,14 @@
 
 def rows_kernel(layout, ids, tree, qm, qs, cm, cs, *refs):
     k = Keys(layout, ids, tree, qm, qs, cm, cs, refs)
-    stats, _, dq_m, dq_s, near, far, token = k.refs
+    stats, att_t, _, att_m, att_s, dq_m, dq_s, near, far, token = k.refs
     token[...] = jnp.zeros_like(token)
     rows = k.rows
     probs, dscore = probs_dscore(k, stats)
     half = near.shape[0]
     put_terms(near, dscore[:half], probs[:half], k)
     put_terms(far, dscore[half : 2 * half], probs[half : 2 * half], k)
+    put_rows(att_t[0], att_m, att_s, rows)
     put_rows(dot_nn(k.keys.T, dscore) * SCALE, dq_m, dq_s, rows)
 
 
@@ -318,9 +320,9 @@
 
     layout = own_all + tuple((prompt_bias, b) for b in near + far)
     blocks = [*own_blocks, *prompt_blocks]
-    rows_shape = shape((rows, HEADS * WIDTH), bf16)
-    outs = [stats_shape(), terms_shape(HEADS, bf16), rows_shape, rows_shape]
-    stats, terms_far, att_m, att_s = call(
+    att_shape = shape((HEADS, HEAD_SIZE, 2 * GROUP * rows), bf16)
+    outs = [stats_shape(), terms_shape(HEADS, bf16), att_shape]
+    stats, terms_far, att_t = call(
         forward_kernel, layout, every, scalars, work, blocks, [], outs, 5
     )
     layout = tuple((prompt_bias, b) for b in near)
@@ -344,17 +346,18 @@
     got_next = across(terms, [(i + 1, i, 0) for i in even])
     layout = own_all + tuple((prompt_bias, b) for b in near + far)
     blocks = [*own_blocks, *prompt_blocks]
-    dq, own_sums = [], []
+    att, dq, own_sums = [], [], []
     total, tie = None, terms
     step, hop = 1, 0
     while step < seq_count:
         if hop:
             got = lax.ppermute(total, "seq", [(i + step, i) for i in range(0, seq_count, 2 * step)])
         if hop < HEADS:
-            outs = [shape((rows, WIDTH), bf16)] * 2 + [terms_shape(1, f32), terms_shape(1, bf16)]
-            d_m, d_s, own_near, own_far, token = call(
-                rows_kernel, layout, (hop, one), scalars, work, blocks, [stats], outs, 8, tie
+            outs = [shape((rows, WIDTH), bf16)] * 4 + [terms_shape(1, f32), terms_shape(1, bf16)]
+            a_m, a_s, d_m, d_s, own_near, own_far, token = call(
+                rows_kernel, layout, (hop, one), scalars, work, blocks, [stats, att_t], outs, 8, tie
             )
+            att.append((a_m, send(a_s, 1)))
             dq.append((d_m, send(d_s, 1)))
             own_sums.append((own_near, own_far))
         else:
@@ -377,7 +380,7 @@
             jnp.concatenate([theirs, mine], axis=1),
         )
 
-    attention, query_grad = both_halves([(att_m, send(att_s, 1))]), both_halves(dq)
+    attention, query_grad = both_halves(att), both_halves(dq)
     total = jnp.where(s == 0, total.astype(f32), jnp.float32(0.0))
     own_near, own_far = [jnp.concatenate(x, axis=1) for x in zip(*own_sums)]
     total = (plus(own_near, send(own_far, 2)) + total).astype(bf16)

time: 82.8 us -> 82.7 us (level)
    ppermute x13 -> x14, waiting for transfers between devices: 8.36 us -> 11.1 us  [send(): return lax.ppermute(x, 'head', [(i, i ^ mask) for i in range(head_count)])]
    ppermute x2, waiting for transfers between devices: 9.41 us -> 6.71 us  [on_device(): lax.ppermute(total, 'seq', [(i + step, i) for i in range(0, seq_count, 2...]
    ppermute x13 -> x14, starting transfers between devices: 6.31 us -> 6.19 us  [send(): return lax.ppermute(x, 'head', [(i, i ^ mask) for i in range(head_count)])]
  transfers between devices with their start and end apart: 22 -> 23, of which waited for: 13 -> 13; matrix products, arithmetic and copies ran while one was open for 5% -> 5% of each run, Pallas kernels for 17% -> 17%
where the time goes in v7:
time: 82.7 us; the launch traced here: 82.4 us
  waiting for transfers between devices  30.8 us (37%)
  starting transfers between devices  23.1 us (28%)
  Pallas kernels  21.9 us (26%)
  other arithmetic  5.33 us (6%)
  between operations  1.01 us (1%)
    pallas_call x4, Pallas kernels, call(): pl.pallas_call(body, in_specs=specs, out_specs=[vmem] * len(outs), out_sh...  19.2 us
    ppermute x14, waiting for transfers between devices, send(): return lax.ppermute(x, 'head', [(i, i ^ mask) for i in range(head_count)])  11.1 us
    ppermute x2, waiting for transfers between devices, on_device(): lax.ppermute(total, 'seq', [(i + step, i) for i in range(0, seq_count, 2...  6.71 us
    ppermute x14, starting transfers between devices, send(): return lax.ppermute(x, 'head', [(i, i ^ mask) for i in range(head_count)])  6.19 us
    ppermute x2, starting transfers between devices, on_device(): got = jnp.concatenate([lax.ppermute(x, 'seq', sends) for x in held], axis=1)  6.18 us
    ppermute x3, starting transfers between devices, across(): return lax.ppermute(x, ('seq', 'head'), flat)  5.57 us
    ppermute x2, waiting for transfers between devices, on_device(): got = lax.ppermute(held, 'seq', sends)  5.28 us
    ppermute x3, waiting for transfers between devices, across(): return lax.ppermute(x, ('seq', 'head'), flat)  4.11 us
  transfers between devices with their start and end apart: 23, of which 13 were waited for; matrix products, arithmetic and copies ran while one was open for 5% of the time, Pallas kernels for 17%

profile of v7, /device:TPU:0, one launch (start us, length us, event | category | flops | bytes accessed | tf_op | source)
XLA Modules:
  0.0 82.4 jit_solution(7470076241430327757)
XLA Ops:
  0.6 4.9 %collective-permute-start = (bf16[128,512]{1,0:T(8,128)(2,1)}, bf16[128,512]{1,0:T(8,128)(2,1)S(1)}, u32[]{:S(2)}, u32[]{:S(2)}) collective-permute-start(bf16[128,512]{1,0:T(8,128)(2,1)} %param.6), channel_id=1, source_target_pairs={{0,4},{1,5},{2,6},{3,7}} | collective-permute-start | bytes 393224 | tf_op jit(solution)/shard_map/ppermute | solution.py:296
  5.5 1.3 %collective-permute-start.1 = (bf16[128,512]{1,0:T(8,128)(2,1)}, bf16[128,512]{1,0:T(8,128)(2,1)S(1)}, u32[]{:S(2)}, u32[]{:S(2)}) collective-permute-start(bf16[128,512]{1,0:T(8,128)(2,1)} %param.7), channel_id=1, source_target_pairs={{0,4},{1,5},{2,6},{3,7}} | collective-permute-start | bytes 393224 | tf_op jit(solution)/shard_map/ppermute | solution.py:296
  6.8 1.0 %pad_maximum_fusion = bf16[128,1024]{1,0:T(8,128)(2,1)S(1)} fusion(bf16[128,512]{1,0:T(8,128)(2,1)} %param.7, bf16[128,512]{1,0:T(8,128)(2,1)} %param.6), kind=kLoop, calls=%fused_computation.7 | loop fusion | flops 524288 | bytes 524288 | tf_op jit(solution)/shard_map/concatenate | solution.py:297
  7.8 1.9 %collective-permute-done = bf16[128,512]{1,0:T(8,128)(2,1)S(1)} collective-permute-done((bf16[128,512]{1,0:T(8,128)(2,1)}, bf16[128,512]{1,0:T(8,128)(2,1)S(1)}, u32[]{:S(2)}, u32[]{:S(2)}) %collective-permute-start) | collective-permute-done | bytes 131104 | tf_op jit(solution)/shard_map/ppermute | solution.py:296
  9.7 1.7 %collective-permute-done.1 = bf16[128,512]{1,0:T(8,128)(2,1)S(1)} collective-permute-done((bf16[128,512]{1,0:T(8,128)(2,1)}, bf16[128,512]{1,0:T(8,128)(2,1)S(1)}, u32[]{:S(2)}, u32[]{:S(2)}) %collective-permute-start.1) | collective-permute-done | bytes 131104 | tf_op jit(solution)/shard_map/ppermute | solution.py:296
  11.4 0.1 maximum_select_fusion.2
  11.4 1.3 %collective-permute-start.2 = (bf16[128,1024]{1,0:T(8,128)(2,1)S(1)}, bf16[128,1024]{1,0:T(8,128)(2,1)S(1)}, u32[]{:S(2)}, u32[]{:S(2)}) collective-permute-start(bf16[128,1024]{1,0:T(8,128)(2,1)S(1)} %maximum_select_fusion.2), channel_id=1, source_target_pairs={{0,16},{4,20},{1,17},{5,21},{2,18},{6,22},{3,19},{7,23}} | collective-permute-start | bytes 786440 | tf_op jit(solution)/shard_map/ppermute | solution.py:293
  12.8 0.0 copy-start.3
  12.8 2.8 %shard_map.84 = (bf16[128,1792]{1,0:T(8,128)(2,1)}, bf16[128,1792]{1,0:T(8,128)(2,1)}, bf16[128,1792]{1,0:T(8,128)(2,1)}, bf16[128,1792]{1,0:T(8,128)(2,1)}) custom-call(s32[1]{0:T(128)} %bitcast.2.side, bf16[128,3584]{1,0:T(8,128)(2,1)} %q.1, bf16[128,3584]{1,0:T(8,128)(2,1)} %c.1), custom_call_target="tpu_custom_call" | custom-call | bytes 3670016 | tf_op jit(solution)/shard_map/pallas_call | solution.py:200
  15.5 0.0 copy-start.4
  15.5 0.1 collective-permute-start.3
  15.6 0.5 collective-permute-start.4
  16.1 1.5 %collective-permute-done.2 = bf16[128,1024]{1,0:T(8,128)(2,1)S(1)} collective-permute-done((bf16[128,1024]{1,0:T(8,128)(2,1)S(1)}, bf16[128,1024]{1,0:T(8,128)(2,1)S(1)}, u32[]{:S(2)}, u32[]{:S(2)}) %collective-permute-start.2) | collective-permute-done | bytes 262176 | tf_op jit(solution)/shard_map/ppermute | solution.py:293
  17.7 0.0 collective-permute-done.3.refs_1_
  17.7 0.6 collective-permute-done.4.refs_3_
  18.3 1.3 %collective-permute-start.8 = (bf16[128,1024]{1,0:T(8,128)(2,1)S(1)}, bf16[128,1024]{1,0:T(8,128)(2,1)S(1)}, u32[]{:S(2)}, u32[]{:S(2)}) collective-permute-start(bf16[128,1024]{1,0:T(8,128)(2,1)S(1)} %broadcast_select_fusion.1), channel_id=1, source_target_pairs={{0,8},{16,24},{4,12},{20,28},{1,9},{17,25},{5,13},{21,29},{2,10},{... | collective-permute-start | bytes 786440 | tf_op jit(solution)/shard_map/ppermute | solution.py:293
  19.7 1.3 %collective-permute-start.7 = (bf16[128,512]{1,0:T(8,128)(2,1)S(1)}, bf16[128,512]{1,0:T(8,128)(2,1)S(1)}, u32[]{:S(2)}, u32[]{:S(2)}) collective-permute-start(bf16[128,512]{1,0:T(8,128)(2,1)S(1)} %pad_maximum_fusion.3), channel_id=1, source_target_pairs={{0,3},{1,2},{2,1},{3,0},{4,7},{5,6},{6,5},{7,4},{8,11},{9,10},{10,... | collective-permute-start | bytes 393224 | tf_op jit(solution)/shard_map/ppermute | solution.py:264
  21.0 0.4 collective-permute-start.5
  21.4 0.6 collective-permute-start.6
  22.0 3.7 %collective-permute-done.8 = bf16[128,1024]{1,0:T(8,128)(2,1)S(1)} collective-permute-done((bf16[128,1024]{1,0:T(8,128)(2,1)S(1)}, bf16[128,1024]{1,0:T(8,128)(2,1)S(1)}, u32[]{:S(2)}, u32[]{:S(2)}) %collective-permute-start.8) | collective-permute-done | bytes 262176 | tf_op jit(solution)/shard_map/ppermute | solution.py:293
  25.7 0.0 copy-start
  25.8 0.0 copy-start.2
  25.8 0.1 constant_dynamic-slice_fusion
  25.9 1.6 %collective-permute-start.10 = (bf16[128,512]{1,0:T(8,128)(2,1)S(1)}, bf16[128,512]{1,0:T(8,128)(2,1)S(1)}, u32[]{:S(2)}, u32[]{:S(2)}) collective-permute-start(bf16[128,512]{1,0:T(8,128)(2,1)S(1)} %pad_maximum_fusion.4.refs_8_.refs_4_), channel_id=1, source_target_pairs={{0,2},{1,3},{2,0},{3,1},{4,6},{5,7},{6,4},{7,5},{8,10},{9,11},{10,... | collective-permute-start | bytes 393224 | tf_op jit(solution)/shard_map/ppermute | solution.py:264
  27.5 0.1 collective-permute-start.11
  27.6 0.9 %collective-permute-done.6.refs_6_ = bf16[128,512]{1,0:T(8,128)(2,1)S(1)} collective-permute-done((bf16[128,512]{1,0:T(8,128)(2,1)S(1)}, bf16[128,512]{1,0:T(8,128)(2,1)S(1)}, u32[]{:S(2)}, u32[]{:S(2)}) %collective-permute-start.6) | collective-permute-done | bytes 131104 | tf_op jit(solution)/shard_map/ppermute | solution.py:264
  28.4 0.0 collective-permute-start.9
  28.4 0.1 pad_add_fusion.ids
  28.5 0.0 collective-permute-done.7.refs_7_
  28.5 0.0 collective-permute-done.5.refs_5_
  28.5 3.3 %collective-permute-done.10.refs_10_ = bf16[128,512]{1,0:T(8,128)(2,1)S(1)} collective-permute-done((bf16[128,512]{1,0:T(8,128)(2,1)S(1)}, bf16[128,512]{1,0:T(8,128)(2,1)S(1)}, u32[]{:S(2)}, u32[]{:S(2)}) %collective-permute-start.10) | collective-permute-done | bytes 131104 | tf_op jit(solution)/shard_map/ppermute | solution.py:264
  31.8 1.6 %collective-permute-done.11.refs_11_ = bf16[128,512]{1,0:T(8,128)(2,1)S(1)} collective-permute-done((bf16[128,512]{1,0:T(8,128)(2,1)S(1)}, bf16[128,512]{1,0:T(8,128)(2,1)S(1)}, u32[]{:S(2)}, u32[]{:S(2)}) %collective-permute-start.11) | collective-permute-done | bytes 131104 | tf_op jit(solution)/shard_map/ppermute | solution.py:264
  33.4 7.6 %shard_map.85 = (f32[2,8,1792]{2,1,0:T(8,128)S(1)}, bf16[256,512]{1,0:T(8,128)(2,1)S(1)}, bf16[2,128,1792]{2,1,0:T(8,128)(2,1)S(1)}) custom-call(s32[2]{0:T(128)S(1)} %pad_add_fusion.ids, s32[4,4]{1,0:T(4,128)S(1)} %copy-done.2, bf16[128,1792]{1,0:T(8,128)(2,1)S(1)} %copy-done, bf16[128,1792]{1,0:T(8,128)(2,1)S(1)} %collective-permute-done.3.refs_1_, ...), custom_call_target="tpu_custom_call" | custom-call | flops 4697620480 | bytes 3670016 | tf_op jit(solution)/shard_map/pallas_call | solution.py:238
  41.0 1.3 %collective-permute-start.13 = (bf16[256,512]{1,0:T(8,128)(2,1)S(1)}, bf16[256,512]{1,0:T(8,128)(2,1)S(1)}, u32[]{:S(2)}, u32[]{:S(2)}) collective-permute-start(bf16[256,512]{1,0:T(8,128)(2,1)S(1)} %get-tuple-element.40), channel_id=1, source_target_pairs={{4,2},{12,10},{20,18},{28,26},{5,3},{13,11},{21,19},{29,27},{6,0},... | collective-permute-start | bytes 786440 | tf_op jit(solution)/shard_map/ppermute | solution.py:341
  42.3 2.8 %collective-permute-start.12 = (bf16[256,512]{1,0:T(8,128)(2,1)S(1)}, bf16[256,512]{1,0:T(8,128)(2,1)S(1)}, u32[]{:S(2)}, u32[]{:S(2)}) collective-permute-start(bf16[256,512]{1,0:T(8,128)(2,1)S(1)} %get-tuple-element.40), channel_id=1, source_target_pairs={{0,2},{8,10},{16,18},{24,26},{1,3},{9,11},{17,19},{25,27},{2,0},{1... | collective-permute-start | bytes 786440 | tf_op jit(solution)/shard_map/ppermute | solution.py:341
  45.1 2.8 %shard_map.86.refs_14_ = bf16[256,512]{1,0:T(8,128)(2,1)S(1)} custom-call(s32[2]{0:T(128)S(1)} %pad_add_fusion.ids, s32[4,4]{1,0:T(4,128)S(1)} %copy-done.2, bf16[128,1792]{1,0:T(8,128)(2,1)S(1)} %copy-done, bf16[128,1792]{1,0:T(8,128)(2,1)S(1)} %collective-permute-done.3.refs_1_, bf16[128,1792]{1,0:T(8,128)(2,1)S(1)} %copy-done.1, ...), custom_call_target="tpu_custom_call" | custom-call | flops 939524096 | bytes 3670016 | tf_op jit(solution)/shard_map/pallas_call | solution.py:238
  47.9 1.5 %collective-permute-start.14 = (bf16[256,512]{1,0:T(8,128)(2,1)S(1)}, bf16[256,512]{1,0:T(8,128)(2,1)S(1)}, u32[]{:S(2)}, u32[]{:S(2)}) collective-permute-start(bf16[256,512]{1,0:T(8,128)(2,1)S(1)} %shard_map.86.refs_14_), channel_id=1, source_target_pairs={{4,0},{12,8},{20,16},{28,24},{5,1},{13,9},{21,17},{29,25},{6,2},{1... | collective-permute-start | bytes 786440 | tf_op jit(solution)/shard_map/ppermute | solution.py:341
  49.4 4.4 %shard_map.87 = (bf16[128,896]{1,0:T(8,128)(2,1)S(1)}, bf16[128,896]{1,0:T(8,128)(2,1)S(1)}, bf16[128,896]{1,0:T(8,128)(2,1)S(1)}, bf16[128,896]{1,0:T(8,128)(2,...) custom-call(s32[2]{0:T(128)S(1)} %pad_add_fusion.ids, ...), custom_call_target="tpu_custom_call" | custom-call | flops 3758096384 | bytes 1835008 | tf_op jit(solution)/shard_map/pallas_call | solution.py:238
  53.8 0.8 collective-permute-start.15
  54.6 0.1 collective-permute-start.17
  54.7 4.1 %collective-permute-done.14 = bf16[256,512]{1,0:T(8,128)(2,1)S(1)} collective-permute-done((bf16[256,512]{1,0:T(8,128)(2,1)S(1)}, bf16[256,512]{1,0:T(8,128)(2,1)S(1)}, u32[]{:S(2)}, u32[]{:S(2)}) %collective-permute-start.14) | collective-permute-done | bytes 262176 | tf_op jit(solution)/shard_map/ppermute | solution.py:341
  58.8 0.0 collective-permute-done.13
  58.8 0.0 collective-permute-done.12
  58.8 0.2 add_convert_fusion.refs_14_
  58.9 1.3 %collective-permute-start.20 = (bf16[256,512]{1,0:T(8,128)(2,1)S(1)}, bf16[256,512]{1,0:T(8,128)(2,1)S(1)}, u32[]{:S(2)}, u32[]{:S(2)}) collective-permute-start(bf16[256,512]{1,0:T(8,128)(2,1)S(1)} %add_convert_fusion.refs_14_), channel_id=1, source_target_pairs={{8,0},{24,16},{9,1},{25,17},{10,2},{26,18},{11,3},{27,19}} | collective-permute-start | bytes 786440 | tf_op jit(solution)/shard_map/ppermute | solution.py:354
  60.2 4.4 %shard_map.88 = (bf16[128,896]{1,0:T(8,128)(2,1)S(1)}, bf16[128,896]{1,0:T(8,128)(2,1)S(1)}, bf16[128,896]{1,0:T(8,128)(2,1)S(1)}, bf16[128,896]{1,0:T(8,128)(2,...) custom-call(s32[2]{0:T(128)S(1)} %pad_add_fusion.ids, ...), custom_call_target="tpu_custom_call" | custom-call | flops 3758096384 | bytes 1835008 | tf_op jit(solution)/shard_map/pallas_call | solution.py:238
  64.6 0.1 collective-permute-start.16
  64.7 0.5 collective-permute-start.18
  65.2 3.9 %collective-permute-done.20 = bf16[256,512]{1,0:T(8,128)(2,1)S(1)} collective-permute-done((bf16[256,512]{1,0:T(8,128)(2,1)S(1)}, bf16[256,512]{1,0:T(8,128)(2,1)S(1)}, u32[]{:S(2)}, u32[]{:S(2)}) %collective-permute-start.20) | collective-permute-done | bytes 262176 | tf_op jit(solution)/shard_map/ppermute | solution.py:354
  69.1 0.2 collective-permute-start.19
  69.3 0.0 collective-permute-done.15
  69.3 1.3 %collective-permute-start.21 = (bf16[256,512]{1,0:T(8,128)(2,1)S(1)}, bf16[256,512]{1,0:T(8,128)(2,1)S(1)}, u32[]{:S(2)}, u32[]{:S(2)}) collective-permute-start(bf16[256,512]{1,0:T(8,128)(2,1)S(1)} %add_add_fusion), channel_id=1, source_target_pairs={{16,0},{17,1},{18,2},{19,3}} | collective-permute-start | bytes 786440 | tf_op jit(solution)/shard_map/ppermute | solution.py:354
  70.6 0.0 collective-permute-done.16
  70.6 1.1 %maximum_select_fusion = bf16[128,3584]{1,0:T(8,128)(2,1)} fusion(bf16[128,896]{1,0:T(8,128)(2,1)S(1)} %collective-permute-done.16, bf16[128,896]{1,0:T(8,128)(2,1)S(1)} %collective-permute-done.15, bf16[128,896]{1,0:T(8,128)(2,1)S(1)} %get-tuple-element.42, bf16[128,896]{1,0:T(8,128)(2,1)S(1)} %get-tuple-element.39, pred[]{:T(512)S(6)} %eq.23), kind=kLoop, calls=%fused_computation | loop fusion | flops 7798784 | bytes 1835009 | tf_op jit(solution)/shard_map/jit(_where)/select_n | solution.py:377
  71.8 4.7 %collective-permute-done.19 = bf16[256,512]{1,0:T(8,128)(2,1)S(1)} collective-permute-done((bf16[256,512]{1,0:T(8,128)(2,1)S(1)}, bf16[256,512]{1,0:T(8,128)(2,1)S(1)}, u32[]{:S(2)}, u32[]{:S(2)}) %collective-permute-start.19) | collective-permute-done | bytes 262176 | tf_op jit(solution)/shard_map/ppermute | solution.py:264
  76.5 2.9 %collective-permute-done.21 = bf16[256,512]{1,0:T(8,128)(2,1)S(1)} collective-permute-done((bf16[256,512]{1,0:T(8,128)(2,1)S(1)}, bf16[256,512]{1,0:T(8,128)(2,1)S(1)}, u32[]{:S(2)}, u32[]{:S(2)}) %collective-permute-start.21) | collective-permute-done | bytes 262176 | tf_op jit(solution)/shard_map/ppermute | solution.py:354
  79.3 0.1 fusion.1
  79.5 0.1 collective-permute-start.22
  79.6 0.0 collective-permute-done.17
  79.6 1.1 %maximum_select_fusion.1 = bf16[128,3584]{1,0:T(8,128)(2,1)} fusion(bf16[128,896]{1,0:T(8,128)(2,1)S(1)} %collective-permute-done.18, bf16[128,896]{1,0:T(8,128)(2,1)S(1)} %collective-permute-done.17, bf16[128,896]{1,0:T(8,128)(2,1)S(1)} %get-tuple-element.46, bf16[128,896]{1,0:T(8,128)(2,1)S(1)} %get-tuple-element.45, pred[]{:T(512)S(6)} %eq.23), kind=kLoop, calls=%fused_computation.1 | loop fusion | flops 7798784 | bytes 1835009 | tf_op jit(solution)/shard_map/jit(_where)/select_n | solution.py:377
  80.7 0.2 collective-permute-done.22
  80.9 0.1 maximum_select_fusion.3
  81.0 0.7 pad_maximum_fusion.7
  81.7 0.7 pad_maximum_fusion.6
  (21 shorter events, 0.4 us)
Async XLA Ops:
  0.6 9.1 %collective-permute-start = (bf16[128,512]{1,0:T(8,128)(2,1)}, bf16[128,512]{1,0:T(8,128)(2,1)S(1)}, u32[]{:S(2)}, u32[]{:S(2)}) collective-permute-start(bf16[128,512]{1,0:T(8,128)(2,1)} %param.6), channel_id=1, source_target_pairs={{0,4},{1,5},{2,6},{3,7}} | collective-permute-start | bytes 393224 | tf_op jit(solution)/shard_map/ppermute | solution.py:296
  5.5 5.9 %collective-permute-start.1 = (bf16[128,512]{1,0:T(8,128)(2,1)}, bf16[128,512]{1,0:T(8,128)(2,1)S(1)}, u32[]{:S(2)}, u32[]{:S(2)}) collective-permute-start(bf16[128,512]{1,0:T(8,128)(2,1)} %param.7), channel_id=1, source_target_pairs={{0,4},{1,5},{2,6},{3,7}} | collective-permute-start | bytes 393224 | tf_op jit(solution)/shard_map/ppermute | solution.py:296
  11.4 6.3 %collective-permute-start.2 = (bf16[128,1024]{1,0:T(8,128)(2,1)S(1)}, bf16[128,1024]{1,0:T(8,128)(2,1)S(1)}, u32[]{:S(2)}, u32[]{:S(2)}) collective-permute-start(bf16[128,1024]{1,0:T(8,128)(2,1)S(1)} %maximum_select_fusion.2), channel_id=1, source_target_pairs={{0,16},{4,20},{1,17},{5,21},{2,18},{6,22},{3,19},{7,23}} | collective-permute-start | bytes 786440 | tf_op jit(solution)/shard_map/ppermute | solution.py:293
  12.8 3.4 %copy-start.3 = (bf16[128,512]{1,0:T(8,128)(2,1)S(1)}, bf16[128,512]{1,0:T(8,128)(2,1)}, u32[]{:S(2)}) copy-start(bf16[128,512]{1,0:T(8,128)(2,1)} %param.6) | copy-start | bytes 393220
  15.5 4.1 %copy-start.4 = (bf16[128,512]{1,0:T(8,128)(2,1)S(1)}, bf16[128,512]{1,0:T(8,128)(2,1)}, u32[]{:S(2)}) copy-start(bf16[128,512]{1,0:T(8,128)(2,1)} %param.7) | copy-start | bytes 393220
  15.5 2.2 %collective-permute-start.3 = (bf16[128,1792]{1,0:T(8,128)(2,1)}, bf16[128,1792]{1,0:T(8,128)(2,1)S(1)}, u32[]{:S(2)}, u32[]{:S(2)}) collective-permute-start(bf16[128,1792]{1,0:T(8,128)(2,1)} %get-tuple-element.30), channel_id=1, source_target_pairs={{0,1},{1,0},{2,3},{3,2},{4,5},{5,4},{6,7},{7,6},{8,9},{9,8},{10,11... | collective-permute-start | bytes 1376264 | tf_op jit(solution)/shard_map/ppermute | solution.py:264
  15.6 2.7 %collective-permute-start.4 = (bf16[128,1792]{1,0:T(8,128)(2,1)}, bf16[128,1792]{1,0:T(8,128)(2,1)S(1)}, u32[]{:S(2)}, u32[]{:S(2)}) collective-permute-start(bf16[128,1792]{1,0:T(8,128)(2,1)} %get-tuple-element.31), channel_id=1, source_target_pairs={{0,1},{1,0},{2,3},{3,2},{4,5},{5,4},{6,7},{7,6},{8,9},{9,8},{10,11... | collective-permute-start | bytes 1376264 | tf_op jit(solution)/shard_map/ppermute | solution.py:264
  18.3 7.4 %collective-permute-start.8 = (bf16[128,1024]{1,0:T(8,128)(2,1)S(1)}, bf16[128,1024]{1,0:T(8,128)(2,1)S(1)}, u32[]{:S(2)}, u32[]{:S(2)}) collective-permute-start(bf16[128,1024]{1,0:T(8,128)(2,1)S(1)} %broadcast_select_fusion.1), channel_id=1, source_target_pairs={{0,8},{16,24},{4,12},{20,28},{1,9},{17,25},{5,13},{21,29},{2,10},{... | collective-permute-start | bytes 786440 | tf_op jit(solution)/shard_map/ppermute | solution.py:293
  19.7 8.8 %collective-permute-start.7 = (bf16[128,512]{1,0:T(8,128)(2,1)S(1)}, bf16[128,512]{1,0:T(8,128)(2,1)S(1)}, u32[]{:S(2)}, u32[]{:S(2)}) collective-permute-start(bf16[128,512]{1,0:T(8,128)(2,1)S(1)} %pad_maximum_fusion.3), channel_id=1, source_target_pairs={{0,3},{1,2},{2,1},{3,0},{4,7},{5,6},{6,5},{7,4},{8,11},{9,10},{10,... | collective-permute-start | bytes 393224 | tf_op jit(solution)/shard_map/ppermute | solution.py:264
  21.0 7.6 %collective-permute-start.5 = (bf16[128,512]{1,0:T(8,128)(2,1)S(1)}, bf16[128,512]{1,0:T(8,128)(2,1)S(1)}, u32[]{:S(2)}, u32[]{:S(2)}) collective-permute-start(bf16[128,512]{1,0:T(8,128)(2,1)S(1)} %pad_maximum_fusion.3), channel_id=1, source_target_pairs={{0,1},{1,0},{2,3},{3,2},{4,5},{5,4},{6,7},{7,6},{8,9},{9,8},{10,11... | collective-permute-start | bytes 393224 | tf_op jit(solution)/shard_map/ppermute | solution.py:264
  21.4 7.1 %collective-permute-start.6 = (bf16[128,512]{1,0:T(8,128)(2,1)S(1)}, bf16[128,512]{1,0:T(8,128)(2,1)S(1)}, u32[]{:S(2)}, u32[]{:S(2)}) collective-permute-start(bf16[128,512]{1,0:T(8,128)(2,1)S(1)} %pad_maximum_fusion.2.refs_4_), channel_id=1, source_target_pairs={{0,2},{1,3},{2,0},{3,1},{4,6},{5,7},{6,4},{7,5},{8,10},{9,11},{10,... | collective-permute-start | bytes 393224 | tf_op jit(solution)/shard_map/ppermute | solution.py:264
  25.7 7.6 %copy-start = (bf16[128,1792]{1,0:T(8,128)(2,1)S(1)}, bf16[128,1792]{1,0:T(8,128)(2,1)}, u32[]{:S(2)}) copy-start(bf16[128,1792]{1,0:T(8,128)(2,1)} %get-tuple-element.32.refs_0_) | copy-start | bytes 1376260
  25.8 7.6 %copy-start.1 = (bf16[128,1792]{1,0:T(8,128)(2,1)S(1)}, bf16[128,1792]{1,0:T(8,128)(2,1)}, u32[]{:S(2)}) copy-start(bf16[128,1792]{1,0:T(8,128)(2,1)} %get-tuple-element.34.refs_2_) | copy-start | bytes 1376260
  25.8 7.6 %copy-start.2 = (s32[4,4]{1,0:T(4,128)S(1)}, s32[4,4]{1,0:T(4,128)}, u32[]{:S(2)}) copy-start(s32[4,4]{1,0:T(4,128)} %tree.7) | copy-start | bytes 196
  25.9 5.9 %collective-permute-start.10 = (bf16[128,512]{1,0:T(8,128)(2,1)S(1)}, bf16[128,512]{1,0:T(8,128)(2,1)S(1)}, u32[]{:S(2)}, u32[]{:S(2)}) collective-permute-start(bf16[128,512]{1,0:T(8,128)(2,1)S(1)} %pad_maximum_fusion.4.refs_8_.refs_4_), channel_id=1, source_target_pairs={{0,2},{1,3},{2,0},{3,1},{4,6},{5,7},{6,4},{7,5},{8,10},{9,11},{10,... | collective-permute-start | bytes 393224 | tf_op jit(solution)/shard_map/ppermute | solution.py:264
  27.5 5.9 %collective-permute-start.11 = (bf16[128,512]{1,0:T(8,128)(2,1)S(1)}, bf16[128,512]{1,0:T(8,128)(2,1)S(1)}, u32[]{:S(2)}, u32[]{:S(2)}) collective-permute-start(bf16[128,512]{1,0:T(8,128)(2,1)S(1)} %pad_maximum_fusion.5), channel_id=1, source_target_pairs={{0,3},{1,2},{2,1},{3,0},{4,7},{5,6},{6,5},{7,4},{8,11},{9,10},{10,... | collective-permute-start | bytes 393224 | tf_op jit(solution)/shard_map/ppermute | solution.py:264
  28.4 4.9 %collective-permute-start.9 = (bf16[128,512]{1,0:T(8,128)(2,1)S(1)}, bf16[128,512]{1,0:T(8,128)(2,1)S(1)}, u32[]{:S(2)}, u32[]{:S(2)}) collective-permute-start(bf16[128,512]{1,0:T(8,128)(2,1)S(1)} %pad_maximum_fusion.5), channel_id=1, source_target_pairs={{0,1},{1,0},{2,3},{3,2},{4,5},{5,4},{6,7},{7,6},{8,9},{9,8},{10,11... | collective-permute-start | bytes 393224 | tf_op jit(solution)/shard_map/ppermute | solution.py:264
  41.0 17.8 %collective-permute-start.13 = (bf16[256,512]{1,0:T(8,128)(2,1)S(1)}, bf16[256,512]{1,0:T(8,128)(2,1)S(1)}, u32[]{:S(2)}, u32[]{:S(2)}) collective-permute-start(bf16[256,512]{1,0:T(8,128)(2,1)S(1)} %get-tuple-element.40), channel_id=1, source_target_pairs={{4,2},{12,10},{20,18},{28,26},{5,3},{13,11},{21,19},{29,27},{6,0},... | collective-permute-start | bytes 786440 | tf_op jit(solution)/shard_map/ppermute | solution.py:341
  42.3 16.5 %collective-permute-start.12 = (bf16[256,512]{1,0:T(8,128)(2,1)S(1)}, bf16[256,512]{1,0:T(8,128)(2,1)S(1)}, u32[]{:S(2)}, u32[]{:S(2)}) collective-permute-start(bf16[256,512]{1,0:T(8,128)(2,1)S(1)} %get-tuple-element.40), channel_id=1, source_target_pairs={{0,2},{8,10},{16,18},{24,26},{1,3},{9,11},{17,19},{25,27},{2,0},{1... | collective-permute-start | bytes 786440 | tf_op jit(solution)/shard_map/ppermute | solution.py:341
  47.9 10.9 %collective-permute-start.14 = (bf16[256,512]{1,0:T(8,128)(2,1)S(1)}, bf16[256,512]{1,0:T(8,128)(2,1)S(1)}, u32[]{:S(2)}, u32[]{:S(2)}) collective-permute-start(bf16[256,512]{1,0:T(8,128)(2,1)S(1)} %shard_map.86.refs_14_), channel_id=1, source_target_pairs={{4,0},{12,8},{20,16},{28,24},{5,1},{13,9},{21,17},{29,25},{6,2},{1... | collective-permute-start | bytes 786440 | tf_op jit(solution)/shard_map/ppermute | solution.py:341
  53.8 15.5 %collective-permute-start.15 = (bf16[128,896]{1,0:T(8,128)(2,1)S(1)}, bf16[128,896]{1,0:T(8,128)(2,1)S(1)}, u32[]{:S(2)}, u32[]{:S(2)}) collective-permute-start(bf16[128,896]{1,0:T(8,128)(2,1)S(1)} %get-tuple-element.43), channel_id=1, source_target_pairs={{0,1},{1,0},{2,3},{3,2},{4,5},{5,4},{6,7},{7,6},{8,9},{9,8},{10,11... | collective-permute-start | bytes 688136 | tf_op jit(solution)/shard_map/ppermute | solution.py:264
  54.6 25.0 %collective-permute-start.17 = (bf16[128,896]{1,0:T(8,128)(2,1)S(1)}, bf16[128,896]{1,0:T(8,128)(2,1)S(1)}, u32[]{:S(2)}, u32[]{:S(2)}) collective-permute-start(bf16[128,896]{1,0:T(8,128)(2,1)S(1)} %get-tuple-element.47), channel_id=1, source_target_pairs={{0,1},{1,0},{2,3},{3,2},{4,5},{5,4},{6,7},{7,6},{8,9},{9,8},{10,11... | collective-permute-start | bytes 688136 | tf_op jit(solution)/shard_map/ppermute | solution.py:264
  58.9 10.1 %collective-permute-start.20 = (bf16[256,512]{1,0:T(8,128)(2,1)S(1)}, bf16[256,512]{1,0:T(8,128)(2,1)S(1)}, u32[]{:S(2)}, u32[]{:S(2)}) collective-permute-start(bf16[256,512]{1,0:T(8,128)(2,1)S(1)} %add_convert_fusion.refs_14_), channel_id=1, source_target_pairs={{8,0},{24,16},{9,1},{25,17},{10,2},{26,18},{11,3},{27,19}} | collective-permute-start | bytes 786440 | tf_op jit(solution)/shard_map/ppermute | solution.py:354
  64.6 6.0 %collective-permute-start.16 = (bf16[128,896]{1,0:T(8,128)(2,1)S(1)}, bf16[128,896]{1,0:T(8,128)(2,1)S(1)}, u32[]{:S(2)}, u32[]{:S(2)}) collective-permute-start(bf16[128,896]{1,0:T(8,128)(2,1)S(1)} %get-tuple-element.44), channel_id=1, source_target_pairs={{0,1},{1,0},{2,3},{3,2},{4,5},{5,4},{6,7},{7,6},{8,9},{9,8},{10,11... | collective-permute-start | bytes 688136 | tf_op jit(solution)/shard_map/ppermute | solution.py:264
  64.7 14.9 %collective-permute-start.18 = (bf16[128,896]{1,0:T(8,128)(2,1)S(1)}, bf16[128,896]{1,0:T(8,128)(2,1)S(1)}, u32[]{:S(2)}, u32[]{:S(2)}) collective-permute-start(bf16[128,896]{1,0:T(8,128)(2,1)S(1)} %get-tuple-element.48), channel_id=1, source_target_pairs={{0,1},{1,0},{2,3},{3,2},{4,5},{5,4},{6,7},{7,6},{8,9},{9,8},{10,11... | collective-permute-start | bytes 688136 | tf_op jit(solution)/shard_map/ppermute | solution.py:264
  69.1 7.4 %collective-permute-start.19 = (bf16[256,512]{1,0:T(8,128)(2,1)S(1)}, bf16[256,512]{1,0:T(8,128)(2,1)S(1)}, u32[]{:S(2)}, u32[]{:S(2)}) collective-permute-start(bf16[256,512]{1,0:T(8,128)(2,1)S(1)} %pad_maximum_fusion.1), channel_id=1, source_target_pairs={{0,2},{1,3},{2,0},{3,1},{4,6},{5,7},{6,4},{7,5},{8,10},{9,11},{10,... | collective-permute-start | bytes 786440 | tf_op jit(solution)/shard_map/ppermute | solution.py:264
  69.3 10.0 %collective-permute-start.21 = (bf16[256,512]{1,0:T(8,128)(2,1)S(1)}, bf16[256,512]{1,0:T(8,128)(2,1)S(1)}, u32[]{:S(2)}, u32[]{:S(2)}) collective-permute-start(bf16[256,512]{1,0:T(8,128)(2,1)S(1)} %add_add_fusion), channel_id=1, source_target_pairs={{16,0},{17,1},{18,2},{19,3}} | collective-permute-start | bytes 786440 | tf_op jit(solution)/shard_map/ppermute | solution.py:354
  79.5 1.4 %collective-permute-start.22 = (bf16[128,512]{1,0:T(8,128)(2,1)S(1)}, bf16[128,512]{1,0:T(8,128)(2,1)S(1)}, u32[]{:S(2)}, u32[]{:S(2)}) collective-permute-start(bf16[128,512]{1,0:T(8,128)(2,1)S(1)} %get-tuple-element.63), channel_id=1, source_target_pairs={{0,1},{1,0},{2,3},{3,2},{4,5},{5,4},{6,7},{7,6},{8,9},{9,8},{10,11... | collective-permute-start | bytes 393224 | tf_op jit(solution)/shard_map/ppermute | solution.py:264
